TPU v7x, 32 devices: a whole 2x2x4 slice. The times are simulated.
32 devices in a mesh: dp: 4 (over y, x), expert: 8 (over z, core).
Axes of the slice: x: 2, y: 2, z: 4, core: 2. Of those that a mesh axis runs over, the one named last changes fastest.
Arguments:
- inputs: bfloat16 [32768, 768], P(('dp', 'expert')), may hold values from -6 to 6
- cotangent: bfloat16 [32768, 768], P(('dp', 'expert')), may hold values from -6 to 6
- document_ids: int32 [32, 1024], P(('dp', 'expert')), may hold values from 0 to 3, never falling along the last dimension, each value on 1 to 512 neighbouring positions
- domain_counts: int32 [8], replicated, may hold values from 1 to 8, 32 in all
- domain_weight: float32 [8], replicated, may hold values from 0.5 to 2
- token_order: int32 [32, 1024], P(('dp', 'expert')), may hold values from 0 to 1023, as said below
- expert_counts: int32 [32, 8], P(('dp', 'expert')), may hold values from 0 to 256, as said below
- dense_weights: float32 [4, 768, 768], P(None, ('dp', 'expert')), may hold values from -2.5 to 2.5
- vector_params: float32 [10, 768], P(None, ('dp', 'expert')), may hold values from -1 to 4
- expert_weights: float32 [8, 2, 768, 3072], P('expert', None, None, 'dp'), may hold values from -0.5 to 0.5
- dense_first: float32 [4, 768, 768], P(None, ('dp', 'expert')), may hold values from -0.00024414062 to 0.00024414062
- dense_second: float32 [4, 768, 768], P(None, ('dp', 'expert')), may hold values from 2.4927888e-11 to 9.971155e-11
- dense_average: float32 [4, 768, 768], P(None, ('dp', 'expert')), may hold values from -0.21875 to 0.21875
- vector_first: float32 [10, 768], P(None, ('dp', 'expert')), may hold values from -0.00024414062 to 0.00024414062
- vector_second: float32 [10, 768], P(None, ('dp', 'expert')), may hold values from 2.4927888e-11 to 9.971155e-11
- vector_average: float32 [10, 768], P(None, ('dp', 'expert')), may hold values from 0.5 to 1.5
- expert_first: float32 [8, 2, 768, 3072], P('expert', None, None, 'dp'), may hold values from -3.8146973e-05 to 3.8146973e-05
- expert_second: float32 [8, 2, 768, 3072], P('expert', None, None, 'dp'), may hold values from 4.998293e-13 to 1.9993172e-12
- expert_average: float32 [8, 2, 768, 3072], P('expert', None, None, 'dp'), may hold values from -0.21875 to 0.21875
Outputs:
- block_output: float32 [32768, 768], P(('dp', 'expert'))
- input_grad: float32 [32768, 768], P(('dp', 'expert'))
- dense_updated: float32 [4, 768, 768], P(None, ('dp', 'expert'))
- dense_first_new: float32 [4, 768, 768], P(None, ('dp', 'expert'))
- dense_second_new: float32 [4, 768, 768], P(None, ('dp', 'expert'))
- dense_average_new: float32 [4, 768, 768], P(None, ('dp', 'expert'))
- vector_updated: float32 [10, 768], P(None, ('dp', 'expert'))
- vector_first_new: float32 [10, 768], P(None, ('dp', 'expert'))
- vector_second_new: float32 [10, 768], P(None, ('dp', 'expert'))
- vector_average_new: float32 [10, 768], P(None, ('dp', 'expert'))
- expert_updated: float32 [8, 2, 768, 3072], P('expert', None, None, 'dp')
- expert_first_new: float32 [8, 2, 768, 3072], P('expert', None, None, 'dp')
- expert_second_new: float32 [8, 2, 768, 3072], P('expert', None, None, 'dp')
- expert_average_new: float32 [8, 2, 768, 3072], P('expert', None, None, 'dp')
- grad_norm: float32 [], replicated
Inputs may be any that keep to these rules, and one draw needn't show every extreme that they name: `token_order`: each row is a permutation of 0 to 1023. `expert_counts`: each row sums to 1024; no entry exceeds 256, every row has an entry equal to 256, and in every draw one expert takes 256 tokens from every row.
All inputs are finite; a program needn't handle non-finite values.
Results may differ from a plain program's by a relative error of at most 0.014.
The roundings to bfloat16 on the way count: a program that leaves them out, or rounds other values in their place, can miss the bound.
Values may be sent and summed in bfloat16 or wider, within the bound.
A program may use at most 320 MiB of HBM per device.

v0:
```python
import jax
import jax.numpy as jnp
from jax import lax
from jax.sharding import PartitionSpec as P

HEADS = 12
HEAD_DIM = 64
LEN = 1024
QBLK = 512
NDOM = 8
STEP = 10


norm_eps = 1e-05
masked_score = -1e30
beta_first = 0.9
beta_second = 0.999
adam_eps = 1e-08
dense_rate = 0.1
vector_rate = 0.5
expert_rate = 0.02
weight_decay = 0.1
ema_keep = 0.9
clip_norm = 1.0


def layer_norm(values_in, gain_row):
    center = values_in - jnp.mean(values_in, axis=-1, keepdims=True)
    spread = jnp.mean(center * center, axis=-1, keepdims=True)
    return center * lax.rsqrt(spread + norm_eps) * gain_row


def block_scores(query_block, key_seq, documents, block_first, seq_start):
    score_scale = HEAD_DIM ** (-0.5)
    scores = (
        jnp.einsum("qhd,khd->hqk", query_block, key_seq, preferred_element_type=jnp.float32)
        * score_scale
    )
    query_pos = block_first - seq_start + jnp.arange(QBLK)
    key_pos = jnp.arange(LEN)
    query_docs = lax.dynamic_slice_in_dim(documents, block_first, QBLK)
    allowed = (key_pos[None, :] <= query_pos[:, None]) & (documents[None, :] == query_docs[:, None])
    return jnp.where(allowed[None], scores, masked_score)


def attend_forward(queries, keys_all, values_all, documents):
    tokens = queries.shape[0]

    def one_block(block_index, carried):
        attn_mixed, totals = carried
        block_first = block_index * QBLK
        seq_start = block_first // LEN * LEN
        query_block = lax.dynamic_slice_in_dim(queries, block_first, QBLK)
        scores = block_scores(query_block, keys_all, documents, block_first, seq_start)
        score_top = jnp.max(scores, axis=-1, keepdims=True)
        weights = jnp.exp(scores - score_top)
        weight_total = jnp.sum(weights, axis=-1, keepdims=True)
        probs_low = (weights / weight_total).astype(jnp.bfloat16)
        block_out = jnp.einsum(
            "hqk,khd->qhd", probs_low, values_all, preferred_element_type=jnp.float32
        )
        attn_mixed = lax.dynamic_update_slice_in_dim(attn_mixed, block_out, block_first, 0)
        totals = lax.dynamic_update_slice_in_dim(
            totals, (score_top + jnp.log(weight_total))[:, :, 0], block_first, 1
        )
        return (attn_mixed, totals)

    initial = (jnp.zeros(queries.shape, jnp.float32), jnp.zeros((HEADS, tokens), jnp.float32))
    return lax.fori_loop(0, tokens // QBLK, one_block, initial)


def attend_backward(queries, keys_all, values_all, documents, totals, grad_mixed):
    tokens = queries.shape[0]
    score_scale = HEAD_DIM ** (-0.5)

    def one_block(block_index, carried):
        grad_queries, grad_keys, grad_values = carried
        block_first = block_index * QBLK
        seq_start = block_first // LEN * LEN
        query_block = lax.dynamic_slice_in_dim(queries, block_first, QBLK)
        grad_block = lax.dynamic_slice_in_dim(grad_mixed, block_first, QBLK)
        scores = block_scores(query_block, keys_all, documents, block_first, seq_start)
        block_totals = lax.dynamic_slice_in_dim(totals, block_first, QBLK, 1)
        probabilities = jnp.exp(scores - block_totals[:, :, None])
        grad_probs = jnp.einsum(
            "qhd,khd->hqk", grad_block, values_all, preferred_element_type=jnp.float32
        )
        inner = jnp.sum(probabilities * grad_probs, axis=-1, keepdims=True)
        grad_scores = (probabilities * (grad_probs - inner)).astype(jnp.bfloat16)
        query_part = (
            jnp.einsum("hqk,khd->qhd", grad_scores, keys_all, preferred_element_type=jnp.float32)
            * score_scale
        )
        key_part = (
            jnp.einsum("hqk,qhd->khd", grad_scores, query_block, preferred_element_type=jnp.float32)
            * score_scale
        )
        value_part = jnp.einsum(
            "hqk,qhd->khd",
            probabilities.astype(jnp.bfloat16),
            grad_block,
            preferred_element_type=jnp.float32,
        )
        grad_queries = lax.dynamic_update_slice_in_dim(grad_queries, query_part, block_first, 0)
        grad_keys = grad_keys + key_part
        grad_values = grad_values + value_part
        return (grad_queries, grad_keys, grad_values)

    zeroed = jnp.zeros(queries.shape, jnp.float32)
    return lax.fori_loop(0, tokens // QBLK, one_block, (zeroed, zeroed, zeroed))


def adam_update(weight, gradient, first_moment, second_moment, average, factor, rate):
    clipped = gradient * factor
    first_new = beta_first * first_moment + (1.0 - beta_first) * clipped
    second_new = beta_second * second_moment + (1.0 - beta_second) * clipped * clipped
    first_hat = first_new / (1.0 - beta_first**STEP)
    second_hat = second_new / (1.0 - beta_second**STEP)
    updated = weight - rate * (
        first_hat / (jnp.sqrt(second_hat) + adam_eps) + weight_decay * weight
    )
    average_new = ema_keep * average + (1.0 - ema_keep) * updated
    return (updated, first_new, second_new, average_new)


def shards(
    inputs,
    cotangent,
    document_ids,
    domain_counts,
    domain_weight,
    token_order,
    expert_counts,
    dense_weights,
    vector_params,
    expert_weights,
    dense_first,
    dense_second,
    dense_average,
    vector_first,
    vector_second,
    vector_average,
    expert_first,
    expert_second,
    expert_average,
):
    tokens, model_width = inputs.shape
    experts_total = expert_counts.shape[1]
    capacity = 2 * tokens // experts_total
    owners = lax.axis_size("expert")
    local_experts = experts_total // owners
    groups = lax.axis_size(("dp", "expert"))
    sequences = tokens // LEN
    dense_low, vector_low = (
        lax.all_gather(dense_weights.astype(jnp.bfloat16), ("dp", "expert"), axis=1, tiled=True),
        lax.all_gather(vector_params.astype(jnp.bfloat16), ("dp", "expert"), axis=1, tiled=True),
    )
    seq_index = lax.axis_index(("dp", "expert")) * sequences + jnp.arange(sequences)
    bounds = jnp.cumsum(domain_counts)
    domain = jnp.sum((seq_index[:, None] >= bounds[None, :]).astype(jnp.int32), axis=1)
    seq_pick = (domain[:, None] == jnp.arange(NDOM)[None, :]).astype(jnp.float32)
    seq_weight = jnp.sum(seq_pick * domain_weight[None, :], axis=1)
    seq_count = jnp.sum(seq_pick * domain_counts[None, :].astype(jnp.float32), axis=1)
    seq_scale = seq_weight * (sequences * groups) / (NDOM * seq_count)
    token_scale = jnp.repeat(seq_scale, LEN)
    row_counts = expert_counts[0]
    row_order = token_order[0]
    count_ends = jnp.cumsum(row_counts)
    count_starts = count_ends - row_counts
    sorted_pos = jnp.arange(tokens)
    sorted_expert = jnp.sum((sorted_pos[:, None] >= count_ends[None, :]).astype(jnp.int32), axis=1)
    sorted_pick = sorted_expert[:, None] == jnp.arange(experts_total)[None, :]
    sorted_start = jnp.sum(jnp.where(sorted_pick, count_starts[None, :], 0), axis=1)
    sorted_slot = sorted_expert * capacity + sorted_pos - sorted_start
    token_slot = jnp.zeros((tokens,), jnp.int32).at[row_order].set(sorted_slot)
    token_expert = jnp.zeros((tokens,), jnp.int32).at[row_order].set(sorted_expert)
    expert_pick = (token_expert[:, None] == jnp.arange(experts_total)[None, :]).astype(jnp.float32)
    slot_valid = (jnp.arange(capacity)[None, :] < row_counts[:, None]).reshape(-1)
    slot_position = (count_starts[:, None] + jnp.arange(capacity)[None, :]).reshape(-1)
    slot_token = row_order[jnp.minimum(slot_position, tokens - 1)]
    inputs_float = inputs.astype(jnp.float32)
    normed_one, norm_one_back = jax.vjp(layer_norm, inputs_float, vector_low[0].astype(jnp.float32))
    normed_low = normed_one.astype(jnp.bfloat16)
    projected = jnp.einsum(
        "td,cde->cte", normed_low, dense_low[:3], preferred_element_type=jnp.float32
    ).astype(jnp.bfloat16)
    shaped = projected.reshape(3, tokens, HEADS, HEAD_DIM)
    documents = document_ids.reshape(-1)
    attn_mixed, totals = attend_forward(shaped[0], shaped[1], shaped[2], documents)
    mixed_low = attn_mixed.reshape(tokens, model_width).astype(jnp.bfloat16)
    hidden_state = inputs_float + jnp.dot(
        mixed_low, dense_low[3], preferred_element_type=jnp.float32
    )
    normed_two, norm_two_back = jax.vjp(layer_norm, hidden_state, vector_low[1].astype(jnp.float32))
    centroids = vector_low[2:].astype(jnp.float32)
    logits = jnp.dot(normed_two, centroids.T, precision=lax.Precision.HIGHEST)
    gate_value = jax.nn.sigmoid(jnp.sum(logits * expert_pick, axis=1))
    sent_rows = normed_two.astype(jnp.bfloat16)
    send_rows = jnp.where(slot_valid[:, None], sent_rows[slot_token], 0).reshape(
        experts_total, capacity, model_width
    )
    received = lax.all_to_all(send_rows, "expert", split_axis=0, concat_axis=0, tiled=True)
    rows_in = received.reshape(owners, local_experts, capacity, model_width)
    own_low = expert_weights.astype(jnp.bfloat16)
    expert_low = lax.all_gather(own_low, "dp", axis=3, tiled=True)
    expert_pre = jnp.einsum(
        "jkcd,kdf->jkcf", rows_in, expert_low[:, 0], preferred_element_type=jnp.float32
    )
    active, gelu_back = jax.vjp(jax.nn.gelu, expert_pre)
    active_low = active.astype(jnp.bfloat16)
    produced = jnp.einsum(
        "jkcf,kdf->jkcd", active_low, expert_low[:, 1], preferred_element_type=jnp.float32
    )
    produced_low = produced.astype(jnp.bfloat16)
    returned = lax.all_to_all(
        produced_low.reshape(experts_total, capacity, model_width),
        "expert",
        split_axis=0,
        concat_axis=0,
        tiled=True,
    )
    returned_rows = returned.reshape(-1, model_width)[token_slot].astype(jnp.float32)
    block_output = hidden_state + gate_value[:, None] * returned_rows
    grad_out = cotangent.astype(jnp.float32) * token_scale[:, None]
    grad_returned = (gate_value[:, None] * grad_out).astype(jnp.bfloat16)
    grad_chosen = jnp.sum(grad_out * returned_rows, axis=1) * gate_value * (1.0 - gate_value)
    grad_rows = jnp.where(slot_valid[:, None], grad_returned[slot_token], 0).reshape(
        experts_total, capacity, model_width
    )
    grad_received = lax.all_to_all(grad_rows, "expert", split_axis=0, concat_axis=0, tiled=True)
    grad_in = grad_received.reshape(owners, local_experts, capacity, model_width)
    grad_active = jnp.einsum(
        "jkcd,kdf->jkcf", grad_in, expert_low[:, 1], preferred_element_type=jnp.float32
    ).astype(jnp.bfloat16)
    grad_pre = gelu_back(grad_active.astype(jnp.float32))[0].astype(jnp.bfloat16)
    grad_sent = jnp.einsum(
        "jkcf,kdf->jkcd", grad_pre, expert_low[:, 0], preferred_element_type=jnp.float32
    )
    grad_sent_low = grad_sent.astype(jnp.bfloat16)
    grad_back = lax.all_to_all(
        grad_sent_low.reshape(experts_total, capacity, model_width),
        "expert",
        split_axis=0,
        concat_axis=0,
        tiled=True,
    )
    grad_sent_rows = grad_back.reshape(-1, model_width)[token_slot].astype(jnp.float32)
    grad_up = jnp.einsum("jkcd,jkcf->kdf", rows_in, grad_pre, preferred_element_type=jnp.float32)
    grad_down = jnp.einsum(
        "jkcd,jkcf->kdf", grad_in, active_low, preferred_element_type=jnp.float32
    )
    expert_grad = lax.psum_scatter(
        jnp.stack([grad_up, grad_down], axis=1).astype(jnp.bfloat16),
        "dp",
        scatter_dimension=3,
        tiled=True,
    ).astype(jnp.float32)
    chosen_grad = grad_chosen[:, None] * expert_pick
    grad_normed_two = grad_sent_rows + jnp.dot(
        chosen_grad, centroids, precision=lax.Precision.HIGHEST
    )
    grad_centroids = jnp.dot(chosen_grad.T, normed_two, precision=lax.Precision.HIGHEST)
    grad_hidden_norm, grad_gain_two = norm_two_back(grad_normed_two)
    grad_hidden = grad_out + grad_hidden_norm
    grad_attn = grad_hidden.astype(jnp.bfloat16)
    grad_out_proj = jnp.dot(mixed_low.T, grad_attn, preferred_element_type=jnp.float32)
    grad_mixed = jnp.dot(grad_attn, dense_low[3].T, preferred_element_type=jnp.float32).astype(
        jnp.bfloat16
    )
    grad_queries, grad_keys, grad_values = attend_backward(
        shaped[0],
        shaped[1],
        shaped[2],
        documents,
        totals,
        grad_mixed.reshape(tokens, HEADS, HEAD_DIM),
    )
    grad_proj = (
        jnp.stack([grad_queries, grad_keys, grad_values])
        .reshape(3, tokens, model_width)
        .astype(jnp.bfloat16)
    )
    grad_in_proj = jnp.einsum(
        "td,cte->cde", normed_low, grad_proj, preferred_element_type=jnp.float32
    )
    grad_normed_one = jnp.einsum(
        "cte,cde->td", grad_proj, dense_low[:3], preferred_element_type=jnp.float32
    )
    grad_input_norm, grad_gain_one = norm_one_back(grad_normed_one)
    input_grad = grad_hidden + grad_input_norm
    dense_grad = jnp.concatenate([grad_in_proj, grad_out_proj[None]], axis=0)
    vector_grad = jnp.concatenate(
        [grad_gain_one[None], grad_gain_two[None], grad_centroids], axis=0
    )
    dense_grad, vector_grad = (
        lax.psum_scatter(dense_grad, ("dp", "expert"), scatter_dimension=1, tiled=True),
        lax.psum_scatter(vector_grad, ("dp", "expert"), scatter_dimension=1, tiled=True),
    )
    squares = (
        jnp.sum(dense_grad * dense_grad)
        + jnp.sum(vector_grad * vector_grad)
        + jnp.sum(expert_grad * expert_grad)
    )
    grad_norm = jnp.sqrt(lax.psum(squares, ("dp", "expert")))
    factor = jnp.minimum(1.0, clip_norm / (grad_norm + 1e-06))
    dense_new = adam_update(
        dense_weights, dense_grad, dense_first, dense_second, dense_average, factor, dense_rate
    )
    vector_new = adam_update(
        vector_params, vector_grad, vector_first, vector_second, vector_average, factor, vector_rate
    )
    expert_new = adam_update(
        expert_weights,
        expert_grad,
        expert_first,
        expert_second,
        expert_average,
        factor,
        expert_rate,
    )
    return (
        block_output,
        input_grad,
        dense_new[0],
        dense_new[1],
        dense_new[2],
        dense_new[3],
        vector_new[0],
        vector_new[1],
        vector_new[2],
        vector_new[3],
        expert_new[0],
        expert_new[1],
        expert_new[2],
        expert_new[3],
        grad_norm,
    )


def solution(mesh):
    placed = (
        P(("dp", "expert"), None),
        P(("dp", "expert"), None),
        P(("dp", "expert"), None),
        P(),
        P(),
        P(("dp", "expert"), None),
        P(("dp", "expert"), None),
        P(None, ("dp", "expert"), None),
        P(None, ("dp", "expert")),
        P("expert", None, None, "dp"),
        P(None, ("dp", "expert"), None),
        P(None, ("dp", "expert"), None),
        P(None, ("dp", "expert"), None),
        P(None, ("dp", "expert")),
        P(None, ("dp", "expert")),
        P(None, ("dp", "expert")),
        P("expert", None, None, "dp"),
        P("expert", None, None, "dp"),
        P("expert", None, None, "dp"),
    )
    return jax.shard_map(
        shards,
        mesh=mesh,
        in_specs=placed,
        out_specs=(
            P(("dp", "expert"), None),
            P(("dp", "expert"), None),
            P(None, ("dp", "expert"), None),
            P(None, ("dp", "expert"), None),
            P(None, ("dp", "expert"), None),
            P(None, ("dp", "expert"), None),
            P(None, ("dp", "expert")),
            P(None, ("dp", "expert")),
            P(None, ("dp", "expert")),
            P(None, ("dp", "expert")),
            P("expert", None, None, "dp"),
            P("expert", None, None, "dp"),
            P("expert", None, None, "dp"),
            P("expert", None, None, "dp"),
            P(),
        ),
        check_vma=False,
    )
```

profile of v0, /device:TPU:0, one launch (start us, length us, event | category | flops | bytes accessed | tf_op | source)
XLA Modules:
  0.0 1185.1 jit_solution(1248415899453731145)
XLA Ops:
  23.3 44.1 %all-gather = bf16[32,24,10]{1,2,0:T(8,128)(2,1)S(1)} all-gather(bf16[1,24,10]{1,2,0:T(8,128)(2,1)S(1)} %convert_bitcast_fusion.1), channel_id=1, replica_groups=mesh['dp'=4,'expert'=8] {'dp','expert'}, dimensions={0}, use_global_device_ids=true | all-gather | bytes 15840 | tf_op jit(solution)/shard_map/all_gather | solution.py:156
  96.1 70.6 %while.37 = (s32[]{:T(128)}, bf16[1024,12,64]{0,2,1:T(8,128)(2,1)}, f32[12,1024]{1,0:T(8,128)S(1)}, s32[1,1024]{1,0:T(1,128)S(1)}, s32[1024]{0:T(1024)S(1)}, /*i...) while((s32[]{:T(128)}, bf16[1024,12,64]{0,2,1:T(8,128)(2,1)}, ...), condition=%wide.region_5.6_spmd, body=%wide.region_2.0_spmd.sunk | while | flops 1687677440 | bytes 190290352 | solution.py:69
  193.7 71.4 %all-to-all-done = bf16[8,256,768]{2,1,0:T(8,128)(2,1)S(1)} async-done(((bf16[8,256,768]{2,1,0:T(8,128)(2,1)}), bf16[8,256,768]{2,1,0:T(8,128)(2,1)S(1)}, u32[]{:S(2)}, u32[]{:S(2)}) %all-to-all-start) | async-done | bytes 3145760 | tf_op jit(solution)/shard_map/all_to_all | solution.py:202
  265.1 16.8 %fusion.65 = f32[8,256,3072]{2,1,0:T(8,128)} fusion(bf16[8,256,768]{2,1,0:T(8,128)(2,1)S(1)} %all-to-all-done, bf16[1,2,768,3072]{3,2,1,0:T(8,128)(2,1)} %all-gather.6.cloned.1.call-done), kind=kOutput, calls=%fused_computation.100 | convolution fusion | flops 9663676416 | bytes 33030144 | tf_op jit(solution)/shard_map/jkcd,kdf->jkcf/dot_general | solution.py:206
  282.0 21.9 %fusion.79 = bf16[8,256,768]{2,1,0:T(8,128)(2,1)} fusion(bf16[1,2,768,3072]{3,2,1,0:T(8,128)(2,1)} %all-gather.6.cloned.1.call-done, f32[8,256,3072]{2,1,0:T(8,128)} %fusion.65), kind=kOutput, calls=%fused_computation.127 | convolution fusion | flops 9721872384 | bytes 33030144 | tf_op jit(solution)/shard_map/jkcf,kdf->jkcd/dot_general | solution.py:211
  334.9 45.1 %all-to-all-done.1 = bf16[8,256,768]{2,1,0:T(8,128)(2,1)} async-done(((bf16[8,256,768]{2,1,0:T(8,128)(2,1)}), bf16[8,256,768]{2,1,0:T(8,128)(2,1)}, u32[]{:S(2)}, u32[]{:S(2)}) %all-to-all-start.1) | async-done | bytes 3145760 | tf_op jit(solution)/shard_map/all_to_all | solution.py:215
  405.0 74.3 %all_to_all.20 = bf16[8,256,768]{2,1,0:T(8,128)(2,1)S(1)} all-to-all(bf16[8,256,768]{2,1,0:T(8,128)(2,1)S(1)} %broadcast_select_fusion), channel_id=1, replica_groups=mesh['dp'=4,'expert'=8] {'expert'}, dimensions={0} | all-to-all | bytes 6291456 | tf_op jit(solution)/shard_map/all_to_all | solution.py:230
  479.2 28.9 %fusion.30 = bf16[8,1,256,3072]{3,2,0,1:T(8,128)(2,1)} fusion(f32[8,256,3072]{2,1,0:T(8,128)} %fusion.65, bf16[8,256,768]{2,1,0:T(8,128)(2,1)S(1)} %all_to_all.20, bf16[1,2,768,3072]{3,2,1,0:T(8,128)(2,1)} %all-gather.6.cloned.1.call-done), kind=kOutput, calls=%fused_computation.54 | convolution fusion | flops 9802088448 | bytes 45613056 | tf_op jit(solution)/shard_map/jkcd,kdf->jkcf/dot_general | solution.py:232
  508.2 14.1 %fusion.82 = bf16[8,256,768]{2,1,0:T(8,128)(2,1)} fusion(bf16[1,2,768,3072]{3,2,1,0:T(8,128)(2,1)S(1)} %bitcast.244, bf16[8,1,256,3072]{3,2,0,1:T(8,128)(2,1)} %fusion.30), kind=kOutput, calls=%fused_computation.128 | convolution fusion | flops 9665249280 | bytes 20447232 | tf_op jit(solution)/shard_map/jkcf,kdf->jkcd/dot_general | solution.py:236
  526.0 71.4 %all-to-all-done.3 = bf16[8,256,768]{2,1,0:T(8,128)(2,1)S(1)} async-done(((bf16[8,256,768]{2,1,0:T(8,128)(2,1)}), bf16[8,256,768]{2,1,0:T(8,128)(2,1)S(1)}, u32[]{:S(2)}, u32[]{:S(2)}) %all-to-all-start.3) | async-done | bytes 3145760 | tf_op jit(solution)/shard_map/all_to_all | solution.py:240
  622.6 168.3 %while.38 = (s32[]{:T(128)}, bf16[1024,12,64]{0,2,1:T(8,128)(2,1)}, f32[1024,12,64]{0,2,1:T(8,128)}, f32[1024,12,64]{0,2,1:T(8,128)}, s32[1,1024]{1,0:T(1,128)S(...) while((s32[]{:T(128)}, bf16[1024,12,64]{0,2,1:T(8,128)(2,1)}, ...), condition=%wide.region_23.24_spmd.clone, body=%wide.region_21.23_spmd.clone.sunk | while | flops 4126796288 | bytes 225638880 | solution.py:110
  634.9 13.3 %bitcast_add_fusion.5 = f32[1024,12,64]{0,2,1:T(8,128)} fusion(f32[1024,12,64]{0,2,1:T(8,128)} %get-tuple-element.880, f32[12,512,1024]{2,1,0:T(8,128)} %fusion.192, f32[12,512]{1,0:T(8,128)S(1)} %constant_dynamic-slice_fusion.4, pred[512,1024]{1,0:T(8,128)(4,1)S(1)} %fusion.193, pred[]{:T(512)S(6)} %compare.23, ...), kind=kOutput, calls=%fused_computation.29.clone.1 | convolution fusion | flops 832045056 | bytes 32800772 | tf_op jit(solution)/shard_map/while/body/eval_jaxpr/hqk,qhd->khd/dot_general | solution.py:98
  648.2 18.1 %multiply_reduce_fusion.7 = (f32[12,512]{1,0:T(8,128)S(1)}, f32[12,512,1024]{2,1,0:T(8,128)}) fusion(f32[12,512,1024]{2,1,0:T(8,128)} %fusion.192, f32[12,512]{1,0:T(8,128)S(1)} %constant_dynamic-slice_fusion.4, pred[512,1024]{1,0:T(8,128)(4,1)S(1)} %fusion.193, bf16[1024,12,64]{0,2,1:T(8,128)(2,1)} %get-tuple-element.905, ...), kind=kOutput, calls=%fused_computation.24.clone.1 | convolution fusion | flops 836757504 | bytes 53264388 | tf_op jit(solution)/shard_map/while/body/eval_jaxpr/qhd,khd->hqk/dot_general | solution.py:85
  666.3 21.3 %multiply_convert_fusion.3 = bf16[12,512,1024]{2,1,0:T(8,128)(2,1)} fusion(f32[12,512,1024]{2,1,0:T(8,128)} %get-tuple-element.812, f32[12,512,1024]{2,1,0:T(8,128)} %fusion.192, f32[12,512]{1,0:T(8,128)S(1)} %get-tuple-element.813, f32[12,512]{1,0:T(8,128)S(1)} %constant_dynamic-slice_fusion.4, pred[512,1024]{1,0:T(8,128)(4,1)S(1)} %fusion.193), kind=kLoop, calls=%fused_computation.23.clone.1 | loop fusion | flops 37748736 | bytes 63488000 | tf_op jit(solution)/shard_map/while/body/eval_jaxpr/convert_element_type | solution.py:89
  717.8 14.2 %bitcast_add_fusion.5 = f32[1024,12,64]{0,2,1:T(8,128)} fusion(f32[1024,12,64]{0,2,1:T(8,128)} %get-tuple-element.880, f32[12,512,1024]{2,1,0:T(8,128)} %fusion.192, f32[12,512]{1,0:T(8,128)S(1)} %constant_dynamic-slice_fusion.4, pred[512,1024]{1,0:T(8,128)(4,1)S(1)} %fusion.193, pred[]{:T(512)S(6)} %compare.23, ...), kind=kOutput, calls=%fused_computation.29.clone.1 | convolution fusion | flops 832045056 | bytes 32800772 | tf_op jit(solution)/shard_map/while/body/eval_jaxpr/hqk,qhd->khd/dot_general | solution.py:98
  732.1 18.1 %multiply_reduce_fusion.7 = (f32[12,512]{1,0:T(8,128)S(1)}, f32[12,512,1024]{2,1,0:T(8,128)}) fusion(f32[12,512,1024]{2,1,0:T(8,128)} %fusion.192, f32[12,512]{1,0:T(8,128)S(1)} %constant_dynamic-slice_fusion.4, pred[512,1024]{1,0:T(8,128)(4,1)S(1)} %fusion.193, bf16[1024,12,64]{0,2,1:T(8,128)(2,1)} %get-tuple-element.905, ...), kind=kOutput, calls=%fused_computation.24.clone.1 | convolution fusion | flops 836757504 | bytes 53264388 | tf_op jit(solution)/shard_map/while/body/eval_jaxpr/qhd,khd->hqk/dot_general | solution.py:85
  750.2 21.3 %multiply_convert_fusion.3 = bf16[12,512,1024]{2,1,0:T(8,128)(2,1)} fusion(f32[12,512,1024]{2,1,0:T(8,128)} %get-tuple-element.812, f32[12,512,1024]{2,1,0:T(8,128)} %fusion.192, f32[12,512]{1,0:T(8,128)S(1)} %get-tuple-element.813, f32[12,512]{1,0:T(8,128)S(1)} %constant_dynamic-slice_fusion.4, pred[512,1024]{1,0:T(8,128)(4,1)S(1)} %fusion.193), kind=kLoop, calls=%fused_computation.23.clone.1 | loop fusion | flops 37748736 | bytes 63488000 | tf_op jit(solution)/shard_map/while/body/eval_jaxpr/convert_element_type | solution.py:89
  828.3 15.8 %fusion.59 = bf16[1,1,768,3072]{3,2,1,0:T(8,128)(2,1)} fusion(bf16[8,256,768]{2,1,0:T(8,128)(2,1)S(1)} %copy-done.28, bf16[8,1,256,3072]{3,2,0,1:T(8,128)(2,1)} %fusion.30), kind=kOutput, calls=%fused_computation.98 | convolution fusion | flops 9666035712 | bytes 20447232 | tf_op jit(solution)/shard_map/jkcd,jkcf->kdf/dot_general | solution.py:248
  844.1 17.5 %fusion.62 = bf16[1,1,768,3072]{3,2,1,0:T(8,128)(2,1)} fusion(bf16[8,256,768]{2,1,0:T(8,128)(2,1)S(1)} %copy-done.30, f32[8,256,3072]{2,1,0:T(8,128)} %fusion.65), kind=kOutput, calls=%fused_computation.99 | convolution fusion | flops 9722658816 | bytes 33030144 | tf_op jit(solution)/shard_map/jkcd,jkcf->kdf/dot_general | solution.py:249
  888.8 37.8 %all-reduce.1 = f32[10,768]{1,0:T(8,128)S(1)} all-reduce(f32[10,768]{1,0:T(8,128)S(1)} %pad_maximum_fusion.5), channel_id=3, replica_groups=mesh['dp'=4,'expert'=8] {'dp','expert'}, use_global_device_ids=true, to_apply=%region_30.31.clone | all-reduce | flops 7680 | bytes 61440
  927.3 88.5 %all-reduce.4.cloned.1.call-done = f32[4,768,768]{2,0,1:T(4,128)} async-done(((f32[4,768,768]{2,0,1:T(4,128)}), f32[4,768,768]{2,0,1:T(4,128)}) %all-reduce.4.cloned.1.call-update) | async-done | bytes 9437200
  1019.5 94.7 %reduce-scatter.3.cloned.1.call-done = bf16[1,2,768,768]{3,2,1,0:T(8,128)(2,1)} async-done(((bf16[1,2,768,3072]{3,2,1,0:T(8,128)(2,1)}), bf16[1,2,768,768]{3,2,1,0:T(8,128)(2,1)}) %reduce-scatter.3.cloned.1.call-update) | async-done | bytes 2359312 | tf_op jit(solution)/shard_map/reduce_scatter | solution.py:252
  1120.7 39.3 %psum.7 = f32[]{:T(128)} all-reduce(f32[]{:T(128)S(6)} %add.354), channel_id=1, replica_groups=mesh['dp'=4,'expert'=8] {'dp','expert'}, use_global_device_ids=true, to_apply=%region_34.35 | all-reduce | flops 1 | bytes 8 | tf_op jit(solution)/shard_map/psum | solution.py:304
  1163.9 13.3 %multiply_add_fusion = (f32[1,2,768,768]{3,2,1,0:T(8,128)}, f32[1,2,768,768]{3,2,1,0:T(8,128)}, f32[1,2,768,768]{3,2,1,0:T(8,128)}, f32[1,2,768,768]{3,2,1,0:T(8,128)}) fusion(f32[1,2,768,768]{3,2,1,0:T(8,128)} %param.41, f32[1,2,768,768]{3,2,1,0:T(8,128)} %param.32, f32[]{:T(128)S(6)} %min.22, bf16[1,2,768,768]{3,2,1,0:T(8,128)(2,1)S(1)} %copy-done.26, ...), kind=kLoop, calls=%fused_computation.95 | loop fusion | flops 23592960 | bytes 40108036 | tf_op jit(solution)/shard_map/add | solution.py:122
  (313 shorter events, 362.7 us)
Async XLA Ops:
  7.2 70.9 %all-gather.4.cloned.1.call-start = ((), (), s32[]{:S(2)}) async-start(), calls=%async_computation.5 | async-start | bytes 4866048 | tf_op jit(solution)/shard_map/all_gather | solution.py:155
  9.0 184.7 %all-gather.6.cloned.1.call-start = ((), (), s32[]{:S(2)}) async-start(), calls=%async_computation.6 | async-start | bytes 11796480 | tf_op jit(solution)/shard_map/all_gather | solution.py:205
  14.1 54.7 %copy-start.34 = (bf16[1024,768]{1,0:T(8,128)(2,1)S(1)}, bf16[1024,768]{1,0:T(8,128)(2,1)}, u32[]{:S(2)}) copy-start(bf16[1024,768]{1,0:T(8,128)(2,1)} %param.23) | copy-start | bytes 4718596
  174.6 435.7 %copy-start.44 = (f32[1024]{0:T(1024)}, f32[1024]{0:T(1024)S(1)}, u32[]{:S(2)}) copy-start(f32[1024]{0:T(1024)S(1)} %broadcast_multiply_fusion) | copy-start | bytes 12292
  175.0 435.3 %copy-start.48 = (f32[1024]{0:T(1024)}, f32[1024]{0:T(1024)S(1)}, u32[]{:S(2)}) copy-start(f32[1024]{0:T(1024)S(1)} %fusion.115) | copy-start | bytes 12292
  190.0 75.1 %all-to-all-start = ((bf16[8,256,768]{2,1,0:T(8,128)(2,1)}), bf16[8,256,768]{2,1,0:T(8,128)(2,1)S(1)}, u32[]{:S(2)}, u32[]{:S(2)}) async-start(bf16[8,256,768]{2,1,0:T(8,128)(2,1)} %broadcast_select_fusion.1), calls=%async_computation | async-start | bytes 6291456 | tf_op jit(solution)/shard_map/all_to_all | solution.py:202
  303.9 76.1 %all-to-all-start.1 = ((bf16[8,256,768]{2,1,0:T(8,128)(2,1)}), bf16[8,256,768]{2,1,0:T(8,128)(2,1)}, u32[]{:S(2)}, u32[]{:S(2)}) async-start(bf16[8,256,768]{2,1,0:T(8,128)(2,1)} %fusion.79), calls=%async_computation.1 | async-start | bytes 6291456 | tf_op jit(solution)/shard_map/all_to_all | solution.py:215
  308.5 24.9 %copy-start.9 = (f32[1024,768]{0,1:T(8,128)S(1)}, f32[1024,768]{0,1:T(8,128)}, u32[]{:S(2)}) copy-start(f32[1024,768]{0,1:T(8,128)} %copy-done.8) | copy-start | bytes 9437188
  313.2 292.5 %copy-start.55 = (s32[1024]{0:T(1024)}, s32[1024]{0:T(1024)S(1)}, u32[]{:S(2)}) copy-start(s32[1024]{0:T(1024)S(1)} %scatter_custom_fusion) | copy-start | bytes 12292
  405.0 103.2 %slice-start = ((s8[9437184]{0:T(1024)(128)(4,1)}), s8[4194304]{0:T(1024)(128)(4,1)S(1)}, s32[]{:S(2)}) async-start(s8[9437184]{0:T(1024)(128)(4,1)} %bitcast.243), calls=%async_computation.9 | async-start | bytes 8388608
  479.2 28.9 %copy-start.29 = (bf16[8,256,768]{2,1,0:T(8,128)(2,1)}, bf16[8,256,768]{2,1,0:T(8,128)(2,1)S(1)}, u32[]{:S(2)}) copy-start(bf16[8,256,768]{2,1,0:T(8,128)(2,1)S(1)} %all_to_all.20) | copy-start | bytes 9437188
  479.2 28.9 %slice-start.1 = ((s8[9437184]{0:T(1024)(128)(4,1)}), s8[4194304]{0:T(1024)(128)(4,1)S(1)}, s32[]{:S(2)}) async-start(s8[9437184]{0:T(1024)(128)(4,1)} %bitcast.243), calls=%async_computation.10 | async-start | bytes 8388608
  479.2 28.9 %slice-start.2 = ((s8[9437184]{0:T(1024)(128)(4,1)}), s8[1048576]{0:T(1024)(128)(4,1)S(1)}, s32[]{:S(2)}) async-start(s8[9437184]{0:T(1024)(128)(4,1)} %bitcast.243), calls=%async_computation.11 | async-start | bytes 2097152
  522.3 75.1 %all-to-all-start.3 = ((bf16[8,256,768]{2,1,0:T(8,128)(2,1)}), bf16[8,256,768]{2,1,0:T(8,128)(2,1)S(1)}, u32[]{:S(2)}, u32[]{:S(2)}) async-start(bf16[8,256,768]{2,1,0:T(8,128)(2,1)} %fusion.82), calls=%async_computation.3 | async-start | bytes 6291456 | tf_op jit(solution)/shard_map/all_to_all | solution.py:240
  525.9 489.9 %all-reduce.4.cloned.1.call-start = ((), (), s32[]{:S(2)}) async-start(), calls=%async_computation.8 | async-start | bytes 18874368
  526.0 79.7 %copy-start.59 = (f32[1024]{0:T(1024)}, f32[1024]{0:T(1024)S(1)}, u32[]{:S(2)}) copy-start(f32[1024]{0:T(1024)S(1)} %subtract_multiply_fusion) | copy-start | bytes 12292
  826.4 287.8 %reduce-scatter.3.cloned.1.call-start = ((), (), s32[]{:S(2)}) async-start(), calls=%async_computation.7 | async-start | bytes 11796480 | tf_op jit(solution)/shard_map/reduce_scatter | solution.py:252
  888.8 229.5 %copy-start.24 = (f32[1024,768]{0,1:T(8,128)S(1)}, f32[1024,768]{0,1:T(8,128)}, u32[]{:S(2)}) copy-start(f32[1024,768]{0,1:T(8,128)} %get-tuple-element.680) | copy-start | bytes 9437188
  1118.3 42.4 %copy-start.70 = (f32[10,24]{1,0:T(8,128)S(1)}, f32[10,24]{1,0:T(8,128)}, u32[]{:S(2)}) copy-start(f32[10,24]{1,0:T(8,128)} %param.31) | copy-start | bytes 2884
  1118.3 42.4 %copy-start.73 = (f32[10,24]{1,0:T(8,128)S(1)}, f32[10,24]{1,0:T(8,128)}, u32[]{:S(2)}) copy-start(f32[10,24]{1,0:T(8,128)} %param.38) | copy-start | bytes 2884
  1118.3 42.4 %copy-start.74 = (f32[10,24]{1,0:T(8,128)S(1)}, f32[10,24]{1,0:T(8,128)}, u32[]{:S(2)}) copy-start(f32[10,24]{1,0:T(8,128)} %param.36) | copy-start | bytes 2884
  1118.4 42.4 %copy-start.75 = (f32[10,24]{1,0:T(8,128)S(1)}, f32[10,24]{1,0:T(8,128)}, u32[]{:S(2)}) copy-start(f32[10,24]{1,0:T(8,128)} %param.37) | copy-start | bytes 2884
  1118.4 43.1 %copy-start.39 = (f32[4,24,768]{2,1,0:T(8,128)S(1)}, f32[4,24,768]{2,1,0:T(8,128)}, u32[]{:S(2)}) copy-start(f32[4,24,768]{2,1,0:T(8,128)} %param.30) | copy-start | bytes 884740
  1120.7 43.2 %copy-start.26 = (bf16[1,2,768,768]{3,2,1,0:T(8,128)(2,1)S(1)}, bf16[1,2,768,768]{3,2,1,0:T(8,128)(2,1)}, u32[]{:S(2)}) copy-start(bf16[1,2,768,768]{3,2,1,0:T(8,128)(2,1)} %reduce-scatter.3.cloned.1.call-done) | copy-start | bytes 7077892
  (72 other events, 486.8 us)
Sparse Core Ops, SparseCore 0:
  11.6 66.4 all-gather.3
  80.5 95.1 all-gather.5
  826.5 189.2 all-reduce.3
  1019.1 95.0 reduce-scatter.2
where the time goes:
time: 1200 us; the launch traced here: 1190 us
  waiting for transfers between devices  379 us (32%)
  matrix products  313 us (26%)
  blocking collectives  195 us (16%)
  other arithmetic  133 us (11%)
  local copies, waits for them, and re-layouts  131 us (11%)
  between operations  20.2 us (2%)
  starting transfers between devices  12.1 us (1%)
    reduce_scatter x1, waiting for transfers between devices, shards(): lax.psum_scatter(jnp.stack([grad_up, grad_down], axis=1).astype(jnp.bfloa...  94.7 us
    unnamed x5, waiting for transfers between devices  88.5 us
    all_to_all x1, blocking collectives, shards(): lax.all_to_all(grad_rows, 'expert', split_axis=0, concat_axis=0, tiled=True)  74.3 us
    all_to_all x1, waiting for transfers between devices, shards(): lax.all_to_all(send_rows, 'expert', split_axis=0, concat_axis=0, tiled=True)  71.4 us
    all_to_all x1, waiting for transfers between devices, shards(): lax.all_to_all(grad_sent_low.reshape(experts_total, capacity, model_width...  71.4 us
    all_to_all x1, waiting for transfers between devices, shards(): lax.all_to_all(produced_low.reshape(experts_total, capacity, model_width)...  45.1 us
    dot_general x4, matrix products, block_scores(): jnp.einsum('qhd,khd->hqk', query_block, key_seq, preferred_element_type=j...  44.3 us
    all_gather x1, blocking collectives, shards(): lax.all_gather(vector_params.astype(jnp.bfloat16), ('dp', 'expert'), axis...  44.1 us
  transfers between devices with their start and end apart: 7, of which 6 were waited for; matrix products, arithmetic and copies ran while one was open for 17% of the time, Pallas kernels for 0%

commit v1 on v0

--- a/solution.py
+++ b/solution.py
@@ -1,12 +1,16 @@
+from functools import partial
+
 import jax
 import jax.numpy as jnp
 from jax import lax
+from jax.experimental import pallas as pl
+from jax.experimental.pallas import tpu as pltpu
 from jax.sharding import PartitionSpec as P
 
 HEADS = 12
 HEAD_DIM = 64
 LEN = 1024
-QBLK = 512
+WINDOW = 512
 NDOM = 8
 STEP = 10
 
@@ -30,84 +34,99 @@
     return center * lax.rsqrt(spread + norm_eps) * gain_row
 
 
-def block_scores(query_block, key_seq, documents, block_first, seq_start):
-    score_scale = HEAD_DIM ** (-0.5)
-    scores = (
-        jnp.einsum("qhd,khd->hqk", query_block, key_seq, preferred_element_type=jnp.float32)
-        * score_scale
-    )
-    query_pos = block_first - seq_start + jnp.arange(QBLK)
-    key_pos = jnp.arange(LEN)
-    query_docs = lax.dynamic_slice_in_dim(documents, block_first, QBLK)
-    allowed = (key_pos[None, :] <= query_pos[:, None]) & (documents[None, :] == query_docs[:, None])
-    return jnp.where(allowed[None], scores, masked_score)
-
-
-def attend_forward(queries, keys_all, values_all, documents):
-    tokens = queries.shape[0]
-
-    def one_block(block_index, carried):
-        attn_mixed, totals = carried
-        block_first = block_index * QBLK
-        seq_start = block_first // LEN * LEN
-        query_block = lax.dynamic_slice_in_dim(queries, block_first, QBLK)
-        scores = block_scores(query_block, keys_all, documents, block_first, seq_start)
-        score_top = jnp.max(scores, axis=-1, keepdims=True)
-        weights = jnp.exp(scores - score_top)
-        weight_total = jnp.sum(weights, axis=-1, keepdims=True)
-        probs_low = (weights / weight_total).astype(jnp.bfloat16)
-        block_out = jnp.einsum(
-            "hqk,khd->qhd", probs_low, values_all, preferred_element_type=jnp.float32
-        )
-        attn_mixed = lax.dynamic_update_slice_in_dim(attn_mixed, block_out, block_first, 0)
-        totals = lax.dynamic_update_slice_in_dim(
-            totals, (score_top + jnp.log(weight_total))[:, :, 0], block_first, 1
-        )
-        return (attn_mixed, totals)
-
-    initial = (jnp.zeros(queries.shape, jnp.float32), jnp.zeros((HEADS, tokens), jnp.float32))
-    return lax.fori_loop(0, tokens // QBLK, one_block, initial)
-
-
-def attend_backward(queries, keys_all, values_all, documents, totals, grad_mixed):
-    tokens = queries.shape[0]
-    score_scale = HEAD_DIM ** (-0.5)
-
-    def one_block(block_index, carried):
-        grad_queries, grad_keys, grad_values = carried
-        block_first = block_index * QBLK
-        seq_start = block_first // LEN * LEN
-        query_block = lax.dynamic_slice_in_dim(queries, block_first, QBLK)
-        grad_block = lax.dynamic_slice_in_dim(grad_mixed, block_first, QBLK)
-        scores = block_scores(query_block, keys_all, documents, block_first, seq_start)
-        block_totals = lax.dynamic_slice_in_dim(totals, block_first, QBLK, 1)
-        probabilities = jnp.exp(scores - block_totals[:, :, None])
-        grad_probs = jnp.einsum(
-            "qhd,khd->hqk", grad_block, values_all, preferred_element_type=jnp.float32
-        )
-        inner = jnp.sum(probabilities * grad_probs, axis=-1, keepdims=True)
-        grad_scores = (probabilities * (grad_probs - inner)).astype(jnp.bfloat16)
-        query_part = (
-            jnp.einsum("hqk,khd->qhd", grad_scores, keys_all, preferred_element_type=jnp.float32)
-            * score_scale
-        )
-        key_part = (
-            jnp.einsum("hqk,qhd->khd", grad_scores, query_block, preferred_element_type=jnp.float32)
-            * score_scale
-        )
-        value_part = jnp.einsum(
-            "hqk,qhd->khd",
-            probabilities.astype(jnp.bfloat16),
-            grad_block,
-            preferred_element_type=jnp.float32,
-        )
-        grad_queries = lax.dynamic_update_slice_in_dim(grad_queries, query_part, block_first, 0)
-        grad_keys = grad_keys + key_part
-        grad_values = grad_values + value_part
-        return (grad_queries, grad_keys, grad_values)
-
-    zeroed = jnp.zeros(queries.shape, jnp.float32)
-    return lax.fori_loop(0, tokens // QBLK, one_block, (zeroed, zeroed, zeroed))
+NT = (((1,), (1,)), ((), ()))
+TN = (((0,), (0,)), ((), ()))
+
+
+def fwd_kernel(QB, q_ref,k_ref,v_ref,dcol_ref,drow_ref,o_ref,lse_ref,bias_ref):
+    reach = WINDOW//QB
+    low_lane = lax.broadcasted_iota(jnp.int32,(QB,128),1) < HEAD_DIM
+    @pl.when(pl.program_id(0)==0)
+    def _():
+        for i in range(LEN//QB):
+            first=max(0,i-reach)*QB; W=(i+1)*QB-first
+            qp=i*QB+lax.broadcasted_iota(jnp.int32,(QB,W),0)
+            kp=first+lax.broadcasted_iota(jnp.int32,(QB,W),1)
+            ok=(kp<=qp)&(dcol_ref[i*QB:(i+1)*QB,:]==drow_ref[:,first:first+W])
+            bias_ref[i*QB:(i+1)*QB,:W]=jnp.where(ok,0.0,masked_score)
+    for i in range(LEN//QB):
+        rows=slice(i*QB,(i+1)*QB)
+        first=max(0,i-reach)*QB; W=(i+1)*QB-first
+        q=q_ref[0,rows,:]*jnp.bfloat16(HEAD_DIM**-0.5)
+        zero=jnp.zeros_like(q)
+        qs=jnp.concatenate([jnp.where(low_lane,q,zero),jnp.where(low_lane,zero,q)],axis=0)
+        s=lax.dot_general(qs,k_ref[0,first:first+W,:],NT,preferred_element_type=jnp.float32)
+        s=(s.reshape(2,QB,W)+bias_ref[rows,:W][None]).reshape(2*QB,W)
+        top=jnp.max(s,axis=1,keepdims=True)
+        e=jnp.exp(s-top)
+        total=jnp.sum(e,axis=1,keepdims=True)
+        p=(e*(1.0/total)).astype(jnp.bfloat16)
+        o=jnp.dot(p,v_ref[0,first:first+W,:],preferred_element_type=jnp.float32)
+        o_ref[rows,:]=jnp.where(low_lane,o[:QB],o[QB:]).astype(jnp.bfloat16)
+        lse=top+jnp.log(total)
+        lse_ref[0,rows,:]=jnp.where(low_lane,lse[:QB],lse[QB:])
+
+def attend_forward(projected, documents, QB=256):
+    T=projected.shape[1]; D=projected.shape[2]
+    dcol=documents.reshape(T,1); drow=documents.reshape(1,T)
+    def sp(c): return pl.BlockSpec((1,T,128),lambda h,c=c:(c,0,h))
+    return pl.pallas_call(partial(fwd_kernel,QB),grid=(D//128,),
+        in_specs=[sp(0),sp(1),sp(2),pl.BlockSpec((T,1),lambda h:(0,0)),pl.BlockSpec((1,T),lambda h:(0,0))],
+        out_specs=[pl.BlockSpec((T,128),lambda h:(0,h)),pl.BlockSpec((1,T,128),lambda h:(h,0,0))],
+        out_shape=[jax.ShapeDtypeStruct((T,D),jnp.bfloat16),jax.ShapeDtypeStruct((D//128,T,128),jnp.float32)],
+        scratch_shapes=[pltpu.VMEM((T,min(T,WINDOW+QB)),jnp.float32)],
+        compiler_params=pltpu.CompilerParams(vmem_limit_bytes=48*2**20),
+    )(projected,projected,projected,dcol,drow)
+
+def bwd_kernel(QB,q_ref,k_ref,v_ref,lse_ref,g_ref,dcol_ref,drow_ref,out_ref,bias_ref,dk_ref,dv_ref):
+    reach=WINDOW//QB
+    low_lane = lax.broadcasted_iota(jnp.int32,(QB,128),1) < HEAD_DIM
+    @pl.when(pl.program_id(0)==0)
+    def _():
+        for i in range(LEN//QB):
+            first=max(0,i-reach)*QB; W=(i+1)*QB-first
+            kp=first+lax.broadcasted_iota(jnp.int32,(W,QB),0)
+            qp=i*QB+lax.broadcasted_iota(jnp.int32,(W,QB),1)
+            ok=(kp<=qp)&(dcol_ref[first:first+W,:]==drow_ref[:,i*QB:(i+1)*QB])
+            bias_ref[:W,i*QB:(i+1)*QB]=jnp.where(ok,0.0,masked_score)
+    dk_ref[...]=jnp.zeros_like(dk_ref)
+    dv_ref[...]=jnp.zeros_like(dv_ref)
+    for i in range(LEN//QB):
+        rows=slice(i*QB,(i+1)*QB)
+        first=max(0,i-reach)*QB; W=(i+1)*QB-first
+        keys=slice(first,first+W)
+        q=q_ref[0,rows,:]*jnp.bfloat16(HEAD_DIM**-0.5)
+        zero=jnp.zeros_like(q)
+        qs=jnp.concatenate([jnp.where(low_lane,q,zero),jnp.where(low_lane,zero,q)],axis=0)
+        g=g_ref[rows,:]
+        gs=jnp.concatenate([jnp.where(low_lane,g,zero),jnp.where(low_lane,zero,g)],axis=0)
+        k=k_ref[0,keys,:]
+        st=lax.dot_general(k,qs,NT,preferred_element_type=jnp.float32)
+        bias=bias_ref[:W,rows]
+        lse=jnp.transpose(lse_ref[0,rows,:])
+        lse=jnp.concatenate([lse[0:1,:],lse[64:65,:]],axis=1)
+        p=jnp.exp(st+jnp.concatenate([bias,bias],axis=1)-lse)
+        dp=lax.dot_general(v_ref[0,keys,:],gs,NT,preferred_element_type=jnp.float32)
+        inner=jnp.sum(p*dp,axis=0,keepdims=True)
+        ds=(p*(dp-inner)).astype(jnp.bfloat16)
+        dk_ref[keys,:]+=jnp.dot(ds,qs,preferred_element_type=jnp.float32)
+        dv_ref[keys,:]+=jnp.dot(p.astype(jnp.bfloat16),gs,preferred_element_type=jnp.float32)
+        dq=lax.dot_general(ds,k,TN,preferred_element_type=jnp.float32)
+        out_ref[0,rows,:]=(jnp.where(low_lane,dq[:QB],dq[QB:])*HEAD_DIM**-0.5).astype(jnp.bfloat16)
+    out_ref[1,:,:]=dk_ref[...].astype(jnp.bfloat16)
+    out_ref[2,:,:]=dv_ref[...].astype(jnp.bfloat16)
+
+def attend_backward(projected, documents, lse, grad_mixed, QB=256):
+    T=projected.shape[1]; D=projected.shape[2]
+    dcol=documents.reshape(T,1); drow=documents.reshape(1,T)
+    def sp(c): return pl.BlockSpec((1,T,128),lambda h,c=c:(c,0,h))
+    return pl.pallas_call(partial(bwd_kernel,QB),grid=(D//128,),
+        in_specs=[sp(0),sp(1),sp(2),pl.BlockSpec((1,T,128),lambda h:(h,0,0)),pl.BlockSpec((T,128),lambda h:(0,h)),pl.BlockSpec((T,1),lambda h:(0,0)),pl.BlockSpec((1,T),lambda h:(0,0))],
+        out_specs=pl.BlockSpec((3,T,128),lambda h:(0,0,h)),
+        out_shape=jax.ShapeDtypeStruct((3,T,D),jnp.bfloat16),
+        scratch_shapes=[pltpu.VMEM((min(T,WINDOW+QB),T),jnp.float32),pltpu.VMEM((T,128),jnp.float32),pltpu.VMEM((T,128),jnp.float32)],
+        compiler_params=pltpu.CompilerParams(vmem_limit_bytes=48*2**20),
+    )(projected,projected,projected,lse,grad_mixed,dcol,drow)
 
 
 def adam_update(weight, gradient, first_moment, second_moment, average, factor, rate):
@@ -172,22 +191,30 @@
     sorted_pick = sorted_expert[:, None] == jnp.arange(experts_total)[None, :]
     sorted_start = jnp.sum(jnp.where(sorted_pick, count_starts[None, :], 0), axis=1)
     sorted_slot = sorted_expert * capacity + sorted_pos - sorted_start
-    token_slot = jnp.zeros((tokens,), jnp.int32).at[row_order].set(sorted_slot)
-    token_expert = jnp.zeros((tokens,), jnp.int32).at[row_order].set(sorted_expert)
+    at_token = row_order[:, None] == jnp.arange(tokens)[None, :]
+    token_slot = jnp.sum(jnp.where(at_token, sorted_slot[:, None], 0), axis=0)
+    token_expert = token_slot // capacity
     expert_pick = (token_expert[:, None] == jnp.arange(experts_total)[None, :]).astype(jnp.float32)
-    slot_valid = (jnp.arange(capacity)[None, :] < row_counts[:, None]).reshape(-1)
-    slot_position = (count_starts[:, None] + jnp.arange(capacity)[None, :]).reshape(-1)
-    slot_token = row_order[jnp.minimum(slot_position, tokens - 1)]
+    slot_pick = token_slot[:, None] == jnp.arange(experts_total * capacity)[None, :]
+    slot_pick = slot_pick.astype(jnp.bfloat16)
+
+    def to_slots(rows):
+        placed = jnp.dot(slot_pick.T, rows, preferred_element_type=jnp.float32)
+        return placed.astype(jnp.bfloat16).reshape(experts_total, capacity, model_width)
+
+    def from_slots(rows):
+        return jnp.dot(
+            slot_pick, rows.reshape(-1, model_width), preferred_element_type=jnp.float32
+        )
+
     inputs_float = inputs.astype(jnp.float32)
     normed_one, norm_one_back = jax.vjp(layer_norm, inputs_float, vector_low[0].astype(jnp.float32))
     normed_low = normed_one.astype(jnp.bfloat16)
     projected = jnp.einsum(
         "td,cde->cte", normed_low, dense_low[:3], preferred_element_type=jnp.float32
     ).astype(jnp.bfloat16)
-    shaped = projected.reshape(3, tokens, HEADS, HEAD_DIM)
     documents = document_ids.reshape(-1)
-    attn_mixed, totals = attend_forward(shaped[0], shaped[1], shaped[2], documents)
-    mixed_low = attn_mixed.reshape(tokens, model_width).astype(jnp.bfloat16)
+    mixed_low, totals = attend_forward(projected, documents)
     hidden_state = inputs_float + jnp.dot(
         mixed_low, dense_low[3], preferred_element_type=jnp.float32
     )
@@ -196,9 +223,7 @@
     logits = jnp.dot(normed_two, centroids.T, precision=lax.Precision.HIGHEST)
     gate_value = jax.nn.sigmoid(jnp.sum(logits * expert_pick, axis=1))
     sent_rows = normed_two.astype(jnp.bfloat16)
-    send_rows = jnp.where(slot_valid[:, None], sent_rows[slot_token], 0).reshape(
-        experts_total, capacity, model_width
-    )
+    send_rows = to_slots(sent_rows)
     received = lax.all_to_all(send_rows, "expert", split_axis=0, concat_axis=0, tiled=True)
     rows_in = received.reshape(owners, local_experts, capacity, model_width)
     own_low = expert_weights.astype(jnp.bfloat16)
@@ -219,14 +244,12 @@
         concat_axis=0,
         tiled=True,
     )
-    returned_rows = returned.reshape(-1, model_width)[token_slot].astype(jnp.float32)
+    returned_rows = from_slots(returned)
     block_output = hidden_state + gate_value[:, None] * returned_rows
     grad_out = cotangent.astype(jnp.float32) * token_scale[:, None]
     grad_returned = (gate_value[:, None] * grad_out).astype(jnp.bfloat16)
     grad_chosen = jnp.sum(grad_out * returned_rows, axis=1) * gate_value * (1.0 - gate_value)
-    grad_rows = jnp.where(slot_valid[:, None], grad_returned[slot_token], 0).reshape(
-        experts_total, capacity, model_width
-    )
+    grad_rows = to_slots(grad_returned)
     grad_received = lax.all_to_all(grad_rows, "expert", split_axis=0, concat_axis=0, tiled=True)
     grad_in = grad_received.reshape(owners, local_experts, capacity, model_width)
     grad_active = jnp.einsum(
@@ -244,7 +267,7 @@
         concat_axis=0,
         tiled=True,
     )
-    grad_sent_rows = grad_back.reshape(-1, model_width)[token_slot].astype(jnp.float32)
+    grad_sent_rows = from_slots(grad_back)
     grad_up = jnp.einsum("jkcd,jkcf->kdf", rows_in, grad_pre, preferred_element_type=jnp.float32)
     grad_down = jnp.einsum(
         "jkcd,jkcf->kdf", grad_in, active_low, preferred_element_type=jnp.float32
@@ -267,19 +290,7 @@
     grad_mixed = jnp.dot(grad_attn, dense_low[3].T, preferred_element_type=jnp.float32).astype(
         jnp.bfloat16
     )
-    grad_queries, grad_keys, grad_values = attend_backward(
-        shaped[0],
-        shaped[1],
-        shaped[2],
-        documents,
-        totals,
-        grad_mixed.reshape(tokens, HEADS, HEAD_DIM),
-    )
-    grad_proj = (
-        jnp.stack([grad_queries, grad_keys, grad_values])
-        .reshape(3, tokens, model_width)
-        .astype(jnp.bfloat16)
-    )
+    grad_proj = attend_backward(projected, documents, totals, grad_mixed)
     grad_in_proj = jnp.einsum(
         "td,cte->cde", normed_low, grad_proj, preferred_element_type=jnp.float32
     )

time: 1200 us -> 943 us (0.79)
  matrix products: 313 us -> 173 us
  local copies, waits for them, and re-layouts: 131 us -> 28.9 us
  other arithmetic: 133 us -> 56.7 us
  blocking collectives: 195 us -> 270 us
  waiting for transfers between devices: 379 us -> 331 us
  Pallas kernels: 0 us -> 45.1 us
    dot_general x14 -> x4, matrix products: 162 us -> 19.6 us  [the longest x2 9.93 us: to_slots(): placed = jnp.dot(slot_pick.T, rows, preferred_element_type=jnp.float32)]
    all_to_all x0 -> x1, blocking collectives: none -> 74.3 us  [shards(): lax.all_to_all(grad_sent_low.reshape(experts_total, capacity, model_width...]
    all_to_all x1 -> x0, waiting for transfers between devices: 71.4 us -> none  [shards(): lax.all_to_all(grad_sent_low.reshape(experts_total, capacity, model_width...]
    all_gather x1, waiting for transfers between devices: 0.02 us -> 56.7 us  [shards(): expert_low = lax.all_gather(own_low, 'dp', axis=3, tiled=True)]
    all_to_all x1, waiting for transfers between devices: 71.4 us -> 14.9 us  [shards(): lax.all_to_all(send_rows, 'expert', split_axis=0, concat_axis=0, tiled=True)]
    gather x7 -> x0, local copies, waits for them, and re-layouts: 45.4 us -> none  [the longest x2 9.69 us: shards(): returned.reshape(-1, model_width)[token_slot].astype(jnp.float32)]
    pallas_call x0 -> x2, Pallas kernels: none -> 45.1 us  [the longest x1 26.8 us: attend_backward(): pl.pallas_call(partial(bwd_kernel, QB), grid=(D // 128,), in_specs=[sp(0)...]
    convert_element_type x3 -> x1, other arithmetic: 42.9 us -> 1.64 us  [shards(): dense_weights.astype(jnp.bfloat16)]
  transfers between devices with their start and end apart: 7 -> 6, of which waited for: 6 -> 6; matrix products, arithmetic and copies ran while one was open for 17% -> 11% of each run, Pallas kernels for 0% -> 2%
where the time goes in v1:
time: 943 us; the launch traced here: 934 us
  waiting for transfers between devices  331 us (35%)
  blocking collectives  270 us (29%)
  matrix products  173 us (18%)
  other arithmetic  56.7 us (6%)
  Pallas kernels  45.1 us (5%)
  local copies, waits for them, and re-layouts  28.9 us (3%)
  between operations  19.8 us (2%)
  starting transfers between devices  9.77 us (1%)
    reduce_scatter x1, waiting for transfers between devices, shards(): lax.psum_scatter(jnp.stack([grad_up, grad_down], axis=1).astype(jnp.bfloa...  95.3 us
    unnamed x5, waiting for transfers between devices  84.1 us
    all_to_all x1, blocking collectives, shards(): lax.all_to_all(grad_sent_low.reshape(experts_total, capacity, model_width...  74.3 us
    all_to_all x1, blocking collectives, shards(): lax.all_to_all(grad_rows, 'expert', split_axis=0, concat_axis=0, tiled=True)  74.2 us
    all_to_all x1, waiting for transfers between devices, shards(): lax.all_to_all(produced_low.reshape(experts_total, capacity, model_width)...  62.6 us
    all_gather x1, waiting for transfers between devices, shards(): expert_low = lax.all_gather(own_low, 'dp', axis=3, tiled=True)  56.7 us
    all_gather x1, blocking collectives, shards(): lax.all_gather(vector_params.astype(jnp.bfloat16), ('dp', 'expert'), axis...  44.1 us
    psum x1, blocking collectives, shards(): grad_norm = jnp.sqrt(lax.psum(squares, ('dp', 'expert')))  39.5 us
  transfers between devices with their start and end apart: 6, of which 6 were waited for; matrix products, arithmetic and copies ran while one was open for 11% of the time, Pallas kernels for 2%

profile of v1, /device:TPU:0, one launch (start us, length us, event | category | flops | bytes accessed | tf_op | source)
XLA Modules:
  0.0 934.1 jit_solution(13172467513213499383)
XLA Ops:
  14.7 44.1 %all-gather = bf16[32,24,10]{1,2,0:T(8,128)(2,1)S(1)} all-gather(bf16[1,24,10]{1,2,0:T(8,128)(2,1)S(1)} %convert_bitcast_fusion.1), channel_id=1, replica_groups=mesh['dp'=4,'expert'=8] {'dp','expert'}, dimensions={0}, use_global_device_ids=true | all-gather | bytes 15840 | tf_op jit(solution)/shard_map/all_gather | solution.py:175
  61.1 17.3 %all-gather.4.cloned.1.call-done = bf16[4,768,768]{2,1,0:T(8,128)(2,1)} async-done(((bf16[4,24,768]{2,1,0:T(8,128)(2,1)}), bf16[4,768,768]{2,1,0:T(8,128)(2,1)}) %all-gather.4.cloned.1.call-update) | async-done | bytes 4718608 | tf_op jit(solution)/shard_map/all_gather | solution.py:174
  78.4 7.7 convert_bitcast_fusion.q_ref.k_ref.v_ref
  86.1 18.3 %shard_map.298 = (bf16[1024,768]{1,0:T(8,128)(2,1)S(1)}, f32[6,1024,128]{2,1,0:T(8,128)S(1)}) custom-call(bf16[3,1024,768]{2,1,0:T(8,128)(2,1)} %convert_bitcast_fusion.q_ref.k_ref.v_ref, bf16[3,1024,768]{2,1,0:T(8,128)(2,1)} %convert_bitcast_fusion.q_ref.k_ref.v_ref, bf16[3,1024,768]{2,1,0:T(8,128)(2,1)} %convert_bitcast_fusion.q_ref.k_ref.v_ref, ...), custom_call_target="tpu_custom_call" | custom-call | tf_op jit(solution)/shard_map/pallas_call | solution.py:73
  119.3 56.7 %all-gather.6.cloned.1.call-done = bf16[1,2,768,3072]{3,2,1,0:T(8,128)(2,1)} async-done(((bf16[1,2,768,768]{3,2,1,0:T(8,128)(2,1)}), bf16[1,2,768,3072]{3,2,1,0:T(8,128)(2,1)}) %all-gather.6.cloned.1.call-update) | async-done | bytes 9437200 | tf_op jit(solution)/shard_map/all_gather | solution.py:230
  176.0 14.9 %all-to-all-done = bf16[8,256,768]{2,1,0:T(8,128)(2,1)} async-done(((bf16[8,256,768]{2,1,0:T(8,128)(2,1)}), bf16[8,256,768]{2,1,0:T(8,128)(2,1)}, u32[]{:S(2)}, u32[]{:S(2)}) %all-to-all-start) | async-done | bytes 3145760 | tf_op jit(solution)/shard_map/all_to_all | solution.py:227
  190.8 17.5 %fusion.48 = f32[8,256,3072]{2,1,0:T(8,128)} fusion(bf16[8,256,768]{2,1,0:T(8,128)(2,1)} %all-to-all-done, bf16[1,2,768,3072]{3,2,1,0:T(8,128)(2,1)} %all-gather.6.cloned.1.call-done), kind=kOutput, calls=%fused_computation.63 | convolution fusion | flops 9663676416 | bytes 33030144 | tf_op jit(solution)/shard_map/jkcd,kdf->jkcf/dot_general | solution.py:231
  208.3 21.9 %fusion.72 = bf16[8,256,768]{2,1,0:T(8,128)(2,1)} fusion(bf16[1,2,768,3072]{3,2,1,0:T(8,128)(2,1)} %all-gather.6.cloned.1.call-done, f32[8,256,3072]{2,1,0:T(8,128)} %fusion.48), kind=kOutput, calls=%fused_computation.91 | convolution fusion | flops 9721872384 | bytes 33030144 | tf_op jit(solution)/shard_map/jkcf,kdf->jkcd/dot_general | solution.py:236
  243.6 62.6 %all-to-all-done.1 = bf16[8,256,768]{2,1,0:T(8,128)(2,1)} async-done(((bf16[8,256,768]{2,1,0:T(8,128)(2,1)}), bf16[8,256,768]{2,1,0:T(8,128)(2,1)}, u32[]{:S(2)}, u32[]{:S(2)}) %all-to-all-start.1) | async-done | bytes 3145760 | tf_op jit(solution)/shard_map/all_to_all | solution.py:240
  316.4 74.2 %all_to_all.20 = bf16[8,256,768]{2,1,0:T(8,128)(2,1)S(1)} all-to-all(bf16[8,256,768]{2,1,0:T(8,128)(2,1)S(1)} %bitcast.149), channel_id=1, replica_groups=mesh['dp'=4,'expert'=8] {'expert'}, dimensions={0} | all-to-all | bytes 6291456 | tf_op jit(solution)/shard_map/all_to_all | solution.py:253
  390.6 28.9 %fusion.2 = bf16[8,1,256,3072]{3,2,0,1:T(8,128)(2,1)} fusion(f32[8,256,3072]{2,1,0:T(8,128)} %fusion.48, bf16[8,256,768]{2,1,0:T(8,128)(2,1)S(1)} %all_to_all.20, bf16[1,2,768,3072]{3,2,1,0:T(8,128)(2,1)} %all-gather.6.cloned.1.call-done), kind=kOutput, calls=%fused_computation.6 | convolution fusion | flops 9802088448 | bytes 45613056 | tf_op jit(solution)/shard_map/jkcd,kdf->jkcf/dot_general | solution.py:255
  419.5 14.3 %fusion.75 = bf16[8,256,768]{2,1,0:T(8,128)(2,1)S(1)} fusion(bf16[1,2,768,3072]{3,2,1,0:T(8,128)(2,1)} %all-gather.6.cloned.1.call-done, bf16[8,1,256,3072]{3,2,0,1:T(8,128)(2,1)} %fusion.2), kind=kOutput, calls=%fused_computation.92 | convolution fusion | flops 9665249280 | bytes 20447232 | tf_op jit(solution)/shard_map/jkcf,kdf->jkcd/dot_general | solution.py:259
  433.9 74.3 %all_to_all.21 = bf16[8,256,768]{2,1,0:T(8,128)(2,1)S(1)} all-to-all(bf16[8,256,768]{2,1,0:T(8,128)(2,1)S(1)} %fusion.75), channel_id=1, replica_groups=mesh['dp'=4,'expert'=8] {'expert'}, dimensions={0} | all-to-all | bytes 6291456 | tf_op jit(solution)/shard_map/all_to_all | solution.py:263
  523.9 26.8 %shard_map.299 = bf16[3,1024,768]{2,1,0:T(8,128)(2,1)} custom-call(bf16[3,1024,768]{2,1,0:T(8,128)(2,1)} %convert_bitcast_fusion.q_ref.k_ref.v_ref, bf16[3,1024,768]{2,1,0:T(8,128)(2,1)} %convert_bitcast_fusion.q_ref.k_ref.v_ref, bf16[3,1024,768]{2,1,0:T(8,128)(2,1)} %convert_bitcast_fusion.q_ref.k_ref.v_ref, f32[6,1024,128]{2,1,0:T(8,128)S(1)} %copy-done.1, ...), custom_call_target="tpu_custom_call" | custom-call | tf_op jit(solution)/shard_map/pallas_call | solution.py:123
  561.3 12.0 %copy.130 = f32[4,768,768]{2,0,1:T(4,128)} copy(f32[4,768,768]{1,2,0:T(8,128)} %pad_maximum_fusion) | data formatting | bytes 18874368 | tf_op jit(solution)/shard_map/concatenate | solution.py:302
  573.4 16.2 %fusion.38 = bf16[1,1,768,3072]{3,2,1,0:T(8,128)(2,1)} fusion(bf16[8,256,768]{2,1,0:T(8,128)(2,1)} %all-to-all-done, bf16[8,1,256,3072]{3,2,0,1:T(8,128)(2,1)} %fusion.2), kind=kOutput, calls=%fused_computation.55 | convolution fusion | flops 9666035712 | bytes 20447232 | tf_op jit(solution)/shard_map/jkcd,jkcf->kdf/dot_general | solution.py:271
  589.7 17.5 %fusion.41 = bf16[1,1,768,3072]{3,2,1,0:T(8,128)(2,1)} fusion(bf16[8,256,768]{2,1,0:T(8,128)(2,1)S(1)} %copy-done.17, f32[8,256,3072]{2,1,0:T(8,128)} %fusion.48), kind=kOutput, calls=%fused_computation.56 | convolution fusion | flops 9722658816 | bytes 33030144 | tf_op jit(solution)/shard_map/jkcd,jkcf->kdf/dot_general | solution.py:272
  607.2 8.4 pad_maximum_fusion.1
  624.0 6.9 fusion.62
  634.0 37.8 %all-reduce.1 = f32[10,768]{1,0:T(8,128)S(1)} all-reduce(f32[10,768]{1,0:T(8,128)S(1)} %pad_maximum_fusion.2), channel_id=3, replica_groups=mesh['dp'=4,'expert'=8] {'dp','expert'}, use_global_device_ids=true, to_apply=%region_22.23.clone | all-reduce | flops 7680 | bytes 61440
  678.7 84.1 %all-reduce.4.cloned.1.call-done = f32[4,768,768]{2,0,1:T(4,128)} async-done(((f32[4,768,768]{2,0,1:T(4,128)}), f32[4,768,768]{2,0,1:T(4,128)}) %all-reduce.4.cloned.1.call-update) | async-done | bytes 9437200
  765.8 95.3 %reduce-scatter.3.cloned.1.call-done = bf16[1,2,768,768]{3,2,1,0:T(8,128)(2,1)} async-done(((bf16[1,2,768,3072]{3,2,1,0:T(8,128)(2,1)}), bf16[1,2,768,768]{3,2,1,0:T(8,128)(2,1)}) %reduce-scatter.3.cloned.1.call-update) | async-done | bytes 2359312 | tf_op jit(solution)/shard_map/reduce_scatter | solution.py:275
  869.1 39.5 %psum.7 = f32[]{:T(128)} all-reduce(f32[]{:T(128)S(6)} %add.151), channel_id=1, replica_groups=mesh['dp'=4,'expert'=8] {'dp','expert'}, use_global_device_ids=true, to_apply=%region_26.27 | all-reduce | flops 1 | bytes 8 | tf_op jit(solution)/shard_map/psum | solution.py:315
  913.0 13.2 %multiply_add_fusion = (f32[1,2,768,768]{3,2,1,0:T(8,128)}, f32[1,2,768,768]{3,2,1,0:T(8,128)}, f32[1,2,768,768]{3,2,1,0:T(8,128)}, f32[1,2,768,768]{3,2,1,0:T(8,128)}) fusion(f32[1,2,768,768]{3,2,1,0:T(8,128)} %param.37, f32[1,2,768,768]{3,2,1,0:T(8,128)} %param.28, f32[]{:T(128)S(6)} %min.3, bf16[1,2,768,768]{3,2,1,0:T(8,128)(2,1)S(1)} %copy-done.15, ...), kind=kLoop, calls=%fused_computation.52 | loop fusion | flops 23592960 | bytes 40108036 | tf_op jit(solution)/shard_map/add | solution.py:141
  (143 shorter events, 104.0 us)
Async XLA Ops:
  7.2 71.2 %all-gather.4.cloned.1.call-start = ((), (), s32[]{:S(2)}) async-start(), calls=%async_computation.5 | async-start | bytes 4866048 | tf_op jit(solution)/shard_map/all_gather | solution.py:174
  8.9 167.1 %all-gather.6.cloned.1.call-start = ((), (), s32[]{:S(2)}) async-start(), calls=%async_computation.6 | async-start | bytes 11796480 | tf_op jit(solution)/shard_map/all_gather | solution.py:230
  12.9 46.1 %copy-start.2 = (s32[1,1024]{1,0:T(1,128)S(1)}, s32[1,1024]{1,0:T(1,128)}, u32[]{:S(2)}) copy-start(s32[1,1024]{1,0:T(1,128)} %drow_ref.3) | copy-start | bytes 12292
  12.9 46.3 %copy-start.37 = (s32[1,8]{1,0:T(1,128)S(1)}, s32[1,8]{1,0:T(1,128)}, u32[]{:S(2)}) copy-start(s32[1,8]{1,0:T(1,128)} %param.25) | copy-start | bytes 100
  12.9 47.0 %copy-start.34 = (s32[1,1024]{1,0:T(1,128)S(1)}, s32[1,1024]{1,0:T(1,128)}, u32[]{:S(2)}) copy-start(s32[1,1024]{1,0:T(1,128)} %param.24) | copy-start | bytes 12292
  14.7 89.8 %copy-start.8 = (bf16[1024,768]{0,1:T(8,128)(2,1)}, bf16[1024,768]{0,1:T(8,128)(2,1)S(1)}, u32[]{:S(2)}) copy-start(bf16[1024,768]{0,1:T(8,128)(2,1)S(1)} %copy.121) | copy-start | bytes 4718596
  59.4 26.7 %copy-start.24 = (f32[768]{0:T(1024)}, f32[768]{0:T(1024)S(1)}, u32[]{:S(2)}) copy-start(f32[768]{0:T(1024)S(1)} %get-tuple-element.99) | copy-start | bytes 9220
  60.6 25.5 %copy-start.22 = (f32[1024]{0:T(1024)}, f32[1024]{0:T(1024)S(1)}, u32[]{:S(2)}) copy-start(f32[1024]{0:T(1024)S(1)} %broadcast_multiply_fusion.1) | copy-start | bytes 12292
  114.3 76.5 %all-to-all-start = ((bf16[8,256,768]{2,1,0:T(8,128)(2,1)}), bf16[8,256,768]{2,1,0:T(8,128)(2,1)}, u32[]{:S(2)}, u32[]{:S(2)}) async-start(bf16[8,256,768]{2,1,0:T(8,128)(2,1)} %bitcast.147), calls=%async_computation | async-start | bytes 6291456 | tf_op jit(solution)/shard_map/all_to_all | solution.py:227
  230.2 76.0 %all-to-all-start.1 = ((bf16[8,256,768]{2,1,0:T(8,128)(2,1)}), bf16[8,256,768]{2,1,0:T(8,128)(2,1)}, u32[]{:S(2)}, u32[]{:S(2)}) async-start(bf16[8,256,768]{2,1,0:T(8,128)(2,1)} %fusion.72), calls=%async_computation.1 | async-start | bytes 6291456 | tf_op jit(solution)/shard_map/all_to_all | solution.py:240
  234.7 528.1 %all-reduce.4.cloned.1.call-start = ((), (), s32[]{:S(2)}) async-start(), calls=%async_computation.8 | async-start | bytes 18874368
  236.6 280.4 %copy-start.12 = (bf16[1024,768]{0,1:T(8,128)(2,1)}, bf16[1024,768]{0,1:T(8,128)(2,1)S(1)}, u32[]{:S(2)}) copy-start(bf16[1024,768]{0,1:T(8,128)(2,1)S(1)} %copy.125) | copy-start | bytes 4718596
  390.6 28.9 %copy-start.16 = (bf16[8,256,768]{2,1,0:T(8,128)(2,1)}, bf16[8,256,768]{2,1,0:T(8,128)(2,1)S(1)}, u32[]{:S(2)}) copy-start(bf16[8,256,768]{2,1,0:T(8,128)(2,1)S(1)} %all_to_all.20) | copy-start | bytes 9437188
  523.9 26.9 %copy-start.9 = (bf16[1024,768]{0,1:T(8,128)(2,1)S(1)}, bf16[1024,768]{0,1:T(8,128)(2,1)}, u32[]{:S(2)}) copy-start(bf16[1024,768]{0,1:T(8,128)(2,1)} %copy-done.8) | copy-start | bytes 4718596
  523.9 26.9 %copy-start.23 = (f32[1024]{0:T(1024)S(1)}, f32[1024]{0:T(1024)}, u32[]{:S(2)}) copy-start(f32[1024]{0:T(1024)} %copy-done.22) | copy-start | bytes 12292
  523.9 26.8 %copy-start.25 = (f32[768]{0:T(1024)S(1)}, f32[768]{0:T(1024)}, u32[]{:S(2)}) copy-start(f32[768]{0:T(1024)} %copy-done.24) | copy-start | bytes 9220
  523.9 26.8 %copy-start.27 = (f32[1024]{0:T(1024)S(1)}, f32[1024]{0:T(1024)}, u32[]{:S(2)}) copy-start(f32[1024]{0:T(1024)} %copy-done.26) | copy-start | bytes 12292
  573.4 287.8 %reduce-scatter.3.cloned.1.call-start = ((), (), s32[]{:S(2)}) async-start(), calls=%async_computation.7 | async-start | bytes 11796480 | tf_op jit(solution)/shard_map/reduce_scatter | solution.py:275
  631.0 41.5 %copy-start.13 = (bf16[1024,768]{0,1:T(8,128)(2,1)S(1)}, bf16[1024,768]{0,1:T(8,128)(2,1)}, u32[]{:S(2)}) copy-start(bf16[1024,768]{0,1:T(8,128)(2,1)} %copy-done.12) | copy-start | bytes 4718596
  865.3 44.0 %copy-start.33 = (f32[10,24]{1,0:T(8,128)S(1)}, f32[10,24]{1,0:T(8,128)}, u32[]{:S(2)}) copy-start(f32[10,24]{1,0:T(8,128)} %param.27) | copy-start | bytes 2884
  865.3 45.5 %copy-start.18 = (f32[4,24,768]{2,1,0:T(8,128)S(1)}, f32[4,24,768]{2,1,0:T(8,128)}, u32[]{:S(2)}) copy-start(f32[4,24,768]{2,1,0:T(8,128)} %param.26) | copy-start | bytes 884740
  865.3 45.5 %copy-start.19 = (f32[4,24,768]{2,1,0:T(8,128)S(1)}, f32[4,24,768]{2,1,0:T(8,128)}, u32[]{:S(2)}) copy-start(f32[4,24,768]{2,1,0:T(8,128)} %param.31) | copy-start | bytes 884740
  865.3 45.4 %copy-start.20 = (f32[4,24,768]{2,1,0:T(8,128)S(1)}, f32[4,24,768]{2,1,0:T(8,128)}, u32[]{:S(2)}) copy-start(f32[4,24,768]{2,1,0:T(8,128)} %param.29) | copy-start | bytes 884740
  865.4 47.6 %copy-start.15 = (bf16[1,2,768,768]{3,2,1,0:T(8,128)(2,1)S(1)}, bf16[1,2,768,768]{3,2,1,0:T(8,128)(2,1)}, u32[]{:S(2)}) copy-start(bf16[1,2,768,768]{3,2,1,0:T(8,128)(2,1)} %reduce-scatter.3.cloned.1.call-done) | copy-start | bytes 7077892
  (20 other events, 127.0 us)
Sparse Core Ops, SparseCore 0:
  11.8 66.5 all-gather.3
  80.8 95.1 all-gather.5
  573.5 189.2 all-reduce.3
  766.1 95.0 reduce-scatter.2

commit v2 on v1

--- a/solution.py
+++ b/solution.py
@@ -129,6 +129,175 @@
     )(projected,projected,projected,lse,grad_mixed,dcol,drow)
 
 
+MESH=pl.DeviceIdType.MESH
+TILE=256
+
+def flip(a,b,n):
+    out=0
+    bit=1
+    while bit<n:
+        out=out+bit*((a//bit+b//bit)%2)
+        bit*=2
+    return out
+
+def gelu_pair(x):
+    c=0.7978845608028654
+    sq=x*x
+    t=jnp.tanh(c*(x+0.044715*(x*sq)))
+    half=0.5*(1.0+t)
+    return x*half, half+x*(0.5*(1.0-t*t))*(c+(3*0.044715*c)*sq)
+
+def moe_kernel(n,cap,send_ref,gate_ref,cot_ref,scale_ref,w_ref,
+               back_ref,chosen_ref,ret_ref,gw_ref,
+               recv,gates,cot,w,gw,ret_s,gs_s,ch_s,g_s,racc,sacc,
+               send_sem,recv_sem,gate_send,gate_recv,back_send,back_recv,ch_send,ch_recv,w_sem,loc_sem,ret_sem):
+    per=TILE//cap
+    chunks=w_ref.shape[0]
+    me=lax.axis_index("expert")
+    barrier=pltpu.get_barrier_semaphore()
+    def greet(o,_):
+        pl.semaphore_signal(barrier,inc=1,device_id={"expert":flip(me,o,n)},device_id_type=MESH)
+        return 0
+    lax.fori_loop(1,n,greet,0)
+    pl.semaphore_wait(barrier,n-1)
+
+    def row_copy(peer):
+        return pltpu.make_async_remote_copy(src_ref=send_ref.at[peer],dst_ref=recv.at[me],
+            send_sem=send_sem.at[peer],recv_sem=recv_sem.at[me],device_id={"expert":peer},device_id_type=MESH)
+    def gate_copy(peer):
+        return pltpu.make_async_remote_copy(src_ref=gate_ref.at[peer],dst_ref=gates.at[me],
+            send_sem=gate_send.at[peer],recv_sem=gate_recv.at[me],device_id={"expert":peer},device_id_type=MESH)
+    def row_in(src):
+        return pltpu.make_async_remote_copy(src_ref=send_ref.at[src],dst_ref=recv.at[src],
+            send_sem=send_sem.at[src],recv_sem=recv_sem.at[src],device_id={"expert":src},device_id_type=MESH)
+    def gate_in(src):
+        return pltpu.make_async_remote_copy(src_ref=gate_ref.at[src],dst_ref=gates.at[src],
+            send_sem=gate_send.at[src],recv_sem=gate_recv.at[src],device_id={"expert":src},device_id_type=MESH)
+    def back_copy(src):
+        return pltpu.make_async_remote_copy(src_ref=gs_s.at[src],dst_ref=back_ref.at[me],
+            send_sem=back_send.at[src],recv_sem=back_recv.at[me],device_id={"expert":src},device_id_type=MESH)
+    def ch_copy(src):
+        return pltpu.make_async_remote_copy(src_ref=ch_s.at[src],dst_ref=chosen_ref.at[me],
+            send_sem=ch_send.at[src],recv_sem=ch_recv.at[me],device_id={"expert":src},device_id_type=MESH)
+    def back_in(src):
+        return pltpu.make_async_remote_copy(src_ref=gs_s.at[src],dst_ref=back_ref.at[src],
+            send_sem=back_send.at[src],recv_sem=back_recv.at[src],device_id={"expert":src},device_id_type=MESH)
+    def ch_in(src):
+        return pltpu.make_async_remote_copy(src_ref=ch_s.at[src],dst_ref=chosen_ref.at[src],
+            send_sem=ch_send.at[src],recv_sem=ch_recv.at[src],device_id={"expert":src},device_id_type=MESH)
+
+    def push(i,_):
+        peer=flip(me,n-1-i,n)
+        gate_copy(peer).start()
+        row_copy(peer).start()
+        return 0
+    lax.fori_loop(0,n-1,push,0)
+    own=[pltpu.make_async_copy(send_ref.at[me],recv.at[me],loc_sem.at[0]),
+         pltpu.make_async_copy(gate_ref.at[me],gates.at[me],loc_sem.at[1]),
+         pltpu.make_async_copy(cot_ref,cot,loc_sem.at[2]),
+         pltpu.make_async_copy(w_ref,w,w_sem)]
+    for c in own: c.start()
+    def wipe(c,_):
+        gw[c]=jnp.zeros(gw.shape[1:],jnp.float32)
+        return 0
+    lax.fori_loop(0,chunks,wipe,0)
+    for c in own: c.wait()
+
+    def tile(t,_):
+        block=flip(me//per,t,n//per)
+        for j in range(per):
+            src=block*per+j
+            @pl.when(src!=me)
+            def _():
+                gate_in(src).wait_recv()
+                row_in(src).wait_recv()
+        at=pl.ds(pl.multiple_of(block*per,per),per)
+        rows=pl.ds(pl.multiple_of(block*TILE,TILE),TILE)
+        gate=jnp.transpose(jnp.sum(gates[at],axis=0))[:,0:1]
+        grad_out=cot[rows,:].astype(jnp.float32)*scale_ref[rows,:]
+        g_s[...]=(gate*grad_out).astype(jnp.bfloat16)
+        racc[...]=jnp.zeros_like(racc)
+        sacc[...]=jnp.zeros_like(sacc)
+        def chunk(c,_):
+            x=recv[at].reshape(TILE,recv.shape[2])
+            g=g_s[...]
+            act,slope=gelu_pair(jnp.dot(x,w[c,0],preferred_element_type=jnp.float32))
+            a=act.astype(jnp.bfloat16)
+            ga=jnp.dot(g,w[c,1],preferred_element_type=jnp.float32).astype(jnp.bfloat16)
+            gp=(ga.astype(jnp.float32)*slope).astype(jnp.bfloat16)
+            racc[...]+=lax.dot_general(a,w[c,1],NT,preferred_element_type=jnp.float32)
+            sacc[...]+=lax.dot_general(gp,w[c,0],NT,preferred_element_type=jnp.float32)
+            gw[c,0]+=lax.dot_general(x,gp,TN,preferred_element_type=jnp.float32)
+            gw[c,1]+=lax.dot_general(g,a,TN,preferred_element_type=jnp.float32)
+            return 0
+        lax.fori_loop(0,chunks,chunk,0)
+        ret=racc[...].astype(jnp.bfloat16)
+        grad_out=cot[rows,:].astype(jnp.float32)*scale_ref[rows,:]
+        chosen=jnp.sum(grad_out*ret.astype(jnp.float32),axis=1,keepdims=True)*gate*(1.0-gate)
+        chosen=jnp.transpose(jnp.broadcast_to(chosen,(TILE,128)))[0:8,:]
+        gs_s[at]=sacc[...].astype(jnp.bfloat16).reshape(per,cap,recv.shape[2])
+        ret_s[at]=ret.reshape(per,cap,recv.shape[2])
+        for j in range(per):
+            src=block*per+j
+            ch_s[src]=chosen
+            @pl.when(src!=me)
+            def _():
+                ch_copy(src).start()
+                back_copy(src).start()
+            @pl.when(src==me)
+            def _():
+                pltpu.make_async_copy(ch_s.at[me],chosen_ref.at[me],loc_sem.at[0]).start()
+                pltpu.make_async_copy(gs_s.at[me],back_ref.at[me],loc_sem.at[1]).start()
+        pltpu.make_async_copy(ret_s.at[at],ret_ref.at[at],ret_sem.at[t]).start()
+        return 0
+    lax.fori_loop(0,n//per,tile,0)
+    def pack(c,_):
+        w[c]=gw[c].astype(jnp.bfloat16)
+        return 0
+    lax.fori_loop(0,chunks,pack,0)
+    out=pltpu.make_async_copy(w,gw_ref,w_sem)
+    out.start()
+    pltpu.make_async_copy(ch_s.at[me],chosen_ref.at[me],loc_sem.at[0]).wait()
+    pltpu.make_async_copy(gs_s.at[me],back_ref.at[me],loc_sem.at[1]).wait()
+    def settle(o,_):
+        peer=flip(me,o,n)
+        gate_copy(peer).wait_send()
+        row_copy(peer).wait_send()
+        ch_copy(peer).wait_send()
+        back_copy(peer).wait_send()
+        ch_in(peer).wait_recv()
+        back_in(peer).wait_recv()
+        return 0
+    lax.fori_loop(1,n,settle,0)
+    def stored(t,_):
+        block=flip(me//per,t,n//per)
+        at=pl.ds(pl.multiple_of(block*per,per),per)
+        pltpu.make_async_copy(ret_s.at[at],ret_ref.at[at],ret_sem.at[t]).wait()
+        return 0
+    lax.fori_loop(0,n//per,stored,0)
+    out.wait()
+
+def moe(send_rows,gate_slots,cot,scale,weights,collective_id=1):
+    n,cap,D=send_rows.shape
+    chunks,_,_,FC=weights.shape
+    any_=pl.BlockSpec(memory_space=pl.ANY)
+    bf=jnp.bfloat16; f32=jnp.float32
+    dma=pltpu.SemaphoreType.DMA
+    flops=6*2*n*cap*D*chunks*FC
+    return pl.pallas_call(partial(moe_kernel,n,cap),
+        out_shape=[jax.ShapeDtypeStruct((n,cap,D),bf),jax.ShapeDtypeStruct((n,8,TILE),f32),
+                   jax.ShapeDtypeStruct((n,cap,D),bf),jax.ShapeDtypeStruct(weights.shape,bf)],
+        in_specs=[any_,any_,any_,pl.BlockSpec(memory_space=pltpu.VMEM),any_],
+        out_specs=[any_]*4,
+        scratch_shapes=[pltpu.VMEM((n,cap,D),bf),pltpu.VMEM((n,8,TILE),f32),pltpu.VMEM((n*cap,D),bf),
+            pltpu.VMEM(weights.shape,bf),pltpu.VMEM(weights.shape,f32),pltpu.VMEM((n,cap,D),bf),pltpu.VMEM((n,cap,D),bf),
+            pltpu.VMEM((n,8,TILE),f32),pltpu.VMEM((TILE,D),bf),pltpu.VMEM((TILE,D),f32),pltpu.VMEM((TILE,D),f32)]
+            +[dma((n,))]*8+[dma(()),dma((3,)),dma((n*cap//TILE,))],
+        compiler_params=pltpu.CompilerParams(vmem_limit_bytes=62*2**20,collective_id=collective_id,has_side_effects=True),
+        cost_estimate=pl.CostEstimate(flops=flops,bytes_accessed=40*2**20,transcendentals=0),
+    )(send_rows,gate_slots,cot,scale,weights)
+
+
 def adam_update(weight, gradient, first_moment, second_moment, average, factor, rate):
     clipped = gradient * factor
     first_new = beta_first * first_moment + (1.0 - beta_first) * clipped
@@ -167,21 +336,22 @@
     experts_total = expert_counts.shape[1]
     capacity = 2 * tokens // experts_total
     owners = lax.axis_size("expert")
-    local_experts = experts_total // owners
     groups = lax.axis_size(("dp", "expert"))
     sequences = tokens // LEN
     dense_low, vector_low = (
         lax.all_gather(dense_weights.astype(jnp.bfloat16), ("dp", "expert"), axis=1, tiled=True),
         lax.all_gather(vector_params.astype(jnp.bfloat16), ("dp", "expert"), axis=1, tiled=True),
     )
-    seq_index = lax.axis_index(("dp", "expert")) * sequences + jnp.arange(sequences)
+    me = lax.axis_index("expert")
+    seq_index = lax.axis_index("dp") * owners + jnp.arange(owners)
     bounds = jnp.cumsum(domain_counts)
     domain = jnp.sum((seq_index[:, None] >= bounds[None, :]).astype(jnp.int32), axis=1)
     seq_pick = (domain[:, None] == jnp.arange(NDOM)[None, :]).astype(jnp.float32)
     seq_weight = jnp.sum(seq_pick * domain_weight[None, :], axis=1)
     seq_count = jnp.sum(seq_pick * domain_counts[None, :].astype(jnp.float32), axis=1)
     seq_scale = seq_weight * (sequences * groups) / (NDOM * seq_count)
-    token_scale = jnp.repeat(seq_scale, LEN)
+    slot_scale = jnp.repeat(seq_scale, capacity)[:, None]
+    token_scale = jnp.broadcast_to(seq_scale[me], (tokens,))
     row_counts = expert_counts[0]
     row_order = token_order[0]
     count_ends = jnp.cumsum(row_counts)
@@ -195,8 +365,8 @@
     token_slot = jnp.sum(jnp.where(at_token, sorted_slot[:, None], 0), axis=0)
     token_expert = token_slot // capacity
     expert_pick = (token_expert[:, None] == jnp.arange(experts_total)[None, :]).astype(jnp.float32)
-    slot_pick = token_slot[:, None] == jnp.arange(experts_total * capacity)[None, :]
-    slot_pick = slot_pick.astype(jnp.bfloat16)
+    slot_match = token_slot[:, None] == jnp.arange(experts_total * capacity)[None, :]
+    slot_pick = slot_match.astype(jnp.bfloat16)
 
     def to_slots(rows):
         placed = jnp.dot(slot_pick.T, rows, preferred_element_type=jnp.float32)
@@ -207,6 +377,11 @@
             slot_pick, rows.reshape(-1, model_width), preferred_element_type=jnp.float32
         )
 
+    cot_received = lax.all_to_all(
+        to_slots(cotangent), "expert", split_axis=0, concat_axis=0, tiled=True
+    ).reshape(-1, model_width)
+    own_low = expert_weights[0].astype(jnp.bfloat16)
+    expert_low = lax.all_gather(own_low, "dp", axis=0)
     inputs_float = inputs.astype(jnp.float32)
     normed_one, norm_one_back = jax.vjp(layer_norm, inputs_float, vector_low[0].astype(jnp.float32))
     normed_low = normed_one.astype(jnp.bfloat16)
@@ -224,60 +399,27 @@
     gate_value = jax.nn.sigmoid(jnp.sum(logits * expert_pick, axis=1))
     sent_rows = normed_two.astype(jnp.bfloat16)
     send_rows = to_slots(sent_rows)
-    received = lax.all_to_all(send_rows, "expert", split_axis=0, concat_axis=0, tiled=True)
-    rows_in = received.reshape(owners, local_experts, capacity, model_width)
-    own_low = expert_weights.astype(jnp.bfloat16)
-    expert_low = lax.all_gather(own_low, "dp", axis=3, tiled=True)
-    expert_pre = jnp.einsum(
-        "jkcd,kdf->jkcf", rows_in, expert_low[:, 0], preferred_element_type=jnp.float32
-    )
-    active, gelu_back = jax.vjp(jax.nn.gelu, expert_pre)
-    active_low = active.astype(jnp.bfloat16)
-    produced = jnp.einsum(
-        "jkcf,kdf->jkcd", active_low, expert_low[:, 1], preferred_element_type=jnp.float32
-    )
-    produced_low = produced.astype(jnp.bfloat16)
-    returned = lax.all_to_all(
-        produced_low.reshape(experts_total, capacity, model_width),
-        "expert",
-        split_axis=0,
-        concat_axis=0,
-        tiled=True,
-    )
+    per = TILE // capacity
+    gate_slots = jnp.sum(
+        jnp.where(slot_match, gate_value[:, None], 0.0), axis=0
+    ).reshape(experts_total, 1, 1, capacity)
+    lane_part = (jnp.arange(per) == me % per).astype(jnp.float32)
+    gate_tiles = jnp.broadcast_to(
+        gate_slots * lane_part[None, None, :, None], (experts_total, 8, per, capacity)
+    ).reshape(experts_total, 8, TILE)
+    grad_back, chosen_tiles, produced_low, grad_expert = moe(
+        send_rows, gate_tiles, cot_received, slot_scale, expert_low
+    )
+    expert_grad = lax.psum_scatter(grad_expert, "dp", scatter_dimension=0).astype(jnp.float32)[None]
+    returned = lax.all_to_all(produced_low, "expert", split_axis=0, concat_axis=0, tiled=True)
     returned_rows = from_slots(returned)
     block_output = hidden_state + gate_value[:, None] * returned_rows
     grad_out = cotangent.astype(jnp.float32) * token_scale[:, None]
-    grad_returned = (gate_value[:, None] * grad_out).astype(jnp.bfloat16)
-    grad_chosen = jnp.sum(grad_out * returned_rows, axis=1) * gate_value * (1.0 - gate_value)
-    grad_rows = to_slots(grad_returned)
-    grad_received = lax.all_to_all(grad_rows, "expert", split_axis=0, concat_axis=0, tiled=True)
-    grad_in = grad_received.reshape(owners, local_experts, capacity, model_width)
-    grad_active = jnp.einsum(
-        "jkcd,kdf->jkcf", grad_in, expert_low[:, 1], preferred_element_type=jnp.float32
-    ).astype(jnp.bfloat16)
-    grad_pre = gelu_back(grad_active.astype(jnp.float32))[0].astype(jnp.bfloat16)
-    grad_sent = jnp.einsum(
-        "jkcf,kdf->jkcd", grad_pre, expert_low[:, 0], preferred_element_type=jnp.float32
-    )
-    grad_sent_low = grad_sent.astype(jnp.bfloat16)
-    grad_back = lax.all_to_all(
-        grad_sent_low.reshape(experts_total, capacity, model_width),
-        "expert",
-        split_axis=0,
-        concat_axis=0,
-        tiled=True,
-    )
     grad_sent_rows = from_slots(grad_back)
-    grad_up = jnp.einsum("jkcd,jkcf->kdf", rows_in, grad_pre, preferred_element_type=jnp.float32)
-    grad_down = jnp.einsum(
-        "jkcd,jkcf->kdf", grad_in, active_low, preferred_element_type=jnp.float32
-    )
-    expert_grad = lax.psum_scatter(
-        jnp.stack([grad_up, grad_down], axis=1).astype(jnp.bfloat16),
-        "dp",
-        scatter_dimension=3,
-        tiled=True,
-    ).astype(jnp.float32)
+    chosen_slots = lax.dynamic_slice_in_dim(
+        chosen_tiles[:, 0, :], me % per * capacity, capacity, axis=1
+    )
+    grad_chosen = jnp.sum(jnp.where(slot_match, chosen_slots.reshape(1, -1), 0.0), axis=1)
     chosen_grad = grad_chosen[:, None] * expert_pick
     grad_normed_two = grad_sent_rows + jnp.dot(
         chosen_grad, centroids, precision=lax.Precision.HIGHEST

time: 943 us -> 867 us (0.919)
  Pallas kernels: 45.1 us -> 181 us
  matrix products: 173 us -> 64.2 us
  waiting for transfers between devices: 331 us -> 226 us
  starting transfers between devices: 9.77 us -> 28.7 us
    all_to_all x2 -> x0, blocking collectives: 148 us -> none  [the longest x1 74.3 us: shards(): lax.all_to_all(grad_sent_low.reshape(experts_total, capacity, model_width...]
    pallas_call x0 -> x1, Pallas kernels: none -> 136 us  [moe(): pl.pallas_call(partial(moe_kernel, n, cap), out_shape=[jax.ShapeDtypeStru...]
    unnamed x5 -> x6, waiting for transfers between devices: 84.1 us -> 216 us
    dot_general x6 -> x0, matrix products: 116 us -> none  [the longest x1 28.9 us: shards(): jnp.einsum('jkcd,kdf->jkcf', grad_in, expert_low[:, 1], preferred_element...]
    reduce_scatter x1 -> x0, waiting for transfers between devices: 95.3 us -> none  [shards(): lax.psum_scatter(jnp.stack([grad_up, grad_down], axis=1).astype(jnp.bfloa...]
    all_to_all x2, waiting for transfers between devices: 77.5 us -> 0.01 us  [the longest x1 0.01 us: shards(): lax.all_to_all(to_slots(cotangent), 'expert', split_axis=0, concat_axis=0...]
    all_gather x1, blocking collectives: 44.1 us -> 118 us  [shards(): lax.all_gather(vector_params.astype(jnp.bfloat16), ('dp', 'expert'), axis...]
    unnamed x1, blocking collectives: 37.8 us -> 105 us
  transfers between devices with their start and end apart: 6 -> 6, of which waited for: 6 -> 3; matrix products, arithmetic and copies ran while one was open for 11% -> 9% of each run, Pallas kernels for 2% -> 2%
where the time goes in v2:
time: 867 us; the launch traced here: 859 us
  blocking collectives  263 us (30%)
  waiting for transfers between devices  226 us (26%)
  Pallas kernels  181 us (21%)
  matrix products  64.2 us (7%)
  other arithmetic  48.2 us (6%)
  local copies, waits for them, and re-layouts  29.9 us (3%)
  starting transfers between devices  28.7 us (3%)
  between operations  18.4 us (2%)
    unnamed x6, waiting for transfers between devices  216 us
    pallas_call x1, Pallas kernels, moe(): pl.pallas_call(partial(moe_kernel, n, cap), out_shape=[jax.ShapeDtypeStru...  136 us
    all_gather x1, blocking collectives, shards(): lax.all_gather(vector_params.astype(jnp.bfloat16), ('dp', 'expert'), axis...  118 us
    unnamed x1, blocking collectives  105 us
    psum x1, blocking collectives, shards(): grad_norm = jnp.sqrt(lax.psum(squares, ('dp', 'expert')))  39.3 us
    pallas_call x1, Pallas kernels, attend_backward(): pl.pallas_call(partial(bwd_kernel, QB), grid=(D // 128,), in_specs=[sp(0)...  26.6 us
    all_to_all x1, starting transfers between devices, shards(): lax.all_to_all(produced_low, 'expert', split_axis=0, concat_axis=0, tiled...  22.3 us
    pallas_call x1, Pallas kernels, attend_forward(): pl.pallas_call(partial(fwd_kernel, QB), grid=(D // 128,), in_specs=[sp(0)...  18.4 us
  transfers between devices with their start and end apart: 6, of which 3 were waited for; matrix products, arithmetic and copies ran while one was open for 9% of the time, Pallas kernels for 2%

profile of v2, /device:TPU:0, one launch (start us, length us, event | category | flops | bytes accessed | tf_op | source)
XLA Modules:
  0.0 859.1 jit_solution(11356988672346006669)
XLA Ops:
  9.0 4.1 convert_element_type.76
  14.2 5.9 fusion.23
  20.1 6.3 all-to-all-start
  30.8 118.4 %all-gather = bf16[32,24,10]{1,2,0:T(8,128)(2,1)S(1)} all-gather(bf16[1,24,10]{1,2,0:T(8,128)(2,1)S(1)} %convert_bitcast_fusion.1), channel_id=1, replica_groups=mesh['dp'=4,'expert'=8] {'dp','expert'}, dimensions={0}, use_global_device_ids=true | all-gather | bytes 15840 | tf_op jit(solution)/shard_map/all_gather | solution.py:343
  156.2 9.3 %convert_bitcast_fusion.q_ref.k_ref.v_ref = bf16[3,1024,768]{2,1,0:T(8,128)(2,1)} fusion(bf16[4,768,768]{2,1,0:T(8,128)(2,1)} %all-gather.4.cloned.1.call-done, bf16[1024,768]{0,1:T(8,128)(2,1)} %copy.120, f32[768]{0:T(1024)S(1)} %get-tuple-element.107, f32[1024]{0:T(1024)S(1)} %fusion.70, f32[1024]{0:T(1024)S(1)} %broadcast_multiply_fusion.1), kind=kOutput, calls=%fused_computation.26 | convolution fusion | flops 3630170112 | bytes 9841664 | tf_op jit(solution)/shard_map/td,cde->cte/dot_general | solution.py:388
  165.4 18.4 %shard_map.298 = (bf16[1024,768]{1,0:T(8,128)(2,1)S(1)}, f32[6,1024,128]{2,1,0:T(8,128)S(1)}) custom-call(bf16[3,1024,768]{2,1,0:T(8,128)(2,1)} %convert_bitcast_fusion.q_ref.k_ref.v_ref, bf16[3,1024,768]{2,1,0:T(8,128)(2,1)} %convert_bitcast_fusion.q_ref.k_ref.v_ref, bf16[3,1024,768]{2,1,0:T(8,128)(2,1)} %convert_bitcast_fusion.q_ref.k_ref.v_ref, ...), custom_call_target="tpu_custom_call" | custom-call | tf_op jit(solution)/shard_map/pallas_call | solution.py:73
  190.7 7.4 fusion.20
  198.2 9.7 %all-gather.6.cloned.1.call-done.w_ref = bf16[4,2,768,768]{3,2,1,0:T(8,128)(2,1)} async-done(((bf16[1,2,768,768]{3,2,1,0:T(8,128)(2,1)}), bf16[4,2,768,768]{3,2,1,0:T(8,128)(2,1)}) %all-gather.6.cloned.1.call-update) | async-done | bytes 9437200 | tf_op jit(solution)/shard_map/all_gather | solution.py:384
  208.5 136.5 %shard_map.299 = (bf16[8,256,768]{2,1,0:T(8,128)(2,1)}, f32[8,8,256]{2,1,0:T(8,128)}, bf16[8,256,768]{2,1,0:T(8,128)(2,1)}, bf16[4,2,768,768]{3,2,1,0:T(8,128)(2,1)}) custom-call(bf16[8,256,768]{2,1,0:T(8,128)(2,1)} %bitcast.82, f32[8,8,256]{2,1,0:T(8,128)} %reshape.212.gate_ref, bf16[2048,768]{1,0:T(8,128)(2,1)} %bitcast.14.cot_ref, f32[2048,1]{1,0:T(8,128)} %bitcast.72, ...), custom_call_target="tpu_custom_call" | custom-call | flops 57982058496 | bytes 41943040 | tf_op jit(solution)/shard_map/pallas_call | solution.py:287
  347.0 5.9 fusion
  363.0 26.6 %shard_map.300 = bf16[3,1024,768]{2,1,0:T(8,128)(2,1)} custom-call(bf16[3,1024,768]{2,1,0:T(8,128)(2,1)} %convert_bitcast_fusion.q_ref.k_ref.v_ref, bf16[3,1024,768]{2,1,0:T(8,128)(2,1)} %convert_bitcast_fusion.q_ref.k_ref.v_ref, bf16[3,1024,768]{2,1,0:T(8,128)(2,1)} %convert_bitcast_fusion.q_ref.k_ref.v_ref, f32[6,1024,128]{2,1,0:T(8,128)S(1)} %copy-done.1, ...), custom_call_target="tpu_custom_call" | custom-call | tf_op jit(solution)/shard_map/pallas_call | solution.py:123
  389.6 6.1 convolution_bitcast_fusion
  395.7 4.6 pad_maximum_fusion
  400.3 12.1 %copy.131 = f32[4,768,768]{2,0,1:T(4,128)} copy(f32[4,768,768]{1,2,0:T(8,128)} %pad_maximum_fusion) | data formatting | bytes 18874368 | tf_op jit(solution)/shard_map/concatenate | solution.py:444
  413.0 22.3 %all-to-all-start.1 = ((bf16[8,256,768]{2,1,0:T(8,128)(2,1)}), bf16[8,256,768]{2,1,0:T(8,128)(2,1)}, u32[]{:S(2)}, u32[]{:S(2)}) async-start(bf16[8,256,768]{2,1,0:T(8,128)(2,1)} %get-tuple-element.22), calls=%async_computation.1 | async-start | bytes 6291456 | tf_op jit(solution)/shard_map/all_to_all | solution.py:414
  435.3 7.5 fusion.27
  445.2 3.9 add_add_fusion.2
  449.1 3.7 copy.134
  455.6 104.9 %all-reduce.1 = f32[10,768]{1,0:T(8,128)S(1)} all-reduce(f32[10,768]{1,0:T(8,128)S(1)} %pad_maximum_fusion.1), channel_id=3, replica_groups=mesh['dp'=4,'expert'=8] {'dp','expert'}, use_global_device_ids=true, to_apply=%region_23.24.clone | all-reduce | flops 7680 | bytes 61440
  561.2 127.4 %all-reduce.5.cloned.1.call-done = f32[4,768,768]{2,0,1:T(4,128)} async-done(((f32[4,768,768]{2,0,1:T(4,128)}), f32[4,768,768]{2,0,1:T(4,128)}) %all-reduce.5.cloned.1.call-update) | async-done | bytes 9437200
  691.6 7.5 multiply_add_fusion.1
  699.1 87.9 %reduce-scatter.5.cloned.1.call-done = bf16[1,2,768,768]{3,2,1,0:T(8,128)(2,1)} async-done(((bf16[4,2,768,768]{3,2,1,0:T(8,128)(2,1)}), bf16[1,2,768,768]{3,2,1,0:T(8,128)(2,1)}) %reduce-scatter.5.cloned.1.call-update) | async-done | bytes 2359312
  794.9 39.3 %psum.7 = f32[]{:T(128)} all-reduce(f32[]{:T(128)S(6)} %add.155), channel_id=1, replica_groups=mesh['dp'=4,'expert'=8] {'dp','expert'}, use_global_device_ids=true, to_apply=%region_27.28 | all-reduce | flops 1 | bytes 8 | tf_op jit(solution)/shard_map/psum | solution.py:457
  837.9 13.3 %multiply_add_fusion = (f32[1,2,768,768]{3,2,1,0:T(8,128)}, f32[1,2,768,768]{3,2,1,0:T(8,128)}, f32[1,2,768,768]{3,2,1,0:T(8,128)}, f32[1,2,768,768]{3,2,1,0:T(8,128)}) fusion(f32[1,2,768,768]{3,2,1,0:T(8,128)} %param.37, f32[1,2,768,768]{3,2,1,0:T(8,128)} %param.28, f32[]{:T(128)S(6)} %min.3, bf16[1,2,768,768]{3,2,1,0:T(8,128)(2,1)S(1)} %copy-done.15, ...), kind=kLoop, calls=%fused_computation.24 | loop fusion | flops 23592960 | bytes 40108036 | tf_op jit(solution)/shard_map/add | solution.py:310
  (127 shorter events, 51.8 us)
Async XLA Ops:
  7.2 149.0 %all-gather.4.cloned.1.call-start = ((), (), s32[]{:S(2)}) async-start(), calls=%async_computation.3 | async-start | bytes 4866048 | tf_op jit(solution)/shard_map/all_gather | solution.py:342
  8.9 4.2 copy-start.26
  8.9 4.6 copy-start.24
  8.9 5.2 copy-start.16
  8.9 198.9 %all-gather.6.cloned.1.call-start = ((), (), s32[]{:S(2)}) async-start(), calls=%async_computation.4 | async-start | bytes 11796480 | tf_op jit(solution)/shard_map/all_gather | solution.py:384
  20.1 178.1 %all-to-all-start = ((bf16[8,256,768]{2,1,0:T(8,128)(2,1)}), bf16[8,256,768]{2,1,0:T(8,128)(2,1)}, u32[]{:S(2)}, u32[]{:S(2)}) async-start(bf16[8,256,768]{2,1,0:T(8,128)(2,1)} %bitcast.13), calls=%async_computation | async-start | bytes 6291456 | tf_op jit(solution)/shard_map/all_to_all | solution.py:380
  26.4 662.1 %all-reduce.5.cloned.1.call-start = ((), (), s32[]{:S(2)}) async-start(), calls=%async_computation.5 | async-start | bytes 18874368
  26.5 4.3 copy-start.19
  26.5 122.9 %copy-start.2 = (s32[1,1024]{1,0:T(1,128)S(1)}, s32[1,1024]{1,0:T(1,128)}, u32[]{:S(2)}) copy-start(s32[1,1024]{1,0:T(1,128)} %drow_ref.3) | copy-start | bytes 12292
  26.5 123.1 %copy-start.27 = (s32[8]{0:T(128)S(1)}, s32[8]{0:T(128)}, u32[]{:S(2)}) copy-start(s32[8]{0:T(128)} %param.22) | copy-start | bytes 100
  26.5 123.5 %copy-start.25 = (f32[8]{0:T(128)S(1)}, f32[8]{0:T(128)}, u32[]{:S(2)}) copy-start(f32[8]{0:T(128)} %param.23) | copy-start | bytes 100
  165.4 18.4 %copy-start.8 = (bf16[1024,768]{0,1:T(8,128)(2,1)S(1)}, bf16[1024,768]{0,1:T(8,128)(2,1)}, u32[]{:S(2)}) copy-start(bf16[1024,768]{0,1:T(8,128)(2,1)} %copy.120) | copy-start | bytes 4718596
  347.0 5.9 copy-start.6
  363.0 26.6 %copy-start.9 = (bf16[1024,768]{0,1:T(8,128)(2,1)S(1)}, bf16[1024,768]{0,1:T(8,128)(2,1)}, u32[]{:S(2)}) copy-start(bf16[1024,768]{0,1:T(8,128)(2,1)} %copy.120) | copy-start | bytes 4718596
  412.4 374.6 %reduce-scatter.5.cloned.1.call-start = ((), (), s32[]{:S(2)}) async-start(), calls=%async_computation.6 | async-start | bytes 11796480
  413.0 22.3 %copy-start.10 = (bf16[1024,768]{0,1:T(8,128)(2,1)S(1)}, bf16[1024,768]{0,1:T(8,128)(2,1)}, u32[]{:S(2)}) copy-start(bf16[1024,768]{0,1:T(8,128)(2,1)} %copy.120) | copy-start | bytes 4718596
  413.0 278.6 %all-to-all-start.1 = ((bf16[8,256,768]{2,1,0:T(8,128)(2,1)}), bf16[8,256,768]{2,1,0:T(8,128)(2,1)}, u32[]{:S(2)}, u32[]{:S(2)}) async-start(bf16[8,256,768]{2,1,0:T(8,128)(2,1)} %get-tuple-element.22), calls=%async_computation.1 | async-start | bytes 6291456 | tf_op jit(solution)/shard_map/all_to_all | solution.py:414
  791.1 43.8 %copy-start.20 = (f32[10,24]{1,0:T(8,128)S(1)}, f32[10,24]{1,0:T(8,128)}, u32[]{:S(2)}) copy-start(f32[10,24]{1,0:T(8,128)} %param.27) | copy-start | bytes 2884
  791.1 43.8 %copy-start.21 = (f32[10,24]{1,0:T(8,128)S(1)}, f32[10,24]{1,0:T(8,128)}, u32[]{:S(2)}) copy-start(f32[10,24]{1,0:T(8,128)} %param.34) | copy-start | bytes 2884
  791.1 43.8 %copy-start.22 = (f32[10,24]{1,0:T(8,128)S(1)}, f32[10,24]{1,0:T(8,128)}, u32[]{:S(2)}) copy-start(f32[10,24]{1,0:T(8,128)} %param.32) | copy-start | bytes 2884
  791.1 43.8 %copy-start.23 = (f32[10,24]{1,0:T(8,128)S(1)}, f32[10,24]{1,0:T(8,128)}, u32[]{:S(2)}) copy-start(f32[10,24]{1,0:T(8,128)} %param.33) | copy-start | bytes 2884
  791.2 44.5 %copy-start.17 = (f32[4,24,768]{2,1,0:T(8,128)S(1)}, f32[4,24,768]{2,1,0:T(8,128)}, u32[]{:S(2)}) copy-start(f32[4,24,768]{2,1,0:T(8,128)} %param.26) | copy-start | bytes 884740
  791.2 44.5 %copy-start.18 = (f32[4,24,768]{2,1,0:T(8,128)S(1)}, f32[4,24,768]{2,1,0:T(8,128)}, u32[]{:S(2)}) copy-start(f32[4,24,768]{2,1,0:T(8,128)} %param.31) | copy-start | bytes 884740
  791.2 46.7 %copy-start.15 = (bf16[1,2,768,768]{3,2,1,0:T(8,128)(2,1)S(1)}, bf16[1,2,768,768]{3,2,1,0:T(8,128)(2,1)}, u32[]{:S(2)}) copy-start(bf16[1,2,768,768]{3,2,1,0:T(8,128)(2,1)} %reduce-scatter.5.cloned.1.call-done) | copy-start | bytes 7077892
  (10 other events, 25.6 us)
Sparse Core Ops, SparseCore 0:
  11.8 99.3 all-gather.3
  113.5 94.2 all-gather.5
  412.5 275.9 all-reduce.4
  691.8 95.0 reduce-scatter.4

commit v3 on v2

--- a/solution.py
+++ b/solution.py
@@ -298,6 +298,222 @@
     )(send_rows,gate_slots,cot,scale,weights)
 
 
+def near(dps,pairs):
+    d=lax.axis_index("dp"); me=lax.axis_index("expert")
+    core=me%2; pair=me//2
+    partner={"expert":me+1-2*core}
+    over=[((d+k)%dps,{"dp":(d+k)%dps}) for k in range(1,dps)]
+    along=[((pair+k)%pairs,{"expert":2*((pair+k)%pairs)+core}) for k in range(1,pairs)]
+    return d,pair,core,partner,over,along
+
+def greet_all(devices):
+    barrier=pltpu.get_barrier_semaphore()
+    for dev in devices:
+        pl.semaphore_signal(barrier,inc=1,device_id=dev,device_id_type=MESH)
+    pl.semaphore_wait(barrier,len(devices))
+
+def remote(src,dst,send,recv,dev):
+    return pltpu.make_async_remote_copy(src_ref=src,dst_ref=dst,send_sem=send,recv_sem=recv,device_id=dev,device_id_type=MESH)
+
+def gather_kernel(dps,pairs,w_ref,v_ref,out_ref,vout_ref,both,blk,vboth,vblk,
+                  s1,r1,loc,zs,zr,vzs,vzr,ds_,dr,vds,vdr,ps,pr):
+    r=w_ref.shape[1]; R=2*r
+    d,pair,core,partner,over,along=near(dps,pairs)
+    greet_all([partner]+[x[1] for x in over]+[x[1] for x in along])
+    mine=pl.ds(pl.multiple_of(core*r,8),r)
+    lanes=pl.ds(pl.multiple_of(core*128,128),128)
+    half=pl.ds(core*2,2); rest=pl.ds(2-core*2,2)
+    def rows(dd,q): return pl.ds(pl.multiple_of((dd*pairs+q)*R,16),R)
+    c1=[remote(w_ref,both.at[:,mine,:],s1.at[0],r1.at[0],partner),
+        remote(v_ref,vboth.at[:,lanes],s1.at[1],r1.at[1],partner)]
+    for c in c1: c.start()
+    both[:,mine,:]=w_ref[...]
+    vboth[:,lanes]=v_ref[...]
+    for c in c1: c.wait()
+    blk[...]=both[...].astype(jnp.bfloat16)
+    vblk[...]=vboth[...].astype(jnp.bfloat16)
+    own=[pltpu.make_async_copy(blk,out_ref.at[:,rows(d,pair),:],loc.at[0]),
+         pltpu.make_async_copy(vblk,vout_ref.at[d,pair],loc.at[1])]
+    for c in own: c.start()
+    zc=[]; dc=[]; pc=[]; vc=[]
+    for q,dev in along:
+        zc.append(remote(blk.at[half],out_ref.at[half,rows(d,pair),:],zs.at[q],zr.at[pair],dev)); zc[-1].start()
+        vc.append(remote(vblk,vout_ref.at[d,pair],vzs.at[q],vzr.at[pair],dev)); vc[-1].start()
+    for dd,dev in over:
+        c=remote(blk.at[half],out_ref.at[half,rows(d,pair),:],ds_.at[dd,pair],dr.at[d,pair],dev); c.start(); dc.append(c)
+    for q,dev in along:
+        here=out_ref.at[half,rows(d,q),:]
+        remote(here,here,zs.at[q],zr.at[q],dev).wait_recv()
+        for dd,dev2 in over:
+            c=remote(here,here,ds_.at[dd,q],dr.at[d,q],dev2); c.start(); dc.append(c)
+        c=remote(here,here,ps.at[d,q],pr.at[d,q],partner); c.start(); pc.append(c)
+    for q,dev in along:
+        remote(vblk,vout_ref.at[d,q],vzs.at[q],vzr.at[q],dev).wait_recv()
+    own[1].wait()
+    for dd,dev in over:
+        c=remote(vout_ref.at[d],vout_ref.at[d],vds.at[dd],vdr.at[d],dev); c.start(); vc.append(c)
+    for q in [pair]+[x[0] for x in along]:
+        for dd,dev in over:
+            here=out_ref.at[half,rows(dd,q),:]
+            remote(here,here,ds_.at[dd,q],dr.at[dd,q],dev).wait_recv()
+            c=remote(here,here,ps.at[dd,q],pr.at[dd,q],partner); c.start(); pc.append(c)
+    for q in [pair]+[x[0] for x in along]:
+        for dd in [d]+[x[0] for x in over]:
+            if q is pair and dd is d: continue
+            there=out_ref.at[rest,rows(dd,q),:]
+            remote(there,there,ps.at[dd,q],pr.at[dd,q],partner).wait_recv()
+    for dd,dev in over:
+        remote(vout_ref.at[dd],vout_ref.at[dd],vds.at[dd],vdr.at[dd],dev).wait_recv()
+    for c in zc+dc+pc+vc: c.wait_send()
+    own[0].wait()
+
+def gather_dense(weights,vectors,dps,n,collective_id=2):
+    pairs=n//2
+    m,r,D=weights.shape
+    V=jnp.zeros((16,128),jnp.float32).at[:vectors.shape[0],:r].set(vectors)
+    dma=pltpu.SemaphoreType.DMA
+    f32=jnp.float32; bf=jnp.bfloat16
+    out,vout=pl.pallas_call(partial(gather_kernel,dps,pairs),
+        out_shape=[jax.ShapeDtypeStruct((m,r*n*dps,D),bf),jax.ShapeDtypeStruct((dps,pairs,16,256),bf)],
+        in_specs=[pl.BlockSpec(memory_space=pltpu.VMEM)]*2,
+        out_specs=[pl.BlockSpec(memory_space=pl.ANY)]*2,
+        scratch_shapes=[pltpu.VMEM((m,2*r,D),f32),pltpu.VMEM((m,2*r,D),bf),pltpu.VMEM((16,256),f32),pltpu.VMEM((16,256),bf),
+            dma((2,)),dma((2,)),dma((2,)),dma((pairs,)),dma((pairs,)),dma((pairs,)),dma((pairs,)),
+            dma((dps,pairs)),dma((dps,pairs)),dma((dps,)),dma((dps,)),dma((dps,pairs)),dma((dps,pairs))],
+        compiler_params=pltpu.CompilerParams(vmem_limit_bytes=16*2**20,collective_id=collective_id,has_side_effects=True),
+        cost_estimate=pl.CostEstimate(flops=0,bytes_accessed=100*2**20,transcendentals=0),
+    )(weights,V)
+    k=vectors.shape[0]
+    vec=vout[:,:,:k].reshape(dps,pairs,k,2,128)[...,:r]
+    vec=jnp.transpose(vec,(2,0,1,3,4)).reshape(k,r*n*dps)
+    return out,vec
+
+def scatter_kernel(dps,pairs,x_ref,mixed_ref,ga_ref,gp_ref,v_ref,out_ref,vout_ref,
+                   left,right,got,own,total,in2,t32,tb,in3,u,in4,v1,v2,v3,
+                   ls,s1,r1,s2,r2,s3,r3,s4,r4,vs1,vr1,vs2,vr2,vs3,vr3):
+    d,pair,core,partner,over,along=near(dps,pairs)
+    rows=out_ref.shape[1]; R=2*rows; D=out_ref.shape[2]
+    loads=[pltpu.make_async_copy(x_ref,left.at[0],ls.at[0]),pltpu.make_async_copy(mixed_ref,left.at[1],ls.at[1]),
+           pltpu.make_async_copy(gp_ref,right.at[pl.ds(0,3)],ls.at[2]),pltpu.make_async_copy(ga_ref,right.at[3],ls.at[3])]
+    for c in loads: c.start()
+    greet_all([partner]+[x[1] for x in over]+[x[1] for x in along])
+    vc=[remote(v_ref,v1,vs1,vr1,partner)]
+    vc[0].start()
+    for c in loads: c.wait()
+    def product(m):
+        return lax.dot_general(left[m//3],right[m],TN,preferred_element_type=jnp.float32)
+    sends=[]
+    for i in range(2):
+        total[i]=product(2-2*core+i).astype(jnp.bfloat16)
+        c=remote(total.at[i],got.at[i],s1.at[i],r1.at[i],partner); c.start(); sends.append(c)
+    for i in range(2):
+        own[i]=product(2*core+i)
+    remote(v_ref,v1,vs1,vr1,partner).wait_recv()
+    v2[d]=v_ref[...]+v1[...]
+    for dd,dev in over:
+        c=remote(v2.at[d],v2.at[d],vs2.at[dd],vr2.at[d],dev); c.start(); vc.append(c)
+    for i in range(2):
+        sends[i].wait_send()
+        remote(total.at[i],got.at[i],s1.at[i],r1.at[i],partner).wait_recv()
+        total[i]=(own[i]+got[i].astype(jnp.float32)).astype(jnp.bfloat16)
+    c2=[]
+    order=along+[(pair,None)]
+    def piece(dd,q): return pl.ds(pl.multiple_of((dd*pairs+q)*R,16),R)
+    for q,_ in order:
+        for dd,dev in over:
+            c=remote(total.at[:,piece(dd,q),:],in2.at[d,q],s2.at[dd,q],r2.at[d,q],dev); c.start(); c2.append(c)
+    for dd,dev in over:
+        remote(v2.at[dd],v2.at[dd],vs2.at[dd],vr2.at[dd],dev).wait_recv()
+    v3[pair]=sum(v2[k] for k in range(dps))
+    for q,dev in along:
+        c=remote(v3.at[pair],v3.at[pair],vs3.at[q],vr3.at[pair],dev); c.start(); vc.append(c)
+    c3=[]
+    for q,zdev in order:
+        acc=total[:,piece(d,q),:].astype(jnp.float32)
+        for dd,dev in over:
+            remote(in2.at[dd,q],in2.at[dd,q],s2.at[dd,q],r2.at[dd,q],dev).wait_recv()
+            acc=acc+in2[dd,q].astype(jnp.float32)
+        if zdev is None:
+            u[...]=acc
+        else:
+            tb[q]=acc.astype(jnp.bfloat16)
+            c=remote(tb.at[q],in3.at[pair],s3.at[q],r3.at[pair],zdev); c.start(); c3.append(c)
+    acc=u[...]
+    for q,dev in along:
+        remote(in3.at[q],in3.at[q],s3.at[q],r3.at[q],dev).wait_recv()
+        acc=acc+in3[q].astype(jnp.float32)
+    u[...]=acc
+    theirs=pl.ds(pl.multiple_of((1-core)*rows,8),rows); mine=pl.ds(pl.multiple_of(core*rows,8),rows)
+    c4=remote(u.at[:,theirs,:],in4,s4,r4,partner); c4.start()
+    for q,dev in along:
+        remote(v3.at[q],v3.at[q],vs3.at[q],vr3.at[q],dev).wait_recv()
+    vout_ref[...]=sum(v3[k] for k in range(pairs))
+    out_ref[pl.ds(2*core,2)]=u[:,mine,:]
+    c4.wait_recv()
+    out_ref[pl.ds(2-2*core,2)]=in4[...]
+    for c in c2+c3+vc+[c4]: c.wait_send()
+
+def scatter_dense(x,mixed,ga,gp,vec,dps,n,collective_id=3):
+    pairs=n//2
+    T,D=x.shape; rows=D//(dps*n); R=2*rows
+    dma=pltpu.SemaphoreType.DMA
+    f32=jnp.float32; bf=jnp.bfloat16
+    any_=pl.BlockSpec(memory_space=pl.ANY); vm=pl.BlockSpec(memory_space=pltpu.VMEM)
+    k=vec.shape[0]
+    V=jnp.zeros((16,D),f32).at[:k].set(vec)
+    out,vout=pl.pallas_call(partial(scatter_kernel,dps,pairs),
+        out_shape=[jax.ShapeDtypeStruct((4,rows,D),f32),jax.ShapeDtypeStruct((16,D),f32)],
+        in_specs=[any_]*4+[vm],out_specs=[vm]*2,
+        scratch_shapes=[pltpu.VMEM((2,T,D),bf),pltpu.VMEM((4,T,D),bf),pltpu.VMEM((2,D,D),bf),pltpu.VMEM((2,D,D),f32),pltpu.VMEM((2,D,D),bf),
+            pltpu.VMEM((dps,pairs,2,R,D),bf),pltpu.VMEM((8,128),f32),pltpu.VMEM((pairs,2,R,D),bf),pltpu.VMEM((pairs,2,R,D),bf),
+            pltpu.VMEM((2,R,D),f32),pltpu.VMEM((2,rows,D),f32),pltpu.VMEM((16,D),f32),pltpu.VMEM((dps,16,D),f32),pltpu.VMEM((pairs,16,D),f32),
+            dma((4,)),dma((2,)),dma((2,)),dma((dps,pairs)),dma((dps,pairs)),dma((pairs,)),dma((pairs,)),dma(()),dma(()),
+            dma(()),dma(()),dma((dps,)),dma((dps,)),dma((pairs,)),dma((pairs,))],
+        compiler_params=pltpu.CompilerParams(vmem_limit_bytes=48*2**20,collective_id=collective_id,has_side_effects=True),
+        cost_estimate=pl.CostEstimate(flops=8*T*D*D,bytes_accessed=100*2**20,transcendentals=0),
+    )(x,mixed,ga,gp,V)
+    dev=lax.axis_index("dp")*n+lax.axis_index("expert")
+    return out,lax.dynamic_slice_in_dim(vout[:k],dev*rows,rows,axis=1)
+
+def norm_kernel(dps,pairs,d_ref,v_ref,e_ref,out_ref,a,b,c,s1,r1,s2,r2,s3,r3):
+    d,pair,core,partner,over,along=near(dps,pairs)
+    greet_all([partner]+[x[1] for x in over]+[x[1] for x in along])
+    def squares(ref):
+        x=ref[...].astype(jnp.float32)
+        return jnp.sum(x*x)
+    part=squares(d_ref)+squares(v_ref)
+    for i in range(e_ref.shape[0]):
+        part=part+squares(e_ref.at[i])
+    a[core]=jnp.full((8,128),part,jnp.float32)
+    cs=[remote(a.at[core],a.at[core],s1,r1.at[core],partner)]
+    cs[0].start()
+    remote(a.at[1-core],a.at[1-core],s1,r1.at[1-core],partner).wait_recv()
+    b[d]=a[0]+a[1]
+    for dd,dev in over:
+        x=remote(b.at[d],b.at[d],s2.at[dd],r2.at[d],dev); x.start(); cs.append(x)
+    for dd,dev in over:
+        remote(b.at[dd],b.at[dd],s2.at[dd],r2.at[dd],dev).wait_recv()
+    c[pair]=sum(b[k] for k in range(dps))
+    for q,dev in along:
+        x=remote(c.at[pair],c.at[pair],s3.at[q],r3.at[pair],dev); x.start(); cs.append(x)
+    for q,dev in along:
+        remote(c.at[q],c.at[q],s3.at[q],r3.at[q],dev).wait_recv()
+    out_ref[...]=sum(c[k] for k in range(pairs))
+    for x in cs: x.wait_send()
+
+def norm_squares(dense,vec,expert,dps,n,collective_id=4):
+    pairs=n//2
+    dma=pltpu.SemaphoreType.DMA; f32=jnp.float32
+    vm=pl.BlockSpec(memory_space=pltpu.VMEM)
+    out=pl.pallas_call(partial(norm_kernel,dps,pairs),
+        out_shape=jax.ShapeDtypeStruct((8,128),f32),in_specs=[vm]*3,out_specs=vm,
+        scratch_shapes=[pltpu.VMEM((2,8,128),f32),pltpu.VMEM((dps,8,128),f32),pltpu.VMEM((pairs,8,128),f32),
+            dma(()),dma((2,)),dma((dps,)),dma((dps,)),dma((pairs,)),dma((pairs,))],
+        compiler_params=pltpu.CompilerParams(vmem_limit_bytes=16*2**20,collective_id=collective_id,has_side_effects=True),
+    )(dense,vec,expert)
+    return out[0,0]
+
+
 def adam_update(weight, gradient, first_moment, second_moment, average, factor, rate):
     clipped = gradient * factor
     first_new = beta_first * first_moment + (1.0 - beta_first) * clipped
@@ -338,10 +554,15 @@
     owners = lax.axis_size("expert")
     groups = lax.axis_size(("dp", "expert"))
     sequences = tokens // LEN
-    dense_low, vector_low = (
-        lax.all_gather(dense_weights.astype(jnp.bfloat16), ("dp", "expert"), axis=1, tiled=True),
-        lax.all_gather(vector_params.astype(jnp.bfloat16), ("dp", "expert"), axis=1, tiled=True),
-    )
+    splits = lax.axis_size("dp")
+    own_rows = dense_weights.shape[1]
+    if own_rows % 8 == 0:
+        dense_low, vector_low = gather_dense(dense_weights, vector_params, splits, owners)
+    else:
+        dense_low, vector_low = (
+            lax.all_gather(dense_weights.astype(jnp.bfloat16), ("dp", "expert"), axis=1, tiled=True),
+            lax.all_gather(vector_params.astype(jnp.bfloat16), ("dp", "expert"), axis=1, tiled=True),
+        )
     me = lax.axis_index("expert")
     seq_index = lax.axis_index("dp") * owners + jnp.arange(owners)
     bounds = jnp.cumsum(domain_counts)
@@ -410,7 +631,8 @@
     grad_back, chosen_tiles, produced_low, grad_expert = moe(
         send_rows, gate_tiles, cot_received, slot_scale, expert_low
     )
-    expert_grad = lax.psum_scatter(grad_expert, "dp", scatter_dimension=0).astype(jnp.float32)[None]
+    expert_low_grad = lax.psum_scatter(grad_expert, "dp", scatter_dimension=0)
+    expert_grad = expert_low_grad.astype(jnp.float32)[None]
     returned = lax.all_to_all(produced_low, "expert", split_axis=0, concat_axis=0, tiled=True)
     returned_rows = from_slots(returned)
     block_output = hidden_state + gate_value[:, None] * returned_rows
@@ -428,33 +650,38 @@
     grad_hidden_norm, grad_gain_two = norm_two_back(grad_normed_two)
     grad_hidden = grad_out + grad_hidden_norm
     grad_attn = grad_hidden.astype(jnp.bfloat16)
-    grad_out_proj = jnp.dot(mixed_low.T, grad_attn, preferred_element_type=jnp.float32)
     grad_mixed = jnp.dot(grad_attn, dense_low[3].T, preferred_element_type=jnp.float32).astype(
         jnp.bfloat16
     )
     grad_proj = attend_backward(projected, documents, totals, grad_mixed)
-    grad_in_proj = jnp.einsum(
-        "td,cte->cde", normed_low, grad_proj, preferred_element_type=jnp.float32
-    )
     grad_normed_one = jnp.einsum(
         "cte,cde->td", grad_proj, dense_low[:3], preferred_element_type=jnp.float32
     )
     grad_input_norm, grad_gain_one = norm_one_back(grad_normed_one)
     input_grad = grad_hidden + grad_input_norm
-    dense_grad = jnp.concatenate([grad_in_proj, grad_out_proj[None]], axis=0)
     vector_grad = jnp.concatenate(
         [grad_gain_one[None], grad_gain_two[None], grad_centroids], axis=0
     )
-    dense_grad, vector_grad = (
-        lax.psum_scatter(dense_grad, ("dp", "expert"), scatter_dimension=1, tiled=True),
-        lax.psum_scatter(vector_grad, ("dp", "expert"), scatter_dimension=1, tiled=True),
-    )
-    squares = (
-        jnp.sum(dense_grad * dense_grad)
-        + jnp.sum(vector_grad * vector_grad)
-        + jnp.sum(expert_grad * expert_grad)
-    )
-    grad_norm = jnp.sqrt(lax.psum(squares, ("dp", "expert")))
+    if own_rows % 8 == 0:
+        dense_grad, vector_grad = scatter_dense(
+            normed_low, mixed_low, grad_attn, grad_proj, vector_grad, splits, owners
+        )
+    else:
+        grad_in_proj = jnp.einsum(
+            "td,cte->cde", normed_low, grad_proj, preferred_element_type=jnp.float32
+        )
+        grad_out_proj = jnp.dot(mixed_low.T, grad_attn, preferred_element_type=jnp.float32)
+        dense_grad, vector_grad = (
+            lax.psum_scatter(
+                jnp.concatenate([grad_in_proj, grad_out_proj[None]], axis=0),
+                ("dp", "expert"),
+                scatter_dimension=1,
+                tiled=True,
+            ),
+            lax.psum_scatter(vector_grad, ("dp", "expert"), scatter_dimension=1, tiled=True),
+        )
+    squares = norm_squares(dense_grad, vector_grad, expert_low_grad, splits, owners)
+    grad_norm = jnp.sqrt(squares)
     factor = jnp.minimum(1.0, clip_norm / (grad_norm + 1e-06))
     dense_new = adam_update(
         dense_weights, dense_grad, dense_first, dense_second, dense_average, factor, dense_rate

time: 867 us -> 517 us (0.60)
  blocking collectives: 263 us -> 0 us
  waiting for transfers between devices: 226 us -> 0.04 us
  Pallas kernels: 181 us -> 368 us
  local copies, waits for them, and re-layouts: 29.9 us -> 12.8 us
  matrix products: 64.2 us -> 49.6 us
  other arithmetic: 48.2 us -> 38.6 us
    unnamed x6 -> x3, waiting for transfers between devices: 216 us -> 0.03 us
    pallas_call x0 -> x3, Pallas kernels: none -> 185 us  [the longest x1 111 us: gather_dense(): pl.pallas_call(partial(gather_kernel, dps, pairs), out_shape=[jax.ShapeDt...]
    all_gather x1 -> x0, blocking collectives: 118 us -> none  [shards(): lax.all_gather(vector_params.astype(jnp.bfloat16), ('dp', 'expert'), axis...]
    unnamed x1 -> x0, blocking collectives: 105 us -> none
    psum x1 -> x0, blocking collectives: 39.3 us -> none  [shards(): grad_norm = jnp.sqrt(lax.psum(squares, ('dp', 'expert')))]
    concatenate x1 -> x0, local copies, waits for them, and re-layouts: 12.1 us -> none  [shards(): dense_grad = jnp.concatenate([grad_in_proj, grad_out_proj[None]], axis=0)]
    all_gather x1, waiting for transfers between devices: 9.67 us -> 0.01 us  [shards(): expert_low = lax.all_gather(own_low, 'dp', axis=0)]
  transfers between devices with their start and end apart: 6 -> 4, of which waited for: 3 -> 0; matrix products, arithmetic and copies ran while one was open for 9% -> 14% of each run, Pallas kernels for 2% -> 43%
where the time goes in v3:
time: 517 us; the launch traced here: 513 us
  Pallas kernels  368 us (71%)
  matrix products  49.6 us (10%)
  other arithmetic  38.6 us (7%)
  starting transfers between devices  27.4 us (5%)
  between operations  16.8 us (3%)
  local copies, waits for them, and re-layouts  12.8 us (2%)
    pallas_call x1, Pallas kernels, moe(): pl.pallas_call(partial(moe_kernel, n, cap), out_shape=[jax.ShapeDtypeStru...  139 us
    pallas_call x1, Pallas kernels, gather_dense(): pl.pallas_call(partial(gather_kernel, dps, pairs), out_shape=[jax.ShapeDt...  111 us
    pallas_call x1, Pallas kernels, scatter_dense(): pl.pallas_call(partial(scatter_kernel, dps, pairs), out_shape=[jax.ShapeD...  62.7 us
    pallas_call x1, Pallas kernels, attend_backward(): pl.pallas_call(partial(bwd_kernel, QB), grid=(D // 128,), in_specs=[sp(0)...  26.6 us
    all_to_all x1, starting transfers between devices, shards(): lax.all_to_all(produced_low, 'expert', split_axis=0, concat_axis=0, tiled...  20.6 us
    pallas_call x1, Pallas kernels, attend_forward(): pl.pallas_call(partial(fwd_kernel, QB), grid=(D // 128,), in_specs=[sp(0)...  18.2 us
    add x3, other arithmetic, adam_update(): average_new = ema_keep * average + (1.0 - ema_keep) * updated  16.2 us
    dot_general x2, matrix products, to_slots(): placed = jnp.dot(slot_pick.T, rows, preferred_element_type=jnp.float32)  14.2 us
  transfers between devices with their start and end apart: 4, of which 0 were waited for; matrix products, arithmetic and copies ran while one was open for 14% of the time, Pallas kernels for 43%

profile of v3, /device:TPU:0, one launch (start us, length us, event | category | flops | bytes accessed | tf_op | source)
XLA Modules:
  0.0 513.4 jit_solution(14769487654085393961)
XLA Ops:
  7.3 4.1 convert_element_type.87
  12.4 5.9 %fusion.16 = bf16[2048,768]{1,0:T(8,128)(2,1)} fusion(bf16[1024,768]{1,0:T(8,128)(2,1)S(1)} %copy-done.20, s32[1024]{0:T(1024)S(1)} %select_reduce_fusion.2), kind=kOutput, calls=%fused_computation.32 | convolution fusion | flops 3224895488 | bytes 4722688 | tf_op jit(solution)/shard_map/dot_general | solution.py:593
  18.4 6.5 %all-to-all-start = ((bf16[8,256,768]{2,1,0:T(8,128)(2,1)}), bf16[8,256,768]{2,1,0:T(8,128)(2,1)}, u32[]{:S(2)}, u32[]{:S(2)}) async-start(bf16[8,256,768]{2,1,0:T(8,128)(2,1)} %bitcast.75), calls=%async_computation | async-start | bytes 6291456 | tf_op jit(solution)/shard_map/all_to_all | solution.py:601
  27.4 110.7 %shard_map.298 = (bf16[4,768,768]{2,1,0:T(8,128)(2,1)S(1)}, bf16[4,4,16,256]{3,2,1,0:T(8,128)(2,1)S(1)}) custom-call(f32[4,24,768]{2,1,0:T(8,128)S(1)} %copy-done.6, f32[16,128]{1,0:T(8,128)S(1)} %scatter.6.v_ref), custom_call_target="tpu_custom_call" | custom-call | bytes 104857600 | tf_op jit(solution)/shard_map/pallas_call | solution.py:376
  138.1 2.2 copy-done.8
  142.7 2.1 fusion.19
  144.8 1.9 fusion.17.x_ref
  146.7 5.4 %convert_bitcast_fusion.q_ref.k_ref.v_ref = bf16[3,1024,768]{2,1,0:T(8,128)(2,1)} fusion(bf16[4,768,768]{2,1,0:T(8,128)(2,1)S(1)} %copy-done.9, bf16[1024,768]{1,0:T(8,128)(2,1)S(1)} %fusion.17.x_ref), kind=kOutput, calls=%fused_computation.22 | convolution fusion | flops 3626237952 | bytes 9830400 | tf_op jit(solution)/shard_map/td,cde->cte/dot_general | solution.py:609
  153.4 18.2 %shard_map.299 = (bf16[1024,768]{1,0:T(8,128)(2,1)S(1)}, f32[6,1024,128]{2,1,0:T(8,128)S(1)}) custom-call(bf16[3,1024,768]{2,1,0:T(8,128)(2,1)} %convert_bitcast_fusion.q_ref.k_ref.v_ref, bf16[3,1024,768]{2,1,0:T(8,128)(2,1)} %convert_bitcast_fusion.q_ref.k_ref.v_ref, bf16[3,1024,768]{2,1,0:T(8,128)(2,1)} %convert_bitcast_fusion.q_ref.k_ref.v_ref, ...), custom_call_target="tpu_custom_call" | custom-call | tf_op jit(solution)/shard_map/pallas_call | solution.py:73
  174.3 2.0 fusion.47
  177.8 8.3 %fusion.15 = bf16[2048,768]{1,0:T(8,128)(2,1)} fusion(s32[1024]{0:T(1024)S(1)} %select_reduce_fusion.2, f32[1024,768]{1,0:T(8,128)} %copy-done.12, f32[768]{0:T(1024)S(1)} %reshape.301, f32[1024]{0:T(1024)S(1)} %fusion.63, f32[1024]{0:T(1024)S(1)} %broadcast_multiply_fusion), kind=kOutput, calls=%fused_computation.31 | convolution fusion | flops 3228041216 | bytes 6306816 | tf_op jit(solution)/shard_map/dot_general | solution.py:593
  186.8 138.8 %shard_map.300 = (bf16[8,256,768]{2,1,0:T(8,128)(2,1)}, f32[8,8,256]{2,1,0:T(8,128)}, bf16[8,256,768]{2,1,0:T(8,128)(2,1)}, bf16[4,2,768,768]{3,2,1,0:T(8,128)(2,1)}) custom-call(bf16[8,256,768]{2,1,0:T(8,128)(2,1)} %bitcast.84, f32[8,8,256]{2,1,0:T(8,128)} %reshape.291.gate_ref, bf16[2048,768]{1,0:T(8,128)(2,1)} %bitcast.12.cot_ref, f32[2048,1]{1,0:T(8,128)} %bitcast.76, ...), custom_call_target="tpu_custom_call" | custom-call | flops 57982058496 | bytes 41943040 | tf_op jit(solution)/shard_map/pallas_call | solution.py:287
  327.0 20.6 %all-to-all-start.1 = ((bf16[8,256,768]{2,1,0:T(8,128)(2,1)}), bf16[8,256,768]{2,1,0:T(8,128)(2,1)}, u32[]{:S(2)}, u32[]{:S(2)}) async-start(bf16[8,256,768]{2,1,0:T(8,128)(2,1)} %get-tuple-element.52), calls=%async_computation.1 | async-start | bytes 6291456 | tf_op jit(solution)/shard_map/all_to_all | solution.py:636
  348.8 5.8 %fusion = f32[1024,768]{1,0:T(8,128)S(1)} fusion(bf16[2048,768]{1,0:T(8,128)(2,1)} %bitcast.83, s32[1024]{0:T(1024)S(1)} %select_reduce_fusion.2), kind=kOutput, calls=%fused_computation.3 | convolution fusion | flops 3223322624 | bytes 6295552 | tf_op jit(solution)/shard_map/dot_general | solution.py:597
  354.6 2.5 multiply_reduce_fusion
  363.4 26.6 %shard_map.301.gp_ref = bf16[3,1024,768]{2,1,0:T(8,128)(2,1)} custom-call(bf16[3,1024,768]{2,1,0:T(8,128)(2,1)} %convert_bitcast_fusion.q_ref.k_ref.v_ref, bf16[3,1024,768]{2,1,0:T(8,128)(2,1)} %convert_bitcast_fusion.q_ref.k_ref.v_ref, bf16[3,1024,768]{2,1,0:T(8,128)(2,1)} %convert_bitcast_fusion.q_ref.k_ref.v_ref, f32[6,1024,128]{2,1,0:T(8,128)S(1)} %copy-done.3, ...), custom_call_target="tpu_custom_call" | custom-call | tf_op jit(solution)/shard_map/pallas_call | solution.py:123
  390.0 7.1 %fusion.20 = (f32[1024]{0:T(1024)S(1)}, f32[1024,768,1]{1,0,2:T(8,128)S(1)}) fusion(bf16[1024,768]{1,0:T(8,128)(2,1)} %param.23, f32[768]{0:T(1024)S(1)} %reshape.300, f32[1024]{0:T(1024)S(1)} %broadcast_multiply_fusion.1, bf16[3,1024,768]{2,1,0:T(8,128)(2,1)} %shard_map.301.gp_ref, bf16[4,768,768]{2,1,0:T(8,128)(2,1)S(1)} %bitcast.74), kind=kOutput, calls=%fused_computation.36 | convolution fusion | flops 3627809792 | bytes 12988416 | tf_op jit(solution)/shard_map/cte,cde->td/dot_general | solution.py:657
  398.9 2.0 fusion.27
  401.0 62.7 %shard_map.302 = (f32[4,24,768]{2,1,0:T(8,128)S(1)}, f32[16,768]{1,0:T(8,128)S(1)}) custom-call(bf16[1024,768]{1,0:T(8,128)(2,1)S(1)} %copy-done.5, bf16[1024,768]{1,0:T(8,128)(2,1)S(1)} %copy-done.11, bf16[1024,768]{1,0:T(8,128)(2,1)S(1)} %fusion.32.ga_ref, bf16[3,1024,768]{2,1,0:T(8,128)(2,1)} %shard_map.301.gp_ref, f32[16,768]{1,0:T(8,128)S(1)} %select_maximum_fusion.v_ref), custom_call_target="tpu_custom_call" | custom-call | flops 4831838208 | bytes 104857600 | tf_op jit(solution)/shard_map/pallas_call | solution.py:464
  463.7 3.4 add_add_fusion.2
  467.1 7.7 %multiply_add_fusion.2 = f32[1024,768]{1,0:T(8,128)} fusion(f32[1024,768]{1,0:T(8,128)} %copy-done.12, bf16[2048,768]{1,0:T(8,128)(2,1)} %bitcast.15, s32[1024]{0:T(1024)S(1)} %select_reduce_fusion.2, f32[1024]{0:T(1024)S(1)} %add_divide_fusion), kind=kOutput, calls=%fused_computation.42 | convolution fusion | flops 3224895488 | bytes 9445376 | tf_op jit(solution)/shard_map/dot_general | solution.py:597
  476.5 11.2 %shard_map.303 = f32[8,128]{1,0:T(8,128)S(1)} custom-call(f32[4,24,768]{2,1,0:T(8,128)S(1)} %get-tuple-element.56.d_ref, f32[10,24]{1,0:T(8,128)S(1)} %constant_dynamic-slice_fusion.v_ref, bf16[2,768,768]{2,1,0:T(8,128)(2,1)S(1)} %bitcast.68), custom_call_target="tpu_custom_call" | custom-call | tf_op jit(solution)/shard_map/pallas_call | solution.py:508
  489.8 2.2 multiply_add_fusion.3
  492.0 13.2 %multiply_add_fusion = (f32[1,2,768,768]{3,2,1,0:T(8,128)}, f32[1,2,768,768]{3,2,1,0:T(8,128)}, f32[1,2,768,768]{3,2,1,0:T(8,128)}, f32[1,2,768,768]{3,2,1,0:T(8,128)}) fusion(f32[1,2,768,768]{3,2,1,0:T(8,128)} %param.41, f32[1,2,768,768]{3,2,1,0:T(8,128)} %param.32, f32[]{:T(128)S(6)} %min.3, bf16[1,2,768,768]{3,2,1,0:T(8,128)(2,1)S(1)} %copy-done.1, ...), kind=kLoop, calls=%fused_computation.18 | loop fusion | flops 23592960 | bytes 40108036 | tf_op jit(solution)/shard_map/add | solution.py:526
  (130 shorter events, 25.5 us)
Async XLA Ops:
  7.2 4.6 copy-start.28
  7.2 5.2 %copy-start.20 = (bf16[1024,768]{1,0:T(8,128)(2,1)S(1)}, bf16[1024,768]{1,0:T(8,128)(2,1)}, u32[]{:S(2)}) copy-start(bf16[1024,768]{1,0:T(8,128)(2,1)} %param.24) | copy-start | bytes 4718596
  7.2 178.9 %all-gather.2.cloned.1.call-start = ((), (), s32[]{:S(2)}) async-start(), calls=%async_computation.3 | async-start | bytes 11796480 | tf_op jit(solution)/shard_map/all_gather | solution.py:605
  18.4 6.7 %copy-start.31 = (s32[8]{0:T(128)S(1)}, s32[8]{0:T(128)}, u32[]{:S(2)}) copy-start(s32[8]{0:T(128)} %param.26) | copy-start | bytes 100
  18.4 7.1 %copy-start.29 = (f32[8]{0:T(128)S(1)}, f32[8]{0:T(128)}, u32[]{:S(2)}) copy-start(f32[8]{0:T(128)} %param.27) | copy-start | bytes 100
  18.4 7.4 %copy-start.7 = (s32[1,1024]{1,0:T(1,128)S(1)}, s32[1,1024]{1,0:T(1,128)}, u32[]{:S(2)}) copy-start(s32[1,1024]{1,0:T(1,128)} %drow_ref.3) | copy-start | bytes 12292
  18.4 9.0 %copy-start.24 = (f32[10,24]{1,0:T(8,128)S(1)}, f32[10,24]{1,0:T(8,128)}, u32[]{:S(2)}) copy-start(f32[10,24]{1,0:T(8,128)} %param.31) | copy-start | bytes 2884
  18.4 9.0 %copy-start.6 = (f32[4,24,768]{2,1,0:T(8,128)S(1)}, f32[4,24,768]{2,1,0:T(8,128)}, u32[]{:S(2)}) copy-start(f32[4,24,768]{2,1,0:T(8,128)} %w_ref.1) | copy-start | bytes 884740
  18.4 167.7 %all-to-all-start = ((bf16[8,256,768]{2,1,0:T(8,128)(2,1)}), bf16[8,256,768]{2,1,0:T(8,128)(2,1)}, u32[]{:S(2)}, u32[]{:S(2)}) async-start(bf16[8,256,768]{2,1,0:T(8,128)(2,1)} %bitcast.75), calls=%async_computation | async-start | bytes 6291456 | tf_op jit(solution)/shard_map/all_to_all | solution.py:601
  24.9 450.0 %reduce-scatter.4.cloned.1.call-start = ((), (), s32[]{:S(2)}) async-start(), calls=%async_computation.4 | async-start | bytes 11796480
  140.9 5.9 %copy-start.9 = (bf16[4,768,768]{2,1,0:T(8,128)(2,1)S(1)}, bf16[4,768,768]{2,1,0:T(8,128)(2,1)}, u32[]{:S(2)}) copy-start(bf16[4,768,768]{2,1,0:T(8,128)(2,1)} %copy-done.8) | copy-start | bytes 14155780
  153.4 18.3 %copy-start.14 = (bf16[1024,768]{1,0:T(8,128)(2,1)S(1)}, bf16[1024,768]{1,0:T(8,128)(2,1)}, u32[]{:S(2)}) copy-start(bf16[1024,768]{1,0:T(8,128)(2,1)} %param.23) | copy-start | bytes 4718596
  327.0 140.1 %all-to-all-start.1 = ((bf16[8,256,768]{2,1,0:T(8,128)(2,1)}), bf16[8,256,768]{2,1,0:T(8,128)(2,1)}, u32[]{:S(2)}, u32[]{:S(2)}) async-start(bf16[8,256,768]{2,1,0:T(8,128)(2,1)} %get-tuple-element.52), calls=%async_computation.1 | async-start | bytes 6291456 | tf_op jit(solution)/shard_map/all_to_all | solution.py:636
  348.8 5.8 %copy-start.13 = (f32[1024,768]{1,0:T(8,128)S(1)}, f32[1024,768]{1,0:T(8,128)}, u32[]{:S(2)}) copy-start(f32[1024,768]{1,0:T(8,128)} %copy-done.12) | copy-start | bytes 9437188
  354.6 6.8 %slice-start = ((s8[4718592]{0:T(1024)(128)(4,1)}), s8[4194304]{0:T(1024)(128)(4,1)S(1)}, s32[]{:S(2)}) async-start(s8[4718592]{0:T(1024)(128)(4,1)} %bitcast.73), calls=%async_computation.5 | async-start | bytes 8388608
  390.0 7.1 %copy-start.15 = (bf16[1024,768]{1,0:T(8,128)(2,1)S(1)}, bf16[1024,768]{1,0:T(8,128)(2,1)}, u32[]{:S(2)}) copy-start(bf16[1024,768]{1,0:T(8,128)(2,1)} %param.23) | copy-start | bytes 4718596
  400.9 62.8 %copy-start.17 = (f32[1024,768]{1,0:T(8,128)S(1)}, f32[1024,768]{1,0:T(8,128)}, u32[]{:S(2)}) copy-start(f32[1024,768]{1,0:T(8,128)} %copy-done.16) | copy-start | bytes 9437188
  400.9 62.8 %copy-start.19 = (f32[1024,768,1]{1,0,2:T(8,128)S(1)}, f32[1024,768,1]{1,0,2:T(8,128)}, u32[]{:S(2)}) copy-start(f32[1024,768,1]{1,0,2:T(8,128)} %copy-done.18) | copy-start | bytes 9437188
  401.0 62.8 %copy-start.22 = (bf16[1024,768]{1,0:T(8,128)(2,1)S(1)}, bf16[1024,768]{1,0:T(8,128)(2,1)}, u32[]{:S(2)}) copy-start(bf16[1024,768]{1,0:T(8,128)(2,1)} %param.24) | copy-start | bytes 4718596
  467.1 21.9 %copy-start.25 = (f32[10,24]{1,0:T(8,128)S(1)}, f32[10,24]{1,0:T(8,128)}, u32[]{:S(2)}) copy-start(f32[10,24]{1,0:T(8,128)} %param.38) | copy-start | bytes 2884
  467.1 21.9 %copy-start.26 = (f32[10,24]{1,0:T(8,128)S(1)}, f32[10,24]{1,0:T(8,128)}, u32[]{:S(2)}) copy-start(f32[10,24]{1,0:T(8,128)} %param.36) | copy-start | bytes 2884
  467.1 21.9 %copy-start.27 = (f32[10,24]{1,0:T(8,128)S(1)}, f32[10,24]{1,0:T(8,128)}, u32[]{:S(2)}) copy-start(f32[10,24]{1,0:T(8,128)} %param.37) | copy-start | bytes 2884
  467.1 22.6 %copy-start.23 = (f32[4,24,768]{2,1,0:T(8,128)S(1)}, f32[4,24,768]{2,1,0:T(8,128)}, u32[]{:S(2)}) copy-start(f32[4,24,768]{2,1,0:T(8,128)} %param.35) | copy-start | bytes 884740
  476.5 15.5 %copy-start.1 = (bf16[1,2,768,768]{3,2,1,0:T(8,128)(2,1)S(1)}, bf16[1,2,768,768]{3,2,1,0:T(8,128)(2,1)}, u32[]{:S(2)}) copy-start(bf16[1,2,768,768]{3,2,1,0:T(8,128)(2,1)} %reduce-scatter.4.cloned.1.call-done) | copy-start | bytes 7077892
  (14 other events, 38.1 us)
Sparse Core Ops, SparseCore 0:
  11.5 125.6 all-gather.1
  325.7 137.5 reduce-scatter.3

commit v4 on v2

--- a/solution.py
+++ b/solution.py
@@ -78,43 +78,62 @@
         compiler_params=pltpu.CompilerParams(vmem_limit_bytes=48*2**20),
     )(projected,projected,projected,dcol,drow)
 
-def bwd_kernel(QB,q_ref,k_ref,v_ref,lse_ref,g_ref,dcol_ref,drow_ref,out_ref,bias_ref,dk_ref,dv_ref):
-    reach=WINDOW//QB
-    low_lane = lax.broadcasted_iota(jnp.int32,(QB,128),1) < HEAD_DIM
-    @pl.when(pl.program_id(0)==0)
+QB = 256
+
+
+def transposed_bias(bias_ref, dcol_ref, drow_ref, QB):
+    reach = WINDOW // QB
+    for i in range(LEN // QB):
+        first = max(0, i - reach) * QB
+        W = (i + 1) * QB - first
+        kp = first + lax.broadcasted_iota(jnp.int32, (W, QB), 0)
+        qp = i * QB + lax.broadcasted_iota(jnp.int32, (W, QB), 1)
+        ok = (kp <= qp) & (dcol_ref[first : first + W, :] == drow_ref[:, i * QB : (i + 1) * QB])
+        bias_ref[:W, i * QB : (i + 1) * QB] = jnp.where(ok, 0.0, masked_score)
+
+
+def head_pair_backward(QB, q_ref, k_ref, v_ref, lse_ref, g_ref, bias_ref, dk_ref, dv_ref, put_dq):
+    reach = WINDOW // QB
+    low_lane = lax.broadcasted_iota(jnp.int32, (QB, 128), 1) < HEAD_DIM
+    dk_ref[...] = jnp.zeros_like(dk_ref)
+    dv_ref[...] = jnp.zeros_like(dv_ref)
+    for i in range(LEN // QB):
+        rows = slice(i * QB, (i + 1) * QB)
+        first = max(0, i - reach) * QB
+        W = (i + 1) * QB - first
+        keys = slice(first, first + W)
+        q = q_ref[0, rows, :] * jnp.bfloat16(HEAD_DIM**-0.5)
+        zero = jnp.zeros_like(q)
+        qs = jnp.concatenate([jnp.where(low_lane, q, zero), jnp.where(low_lane, zero, q)], axis=0)
+        g = g_ref[rows, :]
+        gs = jnp.concatenate([jnp.where(low_lane, g, zero), jnp.where(low_lane, zero, g)], axis=0)
+        k = k_ref[0, keys, :]
+        st = lax.dot_general(k, qs, NT, preferred_element_type=jnp.float32)
+        bias = bias_ref[:W, rows]
+        lse = jnp.transpose(lse_ref[0, rows, :])
+        lse = jnp.concatenate([lse[0:1, :], lse[64:65, :]], axis=1)
+        p = jnp.exp(st + jnp.concatenate([bias, bias], axis=1) - lse)
+        dp = lax.dot_general(v_ref[0, keys, :], gs, NT, preferred_element_type=jnp.float32)
+        inner = jnp.sum(p * dp, axis=0, keepdims=True)
+        ds = (p * (dp - inner)).astype(jnp.bfloat16)
+        dk_ref[keys, :] += jnp.dot(ds, qs, preferred_element_type=jnp.float32)
+        dv_ref[keys, :] += jnp.dot(p.astype(jnp.bfloat16), gs, preferred_element_type=jnp.float32)
+        dq = lax.dot_general(ds, k, TN, preferred_element_type=jnp.float32)
+        put_dq(rows, (jnp.where(low_lane, dq[:QB], dq[QB:]) * HEAD_DIM**-0.5).astype(jnp.bfloat16))
+
+
+def bwd_kernel(QB, q_ref, k_ref, v_ref, lse_ref, g_ref, dcol_ref, drow_ref, out_ref, bias_ref, dk_ref, dv_ref):
+    @pl.when(pl.program_id(0) == 0)
     def _():
-        for i in range(LEN//QB):
-            first=max(0,i-reach)*QB; W=(i+1)*QB-first
-            kp=first+lax.broadcasted_iota(jnp.int32,(W,QB),0)
-            qp=i*QB+lax.broadcasted_iota(jnp.int32,(W,QB),1)
-            ok=(kp<=qp)&(dcol_ref[first:first+W,:]==drow_ref[:,i*QB:(i+1)*QB])
-            bias_ref[:W,i*QB:(i+1)*QB]=jnp.where(ok,0.0,masked_score)
-    dk_ref[...]=jnp.zeros_like(dk_ref)
-    dv_ref[...]=jnp.zeros_like(dv_ref)
-    for i in range(LEN//QB):
-        rows=slice(i*QB,(i+1)*QB)
-        first=max(0,i-reach)*QB; W=(i+1)*QB-first
-        keys=slice(first,first+W)
-        q=q_ref[0,rows,:]*jnp.bfloat16(HEAD_DIM**-0.5)
-        zero=jnp.zeros_like(q)
-        qs=jnp.concatenate([jnp.where(low_lane,q,zero),jnp.where(low_lane,zero,q)],axis=0)
-        g=g_ref[rows,:]
-        gs=jnp.concatenate([jnp.where(low_lane,g,zero),jnp.where(low_lane,zero,g)],axis=0)
-        k=k_ref[0,keys,:]
-        st=lax.dot_general(k,qs,NT,preferred_element_type=jnp.float32)
-        bias=bias_ref[:W,rows]
-        lse=jnp.transpose(lse_ref[0,rows,:])
-        lse=jnp.concatenate([lse[0:1,:],lse[64:65,:]],axis=1)
-        p=jnp.exp(st+jnp.concatenate([bias,bias],axis=1)-lse)
-        dp=lax.dot_general(v_ref[0,keys,:],gs,NT,preferred_element_type=jnp.float32)
-        inner=jnp.sum(p*dp,axis=0,keepdims=True)
-        ds=(p*(dp-inner)).astype(jnp.bfloat16)
-        dk_ref[keys,:]+=jnp.dot(ds,qs,preferred_element_type=jnp.float32)
-        dv_ref[keys,:]+=jnp.dot(p.astype(jnp.bfloat16),gs,preferred_element_type=jnp.float32)
-        dq=lax.dot_general(ds,k,TN,preferred_element_type=jnp.float32)
-        out_ref[0,rows,:]=(jnp.where(low_lane,dq[:QB],dq[QB:])*HEAD_DIM**-0.5).astype(jnp.bfloat16)
-    out_ref[1,:,:]=dk_ref[...].astype(jnp.bfloat16)
-    out_ref[2,:,:]=dv_ref[...].astype(jnp.bfloat16)
+        transposed_bias(bias_ref, dcol_ref, drow_ref, QB)
+
+    def put_dq(rows, value):
+        out_ref[0, rows, :] = value
+
+    head_pair_backward(QB, q_ref, k_ref, v_ref, lse_ref, g_ref, bias_ref, dk_ref, dv_ref, put_dq)
+    out_ref[1, :, :] = dk_ref[...].astype(jnp.bfloat16)
+    out_ref[2, :, :] = dv_ref[...].astype(jnp.bfloat16)
+
 
 def attend_backward(projected, documents, lse, grad_mixed, QB=256):
     T=projected.shape[1]; D=projected.shape[2]
@@ -130,7 +149,7 @@
 
 
 MESH=pl.DeviceIdType.MESH
-TILE=256
+TILE=512
 
 def flip(a,b,n):
     out=0
@@ -148,10 +167,11 @@
     return x*half, half+x*(0.5*(1.0-t*t))*(c+(3*0.044715*c)*sq)
 
 def moe_kernel(n,cap,send_ref,gate_ref,cot_ref,scale_ref,w_ref,
-               back_ref,chosen_ref,ret_ref,gw_ref,
+               back_ref,late_ref,chosen_ref,ret_ref,gw_ref,
                recv,gates,cot,w,gw,ret_s,gs_s,ch_s,g_s,racc,sacc,
                send_sem,recv_sem,gate_send,gate_recv,back_send,back_recv,ch_send,ch_recv,w_sem,loc_sem,ret_sem):
     per=TILE//cap
+    tiles=n//per
     chunks=w_ref.shape[0]
     me=lax.axis_index("expert")
     barrier=pltpu.get_barrier_semaphore()
@@ -161,37 +181,24 @@
     lax.fori_loop(1,n,greet,0)
     pl.semaphore_wait(barrier,n-1)
 
-    def row_copy(peer):
-        return pltpu.make_async_remote_copy(src_ref=send_ref.at[peer],dst_ref=recv.at[me],
-            send_sem=send_sem.at[peer],recv_sem=recv_sem.at[me],device_id={"expert":peer},device_id_type=MESH)
-    def gate_copy(peer):
-        return pltpu.make_async_remote_copy(src_ref=gate_ref.at[peer],dst_ref=gates.at[me],
-            send_sem=gate_send.at[peer],recv_sem=gate_recv.at[me],device_id={"expert":peer},device_id_type=MESH)
-    def row_in(src):
-        return pltpu.make_async_remote_copy(src_ref=send_ref.at[src],dst_ref=recv.at[src],
-            send_sem=send_sem.at[src],recv_sem=recv_sem.at[src],device_id={"expert":src},device_id_type=MESH)
-    def gate_in(src):
-        return pltpu.make_async_remote_copy(src_ref=gate_ref.at[src],dst_ref=gates.at[src],
-            send_sem=gate_send.at[src],recv_sem=gate_recv.at[src],device_id={"expert":src},device_id_type=MESH)
-    def back_copy(src):
-        return pltpu.make_async_remote_copy(src_ref=gs_s.at[src],dst_ref=back_ref.at[me],
-            send_sem=back_send.at[src],recv_sem=back_recv.at[me],device_id={"expert":src},device_id_type=MESH)
-    def ch_copy(src):
-        return pltpu.make_async_remote_copy(src_ref=ch_s.at[src],dst_ref=chosen_ref.at[me],
-            send_sem=ch_send.at[src],recv_sem=ch_recv.at[me],device_id={"expert":src},device_id_type=MESH)
-    def back_in(src):
-        return pltpu.make_async_remote_copy(src_ref=gs_s.at[src],dst_ref=back_ref.at[src],
-            send_sem=back_send.at[src],recv_sem=back_recv.at[src],device_id={"expert":src},device_id_type=MESH)
-    def ch_in(src):
-        return pltpu.make_async_remote_copy(src_ref=ch_s.at[src],dst_ref=chosen_ref.at[src],
-            send_sem=ch_send.at[src],recv_sem=ch_recv.at[src],device_id={"expert":src},device_id_type=MESH)
-
-    def push(i,_):
-        peer=flip(me,n-1-i,n)
-        gate_copy(peer).start()
-        row_copy(peer).start()
+    def copies(src,dst,send,recv_,peer,there):
+        return pltpu.make_async_remote_copy(src_ref=src,dst_ref=dst,send_sem=send.at[peer],recv_sem=recv_.at[there],
+            device_id={"expert":peer},device_id_type=MESH)
+    def row_copy(peer): return copies(send_ref.at[peer],recv.at[me],send_sem,recv_sem,peer,me)
+    def gate_copy(peer): return copies(gate_ref.at[peer],gates.at[me],gate_send,gate_recv,peer,me)
+    def row_in(src): return copies(send_ref.at[src],recv.at[src],send_sem,recv_sem,src,src)
+    def gate_in(src): return copies(gate_ref.at[src],gates.at[src],gate_send,gate_recv,src,src)
+    def back_copy(src): return copies(gs_s.at[src],back_ref.at[flip(src,me,n)],back_send,back_recv,src,me)
+    def ch_copy(src): return copies(ch_s.at[src],chosen_ref.at[flip(src,me,n)],ch_send,ch_recv,src,me)
+    def back_in(src): return copies(gs_s.at[src],back_ref.at[flip(src,me,n)],back_send,back_recv,src,src)
+    def ch_in(src): return copies(ch_s.at[src],chosen_ref.at[flip(src,me,n)],ch_send,ch_recv,src,src)
+
+    def push(o,_):
+        gate_copy(flip(me,o,n)).start()
+        row_copy(flip(me,o,n)).start()
         return 0
-    lax.fori_loop(0,n-1,push,0)
+    last=(tiles-1)*per
+    lax.fori_loop(0,last-1,lambda i,c: push(last-1-i,c),0)
     own=[pltpu.make_async_copy(send_ref.at[me],recv.at[me],loc_sem.at[0]),
          pltpu.make_async_copy(gate_ref.at[me],gates.at[me],loc_sem.at[1]),
          pltpu.make_async_copy(cot_ref,cot,loc_sem.at[2]),
@@ -202,15 +209,22 @@
         return 0
     lax.fori_loop(0,chunks,wipe,0)
     for c in own: c.wait()
+    own_back=pltpu.make_async_copy(gs_s.at[me],back_ref.at[0],loc_sem.at[1])
+    own_ch=pltpu.make_async_copy(ch_s.at[me],chosen_ref.at[0],loc_sem.at[0])
 
     def tile(t,_):
-        block=flip(me//per,t,n//per)
-        for j in range(per):
+        @pl.when(t==1)
+        def _():
+            lax.fori_loop(last,n,push,0)
+        block=flip(me//per,t,tiles)
+        def arrive(j,_):
             src=block*per+j
             @pl.when(src!=me)
             def _():
                 gate_in(src).wait_recv()
                 row_in(src).wait_recv()
+            return 0
+        lax.fori_loop(0,per,arrive,0)
         at=pl.ds(pl.multiple_of(block*per,per),per)
         rows=pl.ds(pl.multiple_of(block*TILE,TILE),TILE)
         gate=jnp.transpose(jnp.sum(gates[at],axis=0))[:,0:1]
@@ -231,71 +245,545 @@
             gw[c,1]+=lax.dot_general(g,a,TN,preferred_element_type=jnp.float32)
             return 0
         lax.fori_loop(0,chunks,chunk,0)
+        gs_s[at]=sacc[...].astype(jnp.bfloat16).reshape(per,cap,recv.shape[2])
+        def give(j,_):
+            src=block*per+j
+            @pl.when(src!=me)
+            def _():
+                back_copy(src).start()
+            @pl.when(src==me)
+            def _():
+                own_back.start()
+            return 0
+        @pl.when(t<tiles-1)
+        def _():
+            lax.fori_loop(0,per,give,0)
+        @pl.when(t==tiles-1)
+        def _():
+            pltpu.make_async_copy(gs_s.at[at],late_ref,loc_sem.at[2]).start()
         ret=racc[...].astype(jnp.bfloat16)
+        ret_s[at]=ret.reshape(per,cap,recv.shape[2])
+        pltpu.make_async_copy(ret_s.at[at],ret_ref.at[at],ret_sem.at[t]).start()
         grad_out=cot[rows,:].astype(jnp.float32)*scale_ref[rows,:]
         chosen=jnp.sum(grad_out*ret.astype(jnp.float32),axis=1,keepdims=True)*gate*(1.0-gate)
         chosen=jnp.transpose(jnp.broadcast_to(chosen,(TILE,128)))[0:8,:]
-        gs_s[at]=sacc[...].astype(jnp.bfloat16).reshape(per,cap,recv.shape[2])
-        ret_s[at]=ret.reshape(per,cap,recv.shape[2])
-        for j in range(per):
+        def tell(j,_):
             src=block*per+j
             ch_s[src]=chosen
             @pl.when(src!=me)
             def _():
                 ch_copy(src).start()
-                back_copy(src).start()
             @pl.when(src==me)
             def _():
-                pltpu.make_async_copy(ch_s.at[me],chosen_ref.at[me],loc_sem.at[0]).start()
-                pltpu.make_async_copy(gs_s.at[me],back_ref.at[me],loc_sem.at[1]).start()
-        pltpu.make_async_copy(ret_s.at[at],ret_ref.at[at],ret_sem.at[t]).start()
+                own_ch.start()
+            return 0
+        lax.fori_loop(0,per,tell,0)
         return 0
-    lax.fori_loop(0,n//per,tile,0)
+    lax.fori_loop(0,tiles,tile,0)
     def pack(c,_):
         w[c]=gw[c].astype(jnp.bfloat16)
+        pltpu.make_async_copy(w.at[c],gw_ref.at[c],w_sem).start()
         return 0
     lax.fori_loop(0,chunks,pack,0)
-    out=pltpu.make_async_copy(w,gw_ref,w_sem)
-    out.start()
-    pltpu.make_async_copy(ch_s.at[me],chosen_ref.at[me],loc_sem.at[0]).wait()
-    pltpu.make_async_copy(gs_s.at[me],back_ref.at[me],loc_sem.at[1]).wait()
+    own_ch.wait()
+    own_back.wait()
+    block=flip(me//per,tiles-1,tiles)
+    at=pl.ds(pl.multiple_of(block*per,per),per)
+    pltpu.make_async_copy(gs_s.at[at],late_ref,loc_sem.at[2]).wait()
     def settle(o,_):
         peer=flip(me,o,n)
         gate_copy(peer).wait_send()
         row_copy(peer).wait_send()
         ch_copy(peer).wait_send()
-        back_copy(peer).wait_send()
         ch_in(peer).wait_recv()
-        back_in(peer).wait_recv()
+        @pl.when(o<last)
+        def _():
+            back_copy(peer).wait_send()
+            back_in(peer).wait_recv()
         return 0
     lax.fori_loop(1,n,settle,0)
     def stored(t,_):
-        block=flip(me//per,t,n//per)
+        block=flip(me//per,t,tiles)
         at=pl.ds(pl.multiple_of(block*per,per),per)
         pltpu.make_async_copy(ret_s.at[at],ret_ref.at[at],ret_sem.at[t]).wait()
         return 0
-    lax.fori_loop(0,n//per,stored,0)
-    out.wait()
-
-def moe(send_rows,gate_slots,cot,scale,weights,collective_id=1):
+    lax.fori_loop(0,tiles,stored,0)
+    pltpu.make_async_copy(w,gw_ref,w_sem).wait()
+
+def late_kernel(n,gs_ref,out_ref,send_sem,recv_sem):
+    per=gs_ref.shape[0]
+    tiles=n//per
+    me=lax.axis_index("expert")
+    block=flip(me//per,tiles-1,tiles)
+    barrier=pltpu.get_barrier_semaphore()
+    def greet(j,_):
+        pl.semaphore_signal(barrier,inc=1,device_id={"expert":block*per+j},device_id_type=MESH)
+        return 0
+    lax.fori_loop(0,per,greet,0)
+    pl.semaphore_wait(barrier,per)
+    def copy(j):
+        k=flip(j,me%per,per)
+        return pltpu.make_async_remote_copy(src_ref=gs_ref.at[j],dst_ref=out_ref.at[k],send_sem=send_sem.at[k],recv_sem=recv_sem.at[k],
+            device_id={"expert":block*per+j},device_id_type=MESH)
+    def go(j,_):
+        copy(j).start()
+        return 0
+    lax.fori_loop(0,per,go,0)
+    def end(j,_):
+        copy(j).wait()
+        return 0
+    lax.fori_loop(0,per,end,0)
+
+def moe(send_rows,gate_slots,cot,scale,weights):
     n,cap,D=send_rows.shape
     chunks,_,_,FC=weights.shape
+    per=TILE//cap
     any_=pl.BlockSpec(memory_space=pl.ANY)
     bf=jnp.bfloat16; f32=jnp.float32
     dma=pltpu.SemaphoreType.DMA
     flops=6*2*n*cap*D*chunks*FC
-    return pl.pallas_call(partial(moe_kernel,n,cap),
-        out_shape=[jax.ShapeDtypeStruct((n,cap,D),bf),jax.ShapeDtypeStruct((n,8,TILE),f32),
+    back,late,chosen,ret,gw=pl.pallas_call(partial(moe_kernel,n,cap),
+        out_shape=[jax.ShapeDtypeStruct((n-per,cap,D),bf),jax.ShapeDtypeStruct((per,cap,D),bf),jax.ShapeDtypeStruct((n,8,TILE),f32),
                    jax.ShapeDtypeStruct((n,cap,D),bf),jax.ShapeDtypeStruct(weights.shape,bf)],
         in_specs=[any_,any_,any_,pl.BlockSpec(memory_space=pltpu.VMEM),any_],
-        out_specs=[any_]*4,
+        out_specs=[any_]*5,
         scratch_shapes=[pltpu.VMEM((n,cap,D),bf),pltpu.VMEM((n,8,TILE),f32),pltpu.VMEM((n*cap,D),bf),
             pltpu.VMEM(weights.shape,bf),pltpu.VMEM(weights.shape,f32),pltpu.VMEM((n,cap,D),bf),pltpu.VMEM((n,cap,D),bf),
             pltpu.VMEM((n,8,TILE),f32),pltpu.VMEM((TILE,D),bf),pltpu.VMEM((TILE,D),f32),pltpu.VMEM((TILE,D),f32)]
-            +[dma((n,))]*8+[dma(()),dma((3,)),dma((n*cap//TILE,))],
-        compiler_params=pltpu.CompilerParams(vmem_limit_bytes=62*2**20,collective_id=collective_id,has_side_effects=True),
+            +[dma((n,))]*8+[dma(()),dma((3,)),dma((n//per,))],
+        compiler_params=pltpu.CompilerParams(vmem_limit_bytes=62*2**20,collective_id=1,has_side_effects=True),
         cost_estimate=pl.CostEstimate(flops=flops,bytes_accessed=40*2**20,transcendentals=0),
     )(send_rows,gate_slots,cot,scale,weights)
+    late=pl.pallas_call(partial(late_kernel,n),
+        out_shape=jax.ShapeDtypeStruct((per,cap,D),bf),in_specs=[any_],out_specs=any_,
+        scratch_shapes=[dma((per,)),dma((per,))],
+        compiler_params=pltpu.CompilerParams(collective_id=5,has_side_effects=True),
+        cost_estimate=pl.CostEstimate(flops=0,bytes_accessed=100*2**20,transcendentals=0),
+    )(late)
+    return back,late,chosen,ret,gw
+
+
+def near(dps,pairs):
+    d=lax.axis_index("dp"); me=lax.axis_index("expert")
+    core=me%2; pair=me//2
+    partner={"expert":me+1-2*core}
+    over=[((d+k)%dps,{"dp":(d+k)%dps}) for k in range(1,dps)]
+    along=[((pair+k)%pairs,{"expert":2*((pair+k)%pairs)+core}) for k in range(1,pairs)]
+    return d,pair,core,partner,over,along
+
+def greet_all(devices):
+    barrier=pltpu.get_barrier_semaphore()
+    for dev in devices:
+        pl.semaphore_signal(barrier,inc=1,device_id=dev,device_id_type=MESH)
+    pl.semaphore_wait(barrier,len(devices))
+
+def remote(src,dst,send,recv,dev):
+    return pltpu.make_async_remote_copy(src_ref=src,dst_ref=dst,send_sem=send,recv_sem=recv,device_id=dev,device_id_type=MESH)
+
+def gather_kernel(dps,pairs,w_ref,v_ref,out_ref,vout_ref,both,blk,vboth,vblk,
+                  s1,r1,loc,us,ur,ls,lr,vzs,vzr,ds_,dr,vds,vdr,ps,pr):
+    r=w_ref.shape[1]; R=2*r
+    d,pair,core,partner,over,along=near(dps,pairs)
+    greet_all([partner]+[x[1] for x in over]+[x[1] for x in along])
+    mine=pl.ds(pl.multiple_of(core*r,8),r)
+    lanes=pl.ds(pl.multiple_of(core*128,128),128)
+    half=pl.ds(core*2,2); rest=pl.ds(2-core*2,2)
+    def rows(dd,q): return pl.ds(pl.multiple_of((dd*pairs+q)*R,16),R)
+    c1=[remote(w_ref,both.at[:,mine,:],s1.at[0],r1.at[0],partner),
+        remote(v_ref,vboth.at[:,lanes],s1.at[1],r1.at[1],partner)]
+    for c in c1: c.start()
+    both[:,mine,:]=w_ref[...]
+    vboth[:,lanes]=v_ref[...]
+    for c in c1: c.wait()
+    blk[...]=both[...].astype(jnp.bfloat16)
+    vblk[...]=vboth[...].astype(jnp.bfloat16)
+    own=[pltpu.make_async_copy(blk,out_ref.at[:,rows(d,pair),:],loc.at[0]),
+         pltpu.make_async_copy(vblk,vout_ref.at[d,pair],loc.at[1])]
+    for c in own: c.start()
+    above={"expert":2*lax.rem(pair+1,pairs)+core}; below={"expert":2*lax.rem(pair+pairs-1,pairs)+core}
+    has_above=pair<pairs-1; has_below=pair>0
+    def up(dd,q,src=None):
+        here=out_ref.at[half,rows(dd,q),:]
+        return remote(here if src is None else src,here,us.at[dd,q],ur.at[dd,q],above)
+    def down(dd,q,src=None):
+        here=out_ref.at[half,rows(dd,q),:]
+        return remote(here if src is None else src,here,ls.at[dd,q],lr.at[dd,q],below)
+    def hand(dd,q):
+        here=out_ref.at[half,rows(dd,q),:]
+        return remote(here,here,ps.at[dd,q],pr.at[dd,q],partner)
+    def over_copy(dd,dev):
+        here=out_ref.at[half,rows(d,pair),:]
+        return remote(blk.at[half],here,ds_.at[dd],dr.at[d],dev)
+    def over_in(dd,dev):
+        here=out_ref.at[half,rows(dd,pair),:]
+        return remote(here,here,ds_.at[dd],dr.at[dd],dev)
+    def v_over(dd,dev): return remote(vblk,vout_ref.at[d,pair],vds.at[dd],vdr.at[d],dev)
+    def v_along(q,dev): return remote(vout_ref.at[:,pair],vout_ref.at[:,pair],vzs.at[q],vzr.at[pair],dev)
+    for dd,dev in over:
+        over_copy(dd,dev).start()
+        v_over(dd,dev).start()
+    mine_out=blk.at[half]
+    @pl.when(has_above)
+    def _(): up(d,pair,mine_out).start()
+    @pl.when(has_below)
+    def _(): down(d,pair,mine_out).start()
+    for dd,dev in over:
+        over_in(dd,dev).wait_recv()
+        @pl.when(has_above)
+        def _(): up(dd,pair).start()
+        @pl.when(has_below)
+        def _(): down(dd,pair).start()
+        hand(dd,pair).start()
+    for dd,dev in over:
+        remote(vblk,vout_ref.at[dd,pair],vds.at[dd],vdr.at[dd],dev).wait_recv()
+    own[1].wait()
+    for q,dev in along: v_along(q,dev).start()
+    groups=[d]+[x[0] for x in over]
+    for k in range(1,pairs):
+        for dd in groups:
+            @pl.when(pair>=k)
+            def _():
+                up(dd,pair-k).wait_recv()
+                @pl.when(has_above)
+                def _(): up(dd,pair-k).start()
+                hand(dd,pair-k).start()
+            @pl.when(pair+k<pairs)
+            def _():
+                down(dd,pair+k).wait_recv()
+                @pl.when(has_below)
+                def _(): down(dd,pair+k).start()
+                hand(dd,pair+k).start()
+    for q,dev in along:
+        remote(vout_ref.at[:,q],vout_ref.at[:,q],vzs.at[q],vzr.at[q],dev).wait_recv()
+    def from_partner(dd,q):
+        there=out_ref.at[rest,rows(dd,q),:]
+        remote(there,there,ps.at[dd,q],pr.at[dd,q],partner).wait_recv()
+    for dd,dev in over: from_partner(dd,pair)
+    for q,_ in along:
+        for dd in groups: from_partner(dd,q)
+    for dd,dev in over:
+        over_copy(dd,dev).wait_send(); v_over(dd,dev).wait_send(); hand(dd,pair).wait_send()
+    for q,dev in along:
+        v_along(q,dev).wait_send()
+        for dd in groups: hand(dd,q).wait_send()
+    for dd in groups:
+        for k in range(pairs):
+            @pl.when((pair>=k)&has_above)
+            def _(): up(dd,pair-k).wait_send()
+            @pl.when((pair+k<pairs)&has_below)
+            def _(): down(dd,pair+k).wait_send()
+    own[0].wait()
+
+def gather_dense(weights,vectors,dps,n,collective_id=2):
+    pairs=n//2
+    m,r,D=weights.shape
+    V=jnp.zeros((16,128),jnp.float32).at[:vectors.shape[0],:r].set(vectors)
+    dma=pltpu.SemaphoreType.DMA
+    f32=jnp.float32; bf=jnp.bfloat16
+    out,vout=pl.pallas_call(partial(gather_kernel,dps,pairs),
+        out_shape=[jax.ShapeDtypeStruct((m,r*n*dps,D),bf),jax.ShapeDtypeStruct((dps,pairs,16,256),bf)],
+        in_specs=[pl.BlockSpec(memory_space=pltpu.VMEM)]*2,
+        out_specs=[pl.BlockSpec(memory_space=pl.ANY)]*2,
+        scratch_shapes=[pltpu.VMEM((m,2*r,D),f32),pltpu.VMEM((m,2*r,D),bf),pltpu.VMEM((16,256),f32),pltpu.VMEM((16,256),bf),
+            dma((2,)),dma((2,)),dma((2,)),dma((dps,pairs)),dma((dps,pairs)),dma((dps,pairs)),dma((dps,pairs)),dma((pairs,)),dma((pairs,)),
+            dma((dps,)),dma((dps,)),dma((dps,)),dma((dps,)),dma((dps,pairs)),dma((dps,pairs))],
+        compiler_params=pltpu.CompilerParams(vmem_limit_bytes=16*2**20,collective_id=collective_id,has_side_effects=True),
+        cost_estimate=pl.CostEstimate(flops=0,bytes_accessed=100*2**20,transcendentals=0),
+    )(weights,V)
+    k=vectors.shape[0]
+    vec=vout[:,:,:k].reshape(dps,pairs,k,2,128)[...,:r]
+    vec=jnp.transpose(vec,(2,0,1,3,4)).reshape(k,r*n*dps)
+    return out,vec
+
+def tail_kernel(dps, pairs, cap, q_ref, k_ref, v_ref, lse_ref, g_ref, dcol_ref, drow_ref, gain_ref,
+                x_ref, mixed_ref, ga_ref, prod_ref, w_ref, gh_ref, in_ref,
+                out_ref, gain_out, returned_ref, dx_ref,
+                bias_ref, dk_ref, dv_ref, left, right, got, own, total, in2, tb, in3, u, in4, w, gh, xin,
+                ls, s1, r1, s2, r2, s3, r3, s4, r4, rs, rr, own_sem, dx_sem):
+    h = pl.program_id(0)
+    n = 2 * pairs
+    me = lax.axis_index("expert")
+    d, pair, core, partner, over, along = near(dps, pairs)
+    rows = out_ref.shape[1]
+    R = 2 * rows
+    T, D = x_ref.shape
+    loads = [
+        pltpu.make_async_copy(x_ref, left.at[0], ls.at[0]),
+        pltpu.make_async_copy(mixed_ref, left.at[1], ls.at[1]),
+        pltpu.make_async_copy(ga_ref, right.at[3], ls.at[2]),
+        pltpu.make_async_copy(w_ref.at[pl.ds(0, 3)], w, ls.at[3]),
+        pltpu.make_async_copy(gh_ref, gh, ls.at[4]),
+        pltpu.make_async_copy(in_ref, xin, ls.at[5]),
+    ]
+
+    def product(m):
+        return lax.dot_general(left[m // 3], right[m], TN, preferred_element_type=jnp.float32)
+
+    def ret_copy(peer):
+        return remote(prod_ref.at[peer], returned_ref.at[me], rs.at[peer], rr.at[me], {"expert": peer})
+
+    def ret_in(peer):
+        return remote(prod_ref.at[peer], returned_ref.at[peer], rs.at[peer], rr.at[peer], {"expert": peer})
+
+    own_ret = pltpu.make_async_copy(prod_ref.at[me], returned_ref.at[me], own_sem)
+
+    def to_partner(i):
+        return remote(total.at[i], got.at[i], s1.at[i], r1.at[i], partner)
+
+    @pl.when(h == 0)
+    def _():
+        for c in loads:
+            c.start()
+        barrier = pltpu.get_barrier_semaphore()
+
+        def greet(o, _):
+            pl.semaphore_signal(barrier, inc=1, device_id={"expert": flip(me, o, n)}, device_id_type=MESH)
+            return 0
+
+        lax.fori_loop(1, n, greet, 0)
+        for _, dev in over:
+            pl.semaphore_signal(barrier, inc=1, device_id=dev, device_id_type=MESH)
+        pl.semaphore_wait(barrier, n - 1 + dps - 1)
+
+        def send(i, _):
+            ret_copy(flip(me, n - 1 - i, n)).start()
+            return 0
+
+        lax.fori_loop(0, n - 1, send, 0)
+        own_ret.start()
+        transposed_bias(bias_ref, dcol_ref, drow_ref, QB)
+        for c in loads[:3]:
+            c.wait()
+        out = product(3)
+
+        @pl.when(core == 0)
+        def _():
+            total[1] = out.astype(jnp.bfloat16)
+            to_partner(1).start()
+
+        @pl.when(core == 1)
+        def _():
+            own[1] = out
+
+    lanes = pl.ds(pl.multiple_of(h * 128, 128), 128)
+    dq_at = lambda r, value: right.__setitem__((0, r, lanes), value)
+    head_pair_backward(QB, q_ref, k_ref, v_ref, lse_ref, g_ref, bias_ref, dk_ref, dv_ref, dq_at)
+    right[1, :, lanes] = dk_ref[...].astype(jnp.bfloat16)
+    right[2, :, lanes] = dv_ref[...].astype(jnp.bfloat16)
+
+    @pl.when(h == pl.num_programs(0) - 1)
+    def _():
+        @pl.when(core == 0)
+        def _():
+            total[0] = product(2).astype(jnp.bfloat16)
+            to_partner(0).start()
+            own[0] = product(0)
+            own[1] = product(1)
+
+        @pl.when(core == 1)
+        def _():
+            total[0] = product(0).astype(jnp.bfloat16)
+            to_partner(0).start()
+            total[1] = product(1).astype(jnp.bfloat16)
+            to_partner(1).start()
+            own[0] = product(2)
+
+        for i in range(2):
+            to_partner(i).wait_send()
+            to_partner(i).wait_recv()
+            total[i] = (own[i] + got[i].astype(jnp.float32)).astype(jnp.bfloat16)
+
+        order = along + [(pair, None)]
+
+        def piece(dd, q):
+            return pl.ds(pl.multiple_of((dd * pairs + q) * R, 16), R)
+
+        c2 = []
+        for q, _ in order:
+            for dd, dev in over:
+                c = remote(total.at[:, piece(dd, q), :], in2.at[d, q], s2.at[dd, q], r2.at[d, q], dev)
+                c.start()
+                c2.append(c)
+        for c in loads[3:]:
+            c.wait()
+        gain = gain_ref[...]
+        gain_sum = jnp.zeros((8, D), jnp.float32)
+        for b in range(T // 256):
+            at = pl.ds(b * 256, 256)
+            gn = sum(
+                lax.dot_general(right[c, at, :], w[c], NT, preferred_element_type=jnp.float32)
+                for c in range(3)
+            )
+            x = xin[at, :].astype(jnp.float32)
+            center = x - jnp.mean(x, axis=-1, keepdims=True)
+            scale = lax.rsqrt(jnp.mean(center * center, axis=-1, keepdims=True) + norm_eps)
+            unit = center * scale
+            gain_sum = gain_sum + jnp.sum((gn * unit).reshape(32, 8, D), axis=0)
+            gu = gn * gain
+            gx = scale * (
+                gu
+                - jnp.mean(gu, axis=-1, keepdims=True)
+                - unit * jnp.mean(gu * unit, axis=-1, keepdims=True)
+            )
+            gh[at, :] = gh[at, :] + gx
+        gain_out[...] = gain_sum
+        dx = pltpu.make_async_copy(gh, dx_ref, dx_sem)
+        dx.start()
+        c3 = []
+        for q, zdev in order:
+            acc = total[:, piece(d, q), :].astype(jnp.float32)
+            for dd, dev in over:
+                remote(in2.at[dd, q], in2.at[dd, q], s2.at[dd, q], r2.at[dd, q], dev).wait_recv()
+                acc = acc + in2[dd, q].astype(jnp.float32)
+            if zdev is None:
+                u[...] = acc
+            else:
+                tb[q] = acc.astype(jnp.bfloat16)
+                c = remote(tb.at[q], in3.at[pair], s3.at[q], r3.at[pair], zdev)
+                c.start()
+                c3.append(c)
+        acc = u[...]
+        for q, dev in along:
+            remote(in3.at[q], in3.at[q], s3.at[q], r3.at[q], dev).wait_recv()
+            acc = acc + in3[q].astype(jnp.float32)
+        u[...] = acc
+        theirs = pl.ds(pl.multiple_of((1 - core) * rows, 8), rows)
+        mine = pl.ds(pl.multiple_of(core * rows, 8), rows)
+        c4 = remote(u.at[:, theirs, :], in4, s4, r4, partner)
+        c4.start()
+        out_ref[pl.ds(2 * core, 2)] = u[:, mine, :]
+        c4.wait_recv()
+        out_ref[pl.ds(2 - 2 * core, 2)] = in4[...]
+        for c in c2 + c3 + [c4]:
+            c.wait_send()
+
+        def settle(o, _):
+            peer = flip(me, o, n)
+            ret_copy(peer).wait_send()
+            ret_in(peer).wait_recv()
+            return 0
+
+        lax.fori_loop(1, n, settle, 0)
+        own_ret.wait()
+        dx.wait()
+
+
+def tail(projected, lse, grad_mixed, documents, gain, normed, mixed, grad_attn, produced, dense_low,
+         grad_hidden, inputs, dps, n):
+    pairs = n // 2
+    _, T, D = projected.shape
+    rows = D // (dps * n)
+    R = 2 * rows
+    cap = produced.shape[1]
+    f32, bf = jnp.float32, jnp.bfloat16
+    dma = pltpu.SemaphoreType.DMA
+    any_ = pl.BlockSpec(memory_space=pl.ANY)
+
+    def sp(c):
+        return pl.BlockSpec((1, T, 128), lambda h, c=c: (c, 0, h))
+
+    fixed = lambda shape: pl.BlockSpec(shape, lambda h: (0,) * len(shape))
+    return pl.pallas_call(
+        partial(tail_kernel, dps, pairs, cap),
+        grid=(D // 128,),
+        out_shape=[
+            jax.ShapeDtypeStruct((4, rows, D), f32),
+            jax.ShapeDtypeStruct((8, D), f32),
+            jax.ShapeDtypeStruct(produced.shape, bf),
+            jax.ShapeDtypeStruct((T, D), f32),
+        ],
+        in_specs=[sp(0), sp(1), sp(2), pl.BlockSpec((1, T, 128), lambda h: (h, 0, 0)),
+                  pl.BlockSpec((T, 128), lambda h: (0, h)), fixed((T, 1)), fixed((1, T)), fixed((1, D))]
+        + [any_] * 7,
+        out_specs=[fixed((4, rows, D)), fixed((8, D)), any_, any_],
+        scratch_shapes=[
+            pltpu.VMEM((min(T, WINDOW + QB), T), f32),
+            pltpu.VMEM((T, 128), f32),
+            pltpu.VMEM((T, 128), f32),
+            pltpu.VMEM((2, T, D), bf),
+            pltpu.VMEM((4, T, D), bf),
+            pltpu.VMEM((2, D, D), bf),
+            pltpu.VMEM((2, D, D), f32),
+            pltpu.VMEM((2, D, D), bf),
+            pltpu.VMEM((dps, pairs, 2, R, D), bf),
+            pltpu.VMEM((pairs, 2, R, D), bf),
+            pltpu.VMEM((pairs, 2, R, D), bf),
+            pltpu.VMEM((2, R, D), f32),
+            pltpu.VMEM((2, rows, D), f32),
+            pltpu.VMEM((3, D, D), bf),
+            pltpu.VMEM((T, D), f32),
+            pltpu.VMEM((T, D), bf),
+            dma((6,)), dma((2,)), dma((2,)), dma((dps, pairs)), dma((dps, pairs)), dma((pairs,)), dma((pairs,)),
+            dma(()), dma(()), dma((n,)), dma((n,)), dma(()), dma(()),
+        ],
+        compiler_params=pltpu.CompilerParams(
+            vmem_limit_bytes=56 * 2**20, collective_id=3, has_side_effects=True
+        ),
+        cost_estimate=pl.CostEstimate(flops=30 * T * D * D, bytes_accessed=100 * 2**20, transcendentals=0),
+    )(projected, projected, projected, lse, grad_mixed, documents.reshape(T, 1), documents.reshape(1, T), gain,
+      normed, mixed, grad_attn, produced, dense_low, grad_hidden, inputs)
+
+
+def norm_kernel(dps, pairs, d_ref, v_ref, e_ref, out_ref, a, b, c, s1, r1, s2, r2, s3, r3):
+    d, pair, core, partner, over, along = near(dps, pairs)
+    greet_all([partner] + [x[1] for x in over] + [x[1] for x in along])
+
+    def squares(ref):
+        x = ref[...].astype(jnp.float32)
+        return jnp.sum(x * x)
+
+    part = squares(d_ref)
+    for i in range(e_ref.shape[0]):
+        part = part + squares(e_ref.at[i])
+    last = lax.broadcasted_iota(jnp.int32, v_ref.shape, 0) == v_ref.shape[0] - 1
+    a[core] = jnp.where(last, part, v_ref[...])
+    cs = [remote(a.at[core], a.at[core], s1, r1.at[core], partner)]
+    cs[0].start()
+    remote(a.at[1 - core], a.at[1 - core], s1, r1.at[1 - core], partner).wait_recv()
+    b[d] = a[0] + a[1]
+    for dd, dev in over:
+        x = remote(b.at[d], b.at[d], s2.at[dd], r2.at[d], dev)
+        x.start()
+        cs.append(x)
+    for dd, dev in over:
+        remote(b.at[dd], b.at[dd], s2.at[dd], r2.at[dd], dev).wait_recv()
+    c[pair] = sum(b[k] for k in range(dps))
+    for q, dev in along:
+        x = remote(c.at[pair], c.at[pair], s3.at[q], r3.at[pair], dev)
+        x.start()
+        cs.append(x)
+    for q, dev in along:
+        remote(c.at[q], c.at[q], s3.at[q], r3.at[q], dev).wait_recv()
+    out_ref[...] = sum(c[k] for k in range(pairs))
+    for x in cs:
+        x.wait_send()
+
+
+def norm_squares(dense, vec, expert, dps, n):
+    pairs = n // 2
+    k, D = vec.shape
+    R = (k // 8 + 1) * 8
+    dma = pltpu.SemaphoreType.DMA
+    vm = pl.BlockSpec(memory_space=pltpu.VMEM)
+    out = pl.pallas_call(
+        partial(norm_kernel, dps, pairs),
+        out_shape=jax.ShapeDtypeStruct((R, D), jnp.float32),
+        in_specs=[vm] * 3,
+        out_specs=vm,
+        scratch_shapes=[
+            pltpu.VMEM((2, R, D), jnp.float32),
+            pltpu.VMEM((dps, R, D), jnp.float32),
+            pltpu.VMEM((pairs, R, D), jnp.float32),
+            dma(()), dma((2,)), dma((dps,)), dma((dps,)), dma((pairs,)), dma((pairs,)),
+        ],
+        compiler_params=pltpu.CompilerParams(
+            vmem_limit_bytes=24 * 2**20, collective_id=4, has_side_effects=True
+        ),
+    )(dense, jnp.pad(vec, ((0, R - k), (0, 0))), expert)
+    total = out[:k]
+    dev = lax.axis_index("dp") * n + lax.axis_index("expert")
+    width = D // (dps * n)
+    return lax.dynamic_slice_in_dim(total, dev * width, width, axis=1), out[R - 1, 0] + jnp.sum(total * total)
 
 
 def adam_update(weight, gradient, first_moment, second_moment, average, factor, rate):
@@ -338,10 +826,15 @@
     owners = lax.axis_size("expert")
     groups = lax.axis_size(("dp", "expert"))
     sequences = tokens // LEN
-    dense_low, vector_low = (
-        lax.all_gather(dense_weights.astype(jnp.bfloat16), ("dp", "expert"), axis=1, tiled=True),
-        lax.all_gather(vector_params.astype(jnp.bfloat16), ("dp", "expert"), axis=1, tiled=True),
-    )
+    splits = lax.axis_size("dp")
+    own_rows = dense_weights.shape[1]
+    if own_rows % 8 == 0:
+        dense_low, vector_low = gather_dense(dense_weights, vector_params, splits, owners)
+    else:
+        dense_low, vector_low = (
+            lax.all_gather(dense_weights.astype(jnp.bfloat16), ("dp", "expert"), axis=1, tiled=True),
+            lax.all_gather(vector_params.astype(jnp.bfloat16), ("dp", "expert"), axis=1, tiled=True),
+        )
     me = lax.axis_index("expert")
     seq_index = lax.axis_index("dp") * owners + jnp.arange(owners)
     bounds = jnp.cumsum(domain_counts)
@@ -377,8 +870,9 @@
             slot_pick, rows.reshape(-1, model_width), preferred_element_type=jnp.float32
         )
 
+    later_cot, dense_low = lax.optimization_barrier((cotangent, dense_low))
     cot_received = lax.all_to_all(
-        to_slots(cotangent), "expert", split_axis=0, concat_axis=0, tiled=True
+        to_slots(later_cot), "expert", split_axis=0, concat_axis=0, tiled=True
     ).reshape(-1, model_width)
     own_low = expert_weights[0].astype(jnp.bfloat16)
     expert_low = lax.all_gather(own_low, "dp", axis=0)
@@ -407,19 +901,25 @@
     gate_tiles = jnp.broadcast_to(
         gate_slots * lane_part[None, None, :, None], (experts_total, 8, per, capacity)
     ).reshape(experts_total, 8, TILE)
-    grad_back, chosen_tiles, produced_low, grad_expert = moe(
+    back_rows, late_rows, chosen_tiles, produced_low, grad_expert = moe(
         send_rows, gate_tiles, cot_received, slot_scale, expert_low
     )
-    expert_grad = lax.psum_scatter(grad_expert, "dp", scatter_dimension=0).astype(jnp.float32)[None]
-    returned = lax.all_to_all(produced_low, "expert", split_axis=0, concat_axis=0, tiled=True)
-    returned_rows = from_slots(returned)
-    block_output = hidden_state + gate_value[:, None] * returned_rows
+    expert_low_grad = lax.psum_scatter(grad_expert, "dp", scatter_dimension=0)
+    expert_grad = expert_low_grad.astype(jnp.float32)[None]
     grad_out = cotangent.astype(jnp.float32) * token_scale[:, None]
-    grad_sent_rows = from_slots(grad_back)
+    back_slot = (token_slot // capacity ^ me) * capacity + token_slot % capacity
+    back_match = back_slot[:, None] == jnp.arange(experts_total * capacity)[None, :]
+    back_pick = back_match.astype(jnp.bfloat16)
+    early = back_rows.shape[0] * capacity
+    grad_sent_rows = jnp.dot(
+        back_pick[:, :early], back_rows.reshape(-1, model_width), preferred_element_type=jnp.float32
+    ) + jnp.dot(
+        back_pick[:, early:], late_rows.reshape(-1, model_width), preferred_element_type=jnp.float32
+    )
     chosen_slots = lax.dynamic_slice_in_dim(
         chosen_tiles[:, 0, :], me % per * capacity, capacity, axis=1
     )
-    grad_chosen = jnp.sum(jnp.where(slot_match, chosen_slots.reshape(1, -1), 0.0), axis=1)
+    grad_chosen = jnp.sum(jnp.where(back_match, chosen_slots.reshape(1, -1), 0.0), axis=1)
     chosen_grad = grad_chosen[:, None] * expert_pick
     grad_normed_two = grad_sent_rows + jnp.dot(
         chosen_grad, centroids, precision=lax.Precision.HIGHEST
@@ -428,33 +928,40 @@
     grad_hidden_norm, grad_gain_two = norm_two_back(grad_normed_two)
     grad_hidden = grad_out + grad_hidden_norm
     grad_attn = grad_hidden.astype(jnp.bfloat16)
-    grad_out_proj = jnp.dot(mixed_low.T, grad_attn, preferred_element_type=jnp.float32)
     grad_mixed = jnp.dot(grad_attn, dense_low[3].T, preferred_element_type=jnp.float32).astype(
         jnp.bfloat16
     )
-    grad_proj = attend_backward(projected, documents, totals, grad_mixed)
-    grad_in_proj = jnp.einsum(
-        "td,cte->cde", normed_low, grad_proj, preferred_element_type=jnp.float32
-    )
-    grad_normed_one = jnp.einsum(
-        "cte,cde->td", grad_proj, dense_low[:3], preferred_element_type=jnp.float32
-    )
-    grad_input_norm, grad_gain_one = norm_one_back(grad_normed_one)
-    input_grad = grad_hidden + grad_input_norm
-    dense_grad = jnp.concatenate([grad_in_proj, grad_out_proj[None]], axis=0)
+    if own_rows % 8 == 0:
+        dense_grad, gain_tiles, returned, input_grad = tail(
+            projected, totals, grad_mixed, documents, vector_low[0:1].astype(jnp.float32), normed_low,
+            mixed_low, grad_attn, produced_low, dense_low, grad_hidden, inputs, splits, owners
+        )
+        grad_gain_one = jnp.sum(gain_tiles, axis=0)
+    else:
+        returned = lax.all_to_all(produced_low, "expert", split_axis=0, concat_axis=0, tiled=True)
+        grad_proj = attend_backward(projected, documents, totals, grad_mixed)
+        grad_normed_one = jnp.einsum(
+            "cte,cde->td", grad_proj, dense_low[:3], preferred_element_type=jnp.float32
+        )
+        grad_input_norm, grad_gain_one = norm_one_back(grad_normed_one)
+        input_grad = grad_hidden + grad_input_norm
+        grad_in_proj = jnp.einsum(
+            "td,cte->cde", normed_low, grad_proj, preferred_element_type=jnp.float32
+        )
+        grad_out_proj = jnp.dot(mixed_low.T, grad_attn, preferred_element_type=jnp.float32)
+        dense_grad = lax.psum_scatter(
+            jnp.concatenate([grad_in_proj, grad_out_proj[None]], axis=0),
+            ("dp", "expert"),
+            scatter_dimension=1,
+            tiled=True,
+        )
+    returned_rows = from_slots(returned)
+    block_output = hidden_state + gate_value[:, None] * returned_rows
     vector_grad = jnp.concatenate(
         [grad_gain_one[None], grad_gain_two[None], grad_centroids], axis=0
     )
-    dense_grad, vector_grad = (
-        lax.psum_scatter(dense_grad, ("dp", "expert"), scatter_dimension=1, tiled=True),
-        lax.psum_scatter(vector_grad, ("dp", "expert"), scatter_dimension=1, tiled=True),
-    )
-    squares = (
-        jnp.sum(dense_grad * dense_grad)
-        + jnp.sum(vector_grad * vector_grad)
-        + jnp.sum(expert_grad * expert_grad)
-    )
-    grad_norm = jnp.sqrt(lax.psum(squares, ("dp", "expert")))
+    vector_grad, squares = norm_squares(dense_grad, vector_grad, expert_low_grad, splits, owners)
+    grad_norm = jnp.sqrt(squares)
     factor = jnp.minimum(1.0, clip_norm / (grad_norm + 1e-06))
     dense_new = adam_update(
         dense_weights, dense_grad, dense_first, dense_second, dense_average, factor, dense_rate

time: 867 us -> 473 us (0.55)
  blocking collectives: 263 us -> 0 us
  waiting for transfers between devices: 226 us -> 26 us
  Pallas kernels: 181 us -> 326 us
  starting transfers between devices: 28.7 us -> 4.82 us
  local copies, waits for them, and re-layouts: 29.9 us -> 12.6 us
  matrix products: 64.2 us -> 48.3 us
  other arithmetic: 48.2 us -> 34 us
    unnamed x6 -> x3, waiting for transfers between devices: 216 us -> 0.03 us
    pallas_call x1 -> x4, Pallas kernels: 26.6 us -> 195 us  [the longest x1 103 us: tail(): pl.pallas_call(partial(tail_kernel, dps, pairs, cap), grid=(D // 128,), o...]
    all_gather x1 -> x0, blocking collectives: 118 us -> none  [shards(): lax.all_gather(vector_params.astype(jnp.bfloat16), ('dp', 'expert'), axis...]
    unnamed x1 -> x0, blocking collectives: 105 us -> none
    psum x1 -> x0, blocking collectives: 39.3 us -> none  [shards(): grad_norm = jnp.sqrt(lax.psum(squares, ('dp', 'expert')))]
    all_to_all x2 -> x1, waiting for transfers between devices: 0.01 us -> 25.9 us  [shards(): lax.all_to_all(to_slots(later_cot), 'expert', split_axis=0, concat_axis=0...]
    all_to_all x2 -> x1, starting transfers between devices: 28.6 us -> 4.57 us  [shards(): lax.all_to_all(to_slots(later_cot), 'expert', split_axis=0, concat_axis=0...]
    pallas_call x1, Pallas kernels: 136 us -> 112 us  [moe(): pl.pallas_call(partial(moe_kernel, n, cap), out_shape=[jax.ShapeDtypeStru...]
  transfers between devices with their start and end apart: 6 -> 3, of which waited for: 3 -> 1; matrix products, arithmetic and copies ran while one was open for 9% -> 14% of each run, Pallas kernels for 2% -> 42%
where the time goes in v4:
time: 473 us; the launch traced here: 469 us
  Pallas kernels  326 us (69%)
  matrix products  48.3 us (10%)
  other arithmetic  34 us (7%)
  waiting for transfers between devices  26 us (5%)
  between operations  17.5 us (4%)
  local copies, waits for them, and re-layouts  12.6 us (3%)
  starting transfers between devices  4.82 us (1%)
    pallas_call x1, Pallas kernels, moe(): pl.pallas_call(partial(moe_kernel, n, cap), out_shape=[jax.ShapeDtypeStru...  112 us
    pallas_call x1, Pallas kernels, tail(): pl.pallas_call(partial(tail_kernel, dps, pairs, cap), grid=(D // 128,), o...  103 us
    pallas_call x1, Pallas kernels, gather_dense(): pl.pallas_call(partial(gather_kernel, dps, pairs), out_shape=[jax.ShapeDt...  55.9 us
    all_to_all x1, waiting for transfers between devices, shards(): lax.all_to_all(to_slots(later_cot), 'expert', split_axis=0, concat_axis=0...  25.9 us
    pallas_call x1, Pallas kernels, moe(): pl.pallas_call(partial(late_kernel, n), out_shape=jax.ShapeDtypeStruct((p...  19.6 us
    pallas_call x1, Pallas kernels, attend_forward(): pl.pallas_call(partial(fwd_kernel, QB), grid=(D // 128,), in_specs=[sp(0)...  18.2 us
    add x3, other arithmetic, adam_update(): average_new = ema_keep * average + (1.0 - ema_keep) * updated  16.4 us
    pallas_call x1, Pallas kernels, norm_squares(): pl.pallas_call(partial(norm_kernel, dps, pairs), out_shape=jax.ShapeDtype...  16.1 us
  transfers between devices with their start and end apart: 3, of which 1 were waited for; matrix products, arithmetic and copies ran while one was open for 14% of the time, Pallas kernels for 42%

profile of v4, /device:TPU:0, one launch (start us, length us, event | category | flops | bytes accessed | tf_op | source)
XLA Modules:
  0.0 468.9 jit_solution(7023037306194733161)
XLA Ops:
  7.3 4.1 convert_element_type.108
  11.4 55.9 %shard_map.298 = (bf16[4,768,768]{2,1,0:T(8,128)(2,1)S(1)}, bf16[4,4,16,256]{3,2,1,0:T(8,128)(2,1)S(1)}) custom-call(f32[4,24,768]{2,1,0:T(8,128)S(1)} %copy-done.3, f32[16,128]{1,0:T(8,128)S(1)} %scatter.4.v_ref), custom_call_target="tpu_custom_call" | custom-call | bytes 104857600 | tf_op jit(solution)/shard_map/pallas_call | solution.py:483
  67.4 2.2 copy-done.6
  70.6 5.9 %fusion.14 = bf16[2048,768]{1,0:T(8,128)(2,1)} fusion(bf16[1024,768]{1,0:T(8,128)(2,1)S(1)} %copy-done.17, s32[1024]{0:T(1024)S(1)} %select_reduce_fusion.2), kind=kOutput, calls=%fused_computation.30 | convolution fusion | flops 3224895488 | bytes 4722688 | tf_op jit(solution)/shard_map/dot_general | solution.py:865
  76.5 4.6 all-to-all-start
  84.7 7.4 %convert_bitcast_fusion.q_ref.k_ref.v_ref = bf16[3,1024,768]{2,1,0:T(8,128)(2,1)} fusion(bf16[4,768,768]{2,1,0:T(8,128)(2,1)} %copy-done.6, bf16[1024,768]{1,0:T(8,128)(2,1)S(1)} %fusion.17.x_ref), kind=kOutput, calls=%fused_computation.19 | convolution fusion | flops 3626237952 | bytes 9830400 | tf_op jit(solution)/shard_map/td,cde->cte/dot_general | solution.py:882
  92.2 18.2 %shard_map.299 = (bf16[1024,768]{1,0:T(8,128)(2,1)S(1)}, f32[6,1024,128]{2,1,0:T(8,128)S(1)}) custom-call(bf16[3,1024,768]{2,1,0:T(8,128)(2,1)} %convert_bitcast_fusion.q_ref.k_ref.v_ref, bf16[3,1024,768]{2,1,0:T(8,128)(2,1)} %convert_bitcast_fusion.q_ref.k_ref.v_ref, bf16[3,1024,768]{2,1,0:T(8,128)(2,1)} %convert_bitcast_fusion.q_ref.k_ref.v_ref, ...), custom_call_target="tpu_custom_call" | custom-call | tf_op jit(solution)/shard_map/pallas_call | solution.py:73
  110.4 3.7 fusion.67
  114.7 1.9 fusion.41
  120.3 6.4 %fusion.13 = bf16[2048,768]{1,0:T(8,128)(2,1)} fusion(s32[1024]{0:T(1024)S(1)} %select_reduce_fusion.2, f32[1024,768]{1,0:T(8,128)S(1)} %get-tuple-element.84, f32[768]{0:T(1024)S(1)} %reshape.288, f32[1024]{0:T(1024)S(1)} %fusion.56, f32[1024]{0:T(1024)S(1)} %broadcast_multiply_fusion.1), kind=kOutput, calls=%fused_computation.29 | convolution fusion | flops 3228041216 | bytes 6306816 | tf_op jit(solution)/shard_map/dot_general | solution.py:865
  126.7 25.9 %all-to-all-done = bf16[8,256,768]{2,1,0:T(8,128)(2,1)} async-done(((bf16[8,256,768]{2,1,0:T(8,128)(2,1)}), bf16[8,256,768]{2,1,0:T(8,128)(2,1)}, u32[]{:S(2)}, u32[]{:S(2)}) %all-to-all-start) | async-done | bytes 3145760 | tf_op jit(solution)/shard_map/all_to_all | solution.py:874
  153.3 112.5 %shard_map.300 = (bf16[6,256,768]{2,1,0:T(8,128)(2,1)}, bf16[2,256,768]{2,1,0:T(8,128)(2,1)}, f32[8,8,512]{2,1,0:T(8,128)}, bf16[8,256,768]{2,1,0:T(8,128)(2,1)}, bf16[4,2,768,768]{3,2,1,0:T(8,128)(2,1)}) custom-call(bf16[8,256,768]{2,1,0:T(8,128)(2,1)} %bitcast.76, f32[8,8,512]{2,1,0:T(8,128)} %broadcast_in_dim.67.gate_ref, ...), custom_call_target="tpu_custom_call" | custom-call | flops 57982058496 | bytes 41943040 | tf_op jit(solution)/shard_map/pallas_call | solution.py:345
  269.8 19.6 %shard_map.301 = bf16[2,256,768]{2,1,0:T(8,128)(2,1)} custom-call(bf16[2,256,768]{2,1,0:T(8,128)(2,1)} %get-tuple-element.49.gs_ref), custom_call_target="tpu_custom_call" | custom-call | bytes 104857600 | tf_op jit(solution)/shard_map/pallas_call | solution.py:357
  290.7 2.3 fusion.23
  293.0 4.2 fusion.3
  297.2 2.7 multiply_reduce_fusion
  301.4 2.8 fusion.64
  304.2 4.4 convolution_convert_fusion.g_ref
  308.6 103.4 %shard_map.302 = (f32[4,24,768]{2,1,0:T(8,128)}, f32[8,768]{1,0:T(8,128)}, bf16[8,256,768]{2,1,0:T(8,128)(2,1)}, f32[1024,768]{1,0:T(8,128)}) custom-call(bf16[3,1024,768]{2,1,0:T(8,128)(2,1)} %convert_bitcast_fusion.q_ref.k_ref.v_ref, bf16[3,1024,768]{2,1,0:T(8,128)(2,1)} %convert_bitcast_fusion.q_ref.k_ref.v_ref, ...), custom_call_target="tpu_custom_call" | custom-call | flops 18119393280 | bytes 104857600 | tf_op jit(solution)/shard_map/pallas_call | solution.py:686
  412.9 2.0 fusion.20
  415.0 7.4 %multiply_add_fusion.2 = f32[1024,768]{1,0:T(8,128)} fusion(f32[1024,768]{1,0:T(8,128)S(1)} %copy-done.11, bf16[2048,768]{1,0:T(8,128)(2,1)} %bitcast.75, s32[1024]{0:T(1024)S(1)} %select_reduce_fusion.2, f32[1024]{0:T(1024)S(1)} %add_divide_fusion), kind=kOutput, calls=%fused_computation.35 | convolution fusion | flops 3224895488 | bytes 9445376 | tf_op jit(solution)/shard_map/dot_general | solution.py:869
  424.1 16.1 %shard_map.303 = f32[16,768]{1,0:T(8,128)S(1)} custom-call(f32[4,24,768]{2,1,0:T(8,128)S(1)} %copy-done.4, f32[16,768]{1,0:T(8,128)S(1)} %select_maximum_fusion.v_ref, bf16[2,768,768]{2,1,0:T(8,128)(2,1)S(1)} %bitcast.61), custom_call_target="tpu_custom_call" | custom-call | tf_op jit(solution)/shard_map/pallas_call | solution.py:768
  442.6 2.2 multiply_add_fusion.3
  445.6 13.4 %multiply_add_fusion = (f32[1,2,768,768]{3,2,1,0:T(8,128)}, f32[1,2,768,768]{3,2,1,0:T(8,128)}, f32[1,2,768,768]{3,2,1,0:T(8,128)}, f32[1,2,768,768]{3,2,1,0:T(8,128)}) fusion(f32[1,2,768,768]{3,2,1,0:T(8,128)} %param.39, f32[1,2,768,768]{3,2,1,0:T(8,128)} %param.30, f32[]{:T(128)S(6)} %min.3, bf16[1,2,768,768]{3,2,1,0:T(8,128)(2,1)S(1)} %copy-done.1, ...), kind=kLoop, calls=%fused_computation.15 | loop fusion | flops 23592960 | bytes 40108036 | tf_op jit(solution)/shard_map/add | solution.py:798
  (125 shorter events, 22.1 us)
Async XLA Ops:
  7.2 4.2 copy-start.21
  7.2 4.2 copy-start.3
  7.2 63.4 %copy-start.17 = (bf16[1024,768]{1,0:T(8,128)(2,1)S(1)}, bf16[1024,768]{1,0:T(8,128)(2,1)}, u32[]{:S(2)}) copy-start(bf16[1024,768]{1,0:T(8,128)(2,1)} %param.22) | copy-start | bytes 4718596
  7.2 62.3 %copy-start.27 = (s32[1,8]{1,0:T(1,128)S(1)}, s32[1,8]{1,0:T(1,128)}, u32[]{:S(2)}) copy-start(s32[1,8]{1,0:T(1,128)} %param.27) | copy-start | bytes 100
  7.2 62.7 %copy-start.25 = (s32[1,1024]{1,0:T(1,128)S(1)}, s32[1,1024]{1,0:T(1,128)}, u32[]{:S(2)}) copy-start(s32[1,1024]{1,0:T(1,128)} %param.26) | copy-start | bytes 12292
  7.2 145.4 %all-gather.2.cloned.1.call-start = ((), (), s32[]{:S(2)}) async-start(), calls=%async_computation.2 | async-start | bytes 11796480 | tf_op jit(solution)/shard_map/all_gather | solution.py:878
  76.5 4.9 %copy-start.12 = (bf16[1024,768]{1,0:T(8,128)(2,1)S(1)}, bf16[1024,768]{1,0:T(8,128)(2,1)}, u32[]{:S(2)}) copy-start(bf16[1024,768]{1,0:T(8,128)(2,1)} %in_ref.1) | copy-start | bytes 4718596
  76.5 76.1 %all-to-all-start = ((bf16[8,256,768]{2,1,0:T(8,128)(2,1)}), bf16[8,256,768]{2,1,0:T(8,128)(2,1)}, u32[]{:S(2)}, u32[]{:S(2)}) async-start(bf16[8,256,768]{2,1,0:T(8,128)(2,1)} %bitcast.64), calls=%async_computation | async-start | bytes 6291456 | tf_op jit(solution)/shard_map/all_to_all | solution.py:874
  81.1 341.3 %reduce-scatter.4.cloned.1.call-start = ((), (), s32[]{:S(2)}) async-start(), calls=%async_computation.3 | async-start | bytes 11796480
  82.8 9.4 %copy-start.2 = (s32[1024,1]{1,0:T(8,128)}, s32[1024,1]{1,0:T(8,128)S(1)}, u32[]{:S(2)}) copy-start(s32[1024,1]{1,0:T(8,128)S(1)} %copy.76.dcol_ref) | copy-start | bytes 12292
  92.2 18.3 %copy-start.13 = (bf16[1024,768]{1,0:T(8,128)(2,1)S(1)}, bf16[1024,768]{1,0:T(8,128)(2,1)}, u32[]{:S(2)}) copy-start(bf16[1024,768]{1,0:T(8,128)(2,1)} %in_ref.1) | copy-start | bytes 4718596
  114.1 6.1 %copy-start.9 = (f32[1024,768]{1,0:T(8,128)}, f32[1024,768]{1,0:T(8,128)S(1)}, u32[]{:S(2)}) copy-start(f32[1024,768]{1,0:T(8,128)S(1)} %get-tuple-element.84) | copy-start | bytes 9437188
  114.2 4.1 copy-start.28
  114.2 4.4 copy-start.26
  268.7 24.3 %copy-start.15 = (pred[1024,2048]{1,0:T(32,128)(4,1)}, pred[1024,2048]{1,0:T(32,128)(4,1)S(1)}, u32[]{:S(2)}) copy-start(pred[1024,2048]{1,0:T(32,128)(4,1)S(1)} %iota_compare_fusion) | copy-start | bytes 6291460
  293.0 4.2 copy-start.10
  304.2 4.4 copy-start.19
  414.9 7.5 %copy-start.4 = (f32[4,24,768]{2,1,0:T(8,128)S(1)}, f32[4,24,768]{2,1,0:T(8,128)}, u32[]{:S(2)}) copy-start(f32[4,24,768]{2,1,0:T(8,128)} %get-tuple-element.54.d_ref) | copy-start | bytes 884740
  414.9 27.7 %copy-start.20 = (f32[4,24,768]{2,1,0:T(8,128)S(1)}, f32[4,24,768]{2,1,0:T(8,128)}, u32[]{:S(2)}) copy-start(f32[4,24,768]{2,1,0:T(8,128)} %param.33) | copy-start | bytes 884740
  414.9 30.0 %copy-start.22 = (f32[10,24]{1,0:T(8,128)S(1)}, f32[10,24]{1,0:T(8,128)}, u32[]{:S(2)}) copy-start(f32[10,24]{1,0:T(8,128)} %param.36) | copy-start | bytes 2884
  414.9 29.9 %copy-start.23 = (f32[10,24]{1,0:T(8,128)S(1)}, f32[10,24]{1,0:T(8,128)}, u32[]{:S(2)}) copy-start(f32[10,24]{1,0:T(8,128)} %param.34) | copy-start | bytes 2884
  414.9 29.9 %copy-start.24 = (f32[10,24]{1,0:T(8,128)S(1)}, f32[10,24]{1,0:T(8,128)}, u32[]{:S(2)}) copy-start(f32[10,24]{1,0:T(8,128)} %param.35) | copy-start | bytes 2884
  424.1 21.5 %copy-start.1 = (bf16[1,2,768,768]{3,2,1,0:T(8,128)(2,1)S(1)}, bf16[1,2,768,768]{3,2,1,0:T(8,128)(2,1)}, u32[]{:S(2)}) copy-start(bf16[1,2,768,768]{3,2,1,0:T(8,128)(2,1)} %reduce-scatter.4.cloned.1.call-done) | copy-start | bytes 7077892
  445.6 13.4 %copy-start.14 = (f32[1024,768]{1,0:T(8,128)S(1)}, f32[1024,768]{1,0:T(8,128)}, u32[]{:S(2)}) copy-start(f32[1024,768]{1,0:T(8,128)} %get-tuple-element.102) | copy-start | bytes 9437188
  (9 other events, 20.9 us)
Sparse Core Ops, SparseCore 0:
  11.5 99.0 all-gather.1
  265.9 93.0 reduce-scatter.3

commit v5 on v4

--- a/solution.py
+++ b/solution.py
@@ -166,10 +166,10 @@
     half=0.5*(1.0+t)
     return x*half, half+x*(0.5*(1.0-t*t))*(c+(3*0.044715*c)*sq)
 
-def moe_kernel(n,cap,send_ref,gate_ref,cot_ref,scale_ref,w_ref,
+def moe_kernel(n,cap,square,send_ref,gate_ref,cot_ref,scale_ref,w_ref,
                back_ref,late_ref,chosen_ref,ret_ref,gw_ref,
                recv,gates,cot,w,gw,ret_s,gs_s,ch_s,g_s,racc,sacc,
-               send_sem,recv_sem,gate_send,gate_recv,back_send,back_recv,ch_send,ch_recv,w_sem,loc_sem,ret_sem):
+               send_sem,recv_sem,gate_send,gate_recv,back_send,back_recv,ch_send,ch_recv,on_send,on_recv,w_sem,loc_sem,ret_sem):
     per=TILE//cap
     tiles=n//per
     chunks=w_ref.shape[0]
@@ -179,7 +179,19 @@
         pl.semaphore_signal(barrier,inc=1,device_id={"expert":flip(me,o,n)},device_id_type=MESH)
         return 0
     lax.fori_loop(1,n,greet,0)
-    pl.semaphore_wait(barrier,n-1)
+    d=lax.axis_index("dp")
+    sides=[flip(d,1,chunks),flip(d,2,chunks)] if square else []
+    for side in sides:
+        pl.semaphore_signal(barrier,inc=1,device_id={"dp":side},device_id_type=MESH)
+    pl.semaphore_wait(barrier,n-1+len(sides))
+    def on_copy(k):
+        return pltpu.make_async_remote_copy(src_ref=w_ref.at[sides[k],k],dst_ref=w.at[sides[k],k],
+            send_sem=on_send.at[k],recv_sem=on_recv.at[k],device_id={"dp":sides[1-k]},device_id_type=MESH)
+    def on_in(k):
+        across=flip(d,3,chunks)
+        return pltpu.make_async_remote_copy(src_ref=w_ref.at[sides[k],k],dst_ref=w.at[across,k],
+            send_sem=on_send.at[k],recv_sem=on_recv.at[k],device_id={"dp":sides[1-k]},device_id_type=MESH)
+    for k in range(len(sides)): on_copy(k).start()
 
     def copies(src,dst,send,recv_,peer,there):
         return pltpu.make_async_remote_copy(src_ref=src,dst_ref=dst,send_sem=send.at[peer],recv_sem=recv_.at[there],
@@ -202,7 +214,7 @@
     own=[pltpu.make_async_copy(send_ref.at[me],recv.at[me],loc_sem.at[0]),
          pltpu.make_async_copy(gate_ref.at[me],gates.at[me],loc_sem.at[1]),
          pltpu.make_async_copy(cot_ref,cot,loc_sem.at[2]),
-         pltpu.make_async_copy(w_ref,w,w_sem)]
+        ]+[pltpu.make_async_copy(w_ref.at[c],w.at[c],w_sem.at[i]) for i,c in enumerate(([d]+sides) if square else range(chunks))]
     for c in own: c.start()
     def wipe(c,_):
         gw[c]=jnp.zeros(gw.shape[1:],jnp.float32)
@@ -228,11 +240,17 @@
         at=pl.ds(pl.multiple_of(block*per,per),per)
         rows=pl.ds(pl.multiple_of(block*TILE,TILE),TILE)
         gate=jnp.transpose(jnp.sum(gates[at],axis=0))[:,0:1]
-        grad_out=cot[rows,:].astype(jnp.float32)*scale_ref[rows,:]
+        scale=jnp.concatenate([jnp.broadcast_to(scale_ref[pl.ds(block*per+j,1),0:1],(cap,1)) for j in range(per)],axis=0)
+        grad_out=cot[rows,:].astype(jnp.float32)*scale
         g_s[...]=(gate*grad_out).astype(jnp.bfloat16)
         racc[...]=jnp.zeros_like(racc)
         sacc[...]=jnp.zeros_like(sacc)
-        def chunk(c,_):
+        def chunk(i,_):
+            c=flip(d,i,chunks)
+            if square:
+                @pl.when((t==0)&(i==chunks-1))
+                def _():
+                    for k in range(2): on_in(k).wait_recv()
             x=recv[at].reshape(TILE,recv.shape[2])
             g=g_s[...]
             act,slope=gelu_pair(jnp.dot(x,w[c,0],preferred_element_type=jnp.float32))
@@ -264,7 +282,7 @@
         ret=racc[...].astype(jnp.bfloat16)
         ret_s[at]=ret.reshape(per,cap,recv.shape[2])
         pltpu.make_async_copy(ret_s.at[at],ret_ref.at[at],ret_sem.at[t]).start()
-        grad_out=cot[rows,:].astype(jnp.float32)*scale_ref[rows,:]
+        grad_out=cot[rows,:].astype(jnp.float32)*scale
         chosen=jnp.sum(grad_out*ret.astype(jnp.float32),axis=1,keepdims=True)*gate*(1.0-gate)
         chosen=jnp.transpose(jnp.broadcast_to(chosen,(TILE,128)))[0:8,:]
         def tell(j,_):
@@ -282,7 +300,7 @@
     lax.fori_loop(0,tiles,tile,0)
     def pack(c,_):
         w[c]=gw[c].astype(jnp.bfloat16)
-        pltpu.make_async_copy(w.at[c],gw_ref.at[c],w_sem).start()
+        pltpu.make_async_copy(w.at[c],gw_ref.at[c],w_sem.at[c]).start()
         return 0
     lax.fori_loop(0,chunks,pack,0)
     own_ch.wait()
@@ -308,7 +326,8 @@
         pltpu.make_async_copy(ret_s.at[at],ret_ref.at[at],ret_sem.at[t]).wait()
         return 0
     lax.fori_loop(0,tiles,stored,0)
-    pltpu.make_async_copy(w,gw_ref,w_sem).wait()
+    for c in range(chunks): pltpu.make_async_copy(w.at[c],gw_ref.at[c],w_sem.at[c]).wait()
+    for k in range(len(sides)): on_copy(k).wait_send()
 
 def late_kernel(n,gs_ref,out_ref,send_sem,recv_sem):
     per=gs_ref.shape[0]
@@ -334,7 +353,7 @@
         return 0
     lax.fori_loop(0,per,end,0)
 
-def moe(send_rows,gate_slots,cot,scale,weights):
+def moe(send_rows,gate_slots,cot,scale,weights,square):
     n,cap,D=send_rows.shape
     chunks,_,_,FC=weights.shape
     per=TILE//cap
@@ -342,7 +361,7 @@
     bf=jnp.bfloat16; f32=jnp.float32
     dma=pltpu.SemaphoreType.DMA
     flops=6*2*n*cap*D*chunks*FC
-    back,late,chosen,ret,gw=pl.pallas_call(partial(moe_kernel,n,cap),
+    back,late,chosen,ret,gw=pl.pallas_call(partial(moe_kernel,n,cap,square),
         out_shape=[jax.ShapeDtypeStruct((n-per,cap,D),bf),jax.ShapeDtypeStruct((per,cap,D),bf),jax.ShapeDtypeStruct((n,8,TILE),f32),
                    jax.ShapeDtypeStruct((n,cap,D),bf),jax.ShapeDtypeStruct(weights.shape,bf)],
         in_specs=[any_,any_,any_,pl.BlockSpec(memory_space=pltpu.VMEM),any_],
@@ -350,17 +369,23 @@
         scratch_shapes=[pltpu.VMEM((n,cap,D),bf),pltpu.VMEM((n,8,TILE),f32),pltpu.VMEM((n*cap,D),bf),
             pltpu.VMEM(weights.shape,bf),pltpu.VMEM(weights.shape,f32),pltpu.VMEM((n,cap,D),bf),pltpu.VMEM((n,cap,D),bf),
             pltpu.VMEM((n,8,TILE),f32),pltpu.VMEM((TILE,D),bf),pltpu.VMEM((TILE,D),f32),pltpu.VMEM((TILE,D),f32)]
-            +[dma((n,))]*8+[dma(()),dma((3,)),dma((n//per,))],
+            +[dma((n,))]*8+[dma((2,)),dma((2,)),dma((chunks,)),dma((3,)),dma((n//per,))],
         compiler_params=pltpu.CompilerParams(vmem_limit_bytes=62*2**20,collective_id=1,has_side_effects=True),
         cost_estimate=pl.CostEstimate(flops=flops,bytes_accessed=40*2**20,transcendentals=0),
     )(send_rows,gate_slots,cot,scale,weights)
-    late=pl.pallas_call(partial(late_kernel,n),
+    return back,late,chosen,ret,gw
+
+def send_late(late,n):
+    per,cap,D=late.shape
+    any_=pl.BlockSpec(memory_space=pl.ANY)
+    bf=jnp.bfloat16
+    dma=pltpu.SemaphoreType.DMA
+    return pl.pallas_call(partial(late_kernel,n),
         out_shape=jax.ShapeDtypeStruct((per,cap,D),bf),in_specs=[any_],out_specs=any_,
         scratch_shapes=[dma((per,)),dma((per,))],
         compiler_params=pltpu.CompilerParams(collective_id=5,has_side_effects=True),
         cost_estimate=pl.CostEstimate(flops=0,bytes_accessed=100*2**20,transcendentals=0),
     )(late)
-    return back,late,chosen,ret,gw
 
 
 def near(dps,pairs):
@@ -380,155 +405,411 @@
 def remote(src,dst,send,recv,dev):
     return pltpu.make_async_remote_copy(src_ref=src,dst_ref=dst,send_sem=send,recv_sem=recv,device_id=dev,device_id_type=MESH)
 
-def gather_kernel(dps,pairs,w_ref,v_ref,out_ref,vout_ref,both,blk,vboth,vblk,
-                  s1,r1,loc,us,ur,ls,lr,vzs,vzr,ds_,dr,vds,vdr,ps,pr):
-    r=w_ref.shape[1]; R=2*r
-    d,pair,core,partner,over,along=near(dps,pairs)
-    greet_all([partner]+[x[1] for x in over]+[x[1] for x in along])
-    mine=pl.ds(pl.multiple_of(core*r,8),r)
-    lanes=pl.ds(pl.multiple_of(core*128,128),128)
-    half=pl.ds(core*2,2); rest=pl.ds(2-core*2,2)
-    def rows(dd,q): return pl.ds(pl.multiple_of((dd*pairs+q)*R,16),R)
-    c1=[remote(w_ref,both.at[:,mine,:],s1.at[0],r1.at[0],partner),
-        remote(v_ref,vboth.at[:,lanes],s1.at[1],r1.at[1],partner)]
-    for c in c1: c.start()
-    both[:,mine,:]=w_ref[...]
-    vboth[:,lanes]=v_ref[...]
-    for c in c1: c.wait()
-    blk[...]=both[...].astype(jnp.bfloat16)
-    vblk[...]=vboth[...].astype(jnp.bfloat16)
-    own=[pltpu.make_async_copy(blk,out_ref.at[:,rows(d,pair),:],loc.at[0]),
-         pltpu.make_async_copy(vblk,vout_ref.at[d,pair],loc.at[1])]
-    for c in own: c.start()
-    above={"expert":2*lax.rem(pair+1,pairs)+core}; below={"expert":2*lax.rem(pair+pairs-1,pairs)+core}
-    has_above=pair<pairs-1; has_below=pair>0
-    def up(dd,q,src=None):
-        here=out_ref.at[half,rows(dd,q),:]
-        return remote(here if src is None else src,here,us.at[dd,q],ur.at[dd,q],above)
-    def down(dd,q,src=None):
-        here=out_ref.at[half,rows(dd,q),:]
-        return remote(here if src is None else src,here,ls.at[dd,q],lr.at[dd,q],below)
-    def hand(dd,q):
-        here=out_ref.at[half,rows(dd,q),:]
-        return remote(here,here,ps.at[dd,q],pr.at[dd,q],partner)
-    def over_copy(dd,dev):
-        here=out_ref.at[half,rows(d,pair),:]
-        return remote(blk.at[half],here,ds_.at[dd],dr.at[d],dev)
-    def over_in(dd,dev):
-        here=out_ref.at[half,rows(dd,pair),:]
-        return remote(here,here,ds_.at[dd],dr.at[dd],dev)
-    def v_over(dd,dev): return remote(vblk,vout_ref.at[d,pair],vds.at[dd],vdr.at[d],dev)
-    def v_along(q,dev): return remote(vout_ref.at[:,pair],vout_ref.at[:,pair],vzs.at[q],vzr.at[pair],dev)
-    for dd,dev in over:
-        over_copy(dd,dev).start()
-        v_over(dd,dev).start()
-    mine_out=blk.at[half]
-    @pl.when(has_above)
-    def _(): up(d,pair,mine_out).start()
-    @pl.when(has_below)
-    def _(): down(d,pair,mine_out).start()
-    for dd,dev in over:
-        over_in(dd,dev).wait_recv()
-        @pl.when(has_above)
-        def _(): up(dd,pair).start()
-        @pl.when(has_below)
-        def _(): down(dd,pair).start()
-        hand(dd,pair).start()
-    for dd,dev in over:
-        remote(vblk,vout_ref.at[dd,pair],vds.at[dd],vdr.at[dd],dev).wait_recv()
-    own[1].wait()
-    for q,dev in along: v_along(q,dev).start()
-    groups=[d]+[x[0] for x in over]
-    for k in range(1,pairs):
+def upright(row):
+    return jnp.transpose(row.astype(jnp.float32))[:, 0:1].astype(jnp.int32)
+
+
+def head_kernel(dps, pairs, n, cap, w_ref, v_ref, x_ref, cot_ref, order_ref, counts_ref, drow_ref, ew_ref,
+                w_out, vec_out, slot_out, cot_out, proj_out, normed_out, mixed_out, lse_out, hidden_out,
+                gate_out, send_out, tile_out, ew_out,
+                ew32, ew, both, blk, vboth, vblk, w, vall, slots, unit, normed, proj, mixed, lse, bias, sent, cots, sends,
+                tiles, s1, r1, loc, zs, zr, vzs, vzr, ds_, dr, vds, vdr, ps, pr, cs, cr, ewl, xs, xr, ys, yr, out_sem, send_sem):
+    r = w_ref.shape[1]
+    R = 2 * r
+    T, D = x_ref.shape
+    d, pair, core, partner, over, along = near(dps, pairs)
+    me = lax.axis_index("expert")
+    bf, f32 = jnp.bfloat16, jnp.float32
+    ew_load = pltpu.make_async_copy(ew_ref.at[0], ew32, ewl.at[0])
+    ew_load.start()
+    barrier = pltpu.get_barrier_semaphore()
+
+    def greet(o, _):
+        pl.semaphore_signal(barrier, inc=1, device_id={"expert": flip(me, o, n)}, device_id_type=MESH)
+        return 0
+
+    lax.fori_loop(1, n, greet, 0)
+    for _, dev in over:
+        pl.semaphore_signal(barrier, inc=1, device_id=dev, device_id_type=MESH)
+    pl.semaphore_wait(barrier, n - 1 + dps - 1)
+
+    side_x, side_y = flip(d, 1, dps), flip(d, 2, dps)
+    to_x, to_y = {"dp": side_x}, {"dp": side_y}
+
+    def x_copy(src, slot, m):
+        return remote(src, ew_out.at[slot, m], xs.at[slot, m], xr.at[slot, m], to_x)
+
+    def y_copy(src, slot, m):
+        return remote(src, ew_out.at[slot, m], ys.at[slot, m], yr.at[slot, m], to_y)
+
+    mine = pl.ds(pl.multiple_of(core * r, 8), r)
+    half = pl.ds(core * 2, 2)
+    rest = pl.ds(2 - core * 2, 2)
+
+    def rows(dd, q):
+        return pl.ds(pl.multiple_of((dd * pairs + q) * R, 16), R)
+
+    c1 = [
+        remote(w_ref, both.at[:, mine, :], s1.at[0], r1.at[0], partner),
+        remote(v_ref, vboth.at[core], s1.at[1], r1.at[1], partner),
+    ]
+    for c in c1:
+        c.start()
+    both[:, mine, :] = w_ref[...]
+    vboth[core] = v_ref[...]
+    for c in c1:
+        c.wait()
+    blk[...] = both[...].astype(bf)
+    vblk[...] = (vboth[0] + vboth[1]).astype(bf)
+    w[:, rows(d, pair), :] = blk[...]
+    vall[d, pair] = vblk[...]
+    def along_copy(q, dev):
+        return remote(blk.at[half], w.at[half, rows(d, pair), :], zs.at[q], zr.at[pair], dev)
+
+    def over_copy(dd, q, dev):
+        here = w.at[half, rows(d, q), :]
+        return remote(here, here, ds_.at[dd, q], dr.at[d, q], dev)
+
+    def hand(dd, q):
+        here = w.at[half, rows(dd, q), :]
+        return remote(here, here, ps.at[dd, q], pr.at[dd, q], partner)
+
+    def v_along(q, dev):
+        return remote(vblk, vall.at[d, pair], vzs.at[q], vzr.at[pair], dev)
+
+    def v_over(dd, dev):
+        return remote(vall.at[d], vall.at[d], vds.at[dd], vdr.at[d], dev)
+
+    for q, dev in along:
+        along_copy(q, dev).start()
+        v_along(q, dev).start()
+    for dd, dev in over:
+        over_copy(dd, pair, dev).start()
+
+    tokens_across = lax.broadcasted_iota(jnp.int32, (T, T), 1)
+    position = lax.broadcasted_iota(jnp.int32, (8, T), 1)
+    sorted_slot, end = position, 0
+    for e in range(n):
+        count = counts_ref[0, e]
+        end = end + count
+        sorted_slot = sorted_slot + jnp.where(position >= end, cap - count, 0)
+    slot_col = upright(sorted_slot)
+    order_col = upright(jnp.broadcast_to(order_ref[...], (8, T)))
+    slots[...] = jnp.broadcast_to(
+        jnp.sum(jnp.where(order_col == tokens_across, slot_col, 0), axis=0, keepdims=True), (8, T)
+    )
+    doc_col = upright(jnp.broadcast_to(drow_ref[...], (8, T)))
+
+    def pick(p):
+        here = lax.broadcasted_iota(jnp.int32, (cap, T), 0) + p * cap
+        return here == slots[0:1, :]
+
+    def cot_copy(p):
+        return remote(cots.at[p], cot_out.at[me], cs.at[p], cr.at[me], {"expert": p})
+
+    def cot_in(p):
+        return remote(cots.at[p], cot_out.at[p], cs.at[p], cr.at[p], {"expert": p})
+
+    def place(i, _):
+        p = flip(me, n - 1 - i, n)
+        cots[p] = jnp.dot(pick(p).astype(bf), cot_ref[...], preferred_element_type=f32).astype(bf)
+
+        return 0
+
+    groups = [d] + [x[0] for x in over]
+    lax.fori_loop(0, n // 2, place, 0)
+    for q, dev in along:
+        here = w.at[half, rows(d, q), :]
+        remote(here, here, zs.at[q], zr.at[q], dev).wait_recv()
+        for dd, dev2 in over:
+            over_copy(dd, q, dev2).start()
+        hand(d, q).start()
+    for q, dev in along:
+        remote(vblk, vall.at[d, q], vzs.at[q], vzr.at[q], dev).wait_recv()
+    for dd, dev in over:
+        v_over(dd, dev).start()
+    ew_load.wait()
+    for m in range(2):
+        ew[m] = ew32[m].astype(bf)
+    own_ew = pltpu.make_async_copy(ew, ew_out.at[d], ewl.at[0])
+    own_ew.start()
+    for m in range(2):
+        x_copy(ew.at[m], d, m).start()
+        y_copy(ew.at[1 - m], d, 1 - m).start()
+    lax.fori_loop(n // 2, n, place, 0)
+
+    def give(i, _):
+        cot_copy(flip(me, n - 1 - i, n)).start()
+        return 0
+
+    lax.fori_loop(0, n - 1, give, 0)
+    own_cot = pltpu.make_async_copy(cots.at[me], cot_out.at[me], loc.at[0])
+    own_cot.start()
+
+    def unit_rows(b):
+        at = pl.ds(b * 256, 256)
+        x = x_ref[at, :].astype(f32)
+        center = x - jnp.mean(x, axis=-1, keepdims=True)
+        unit[at, :] = center * lax.rsqrt(jnp.mean(center * center, axis=-1, keepdims=True) + norm_eps)
+
+    for b in range(T // 256):
+        unit_rows(b)
+    for i in range(LEN // QB):
+        first = max(0, i - WINDOW // QB) * QB
+        W = (i + 1) * QB - first
+        qp = i * QB + lax.broadcasted_iota(jnp.int32, (QB, W), 0)
+        kp = first + lax.broadcasted_iota(jnp.int32, (QB, W), 1)
+        ok = (kp <= qp) & (doc_col[i * QB : (i + 1) * QB, :] == drow_ref[:, first : first + W])
+        bias[i * QB : (i + 1) * QB, :W] = jnp.where(ok, 0.0, masked_score)
+    for q in [pair] + [x[0] for x in along]:
+        for dd, dev in over:
+            here = w.at[half, rows(dd, q), :]
+            remote(here, here, ds_.at[dd, q], dr.at[dd, q], dev).wait_recv()
+            hand(dd, q).start()
+    for dd, dev in over:
+        remote(vall.at[dd], vall.at[dd], vds.at[dd], vdr.at[dd], dev).wait_recv()
+    vec = jnp.zeros(vec_out.shape, f32)
+    for dd in range(dps):
+        for q in range(pairs):
+            vec = vec + vall[dd, q].astype(f32)
+    vec_out[...] = vec
+    slot_out[...] = slots[...]
+    normed[...] = (unit[...] * vec_out[0:1, :]).astype(bf)
+
+    def from_partner(dd, q):
+        there = w.at[rest, rows(dd, q), :]
+        remote(there, there, ps.at[dd, q], pr.at[dd, q], partner).wait_recv()
+
+    for dd, dev in over:
+        from_partner(dd, pair)
+    for q, _ in along:
         for dd in groups:
-            @pl.when(pair>=k)
-            def _():
-                up(dd,pair-k).wait_recv()
-                @pl.when(has_above)
-                def _(): up(dd,pair-k).start()
-                hand(dd,pair-k).start()
-            @pl.when(pair+k<pairs)
-            def _():
-                down(dd,pair+k).wait_recv()
-                @pl.when(has_below)
-                def _(): down(dd,pair+k).start()
-                hand(dd,pair+k).start()
-    for q,dev in along:
-        remote(vout_ref.at[:,q],vout_ref.at[:,q],vzs.at[q],vzr.at[q],dev).wait_recv()
-    def from_partner(dd,q):
-        there=out_ref.at[rest,rows(dd,q),:]
-        remote(there,there,ps.at[dd,q],pr.at[dd,q],partner).wait_recv()
-    for dd,dev in over: from_partner(dd,pair)
-    for q,_ in along:
-        for dd in groups: from_partner(dd,q)
-    for dd,dev in over:
-        over_copy(dd,dev).wait_send(); v_over(dd,dev).wait_send(); hand(dd,pair).wait_send()
-    for q,dev in along:
-        v_along(q,dev).wait_send()
-        for dd in groups: hand(dd,q).wait_send()
-    for dd in groups:
-        for k in range(pairs):
-            @pl.when((pair>=k)&has_above)
-            def _(): up(dd,pair-k).wait_send()
-            @pl.when((pair+k<pairs)&has_below)
-            def _(): down(dd,pair+k).wait_send()
-    own[0].wait()
-
-def gather_dense(weights,vectors,dps,n,collective_id=2):
-    pairs=n//2
-    m,r,D=weights.shape
-    V=jnp.zeros((16,128),jnp.float32).at[:vectors.shape[0],:r].set(vectors)
-    dma=pltpu.SemaphoreType.DMA
-    f32=jnp.float32; bf=jnp.bfloat16
-    out,vout=pl.pallas_call(partial(gather_kernel,dps,pairs),
-        out_shape=[jax.ShapeDtypeStruct((m,r*n*dps,D),bf),jax.ShapeDtypeStruct((dps,pairs,16,256),bf)],
-        in_specs=[pl.BlockSpec(memory_space=pltpu.VMEM)]*2,
-        out_specs=[pl.BlockSpec(memory_space=pl.ANY)]*2,
-        scratch_shapes=[pltpu.VMEM((m,2*r,D),f32),pltpu.VMEM((m,2*r,D),bf),pltpu.VMEM((16,256),f32),pltpu.VMEM((16,256),bf),
-            dma((2,)),dma((2,)),dma((2,)),dma((dps,pairs)),dma((dps,pairs)),dma((dps,pairs)),dma((dps,pairs)),dma((pairs,)),dma((pairs,)),
-            dma((dps,)),dma((dps,)),dma((dps,)),dma((dps,)),dma((dps,pairs)),dma((dps,pairs))],
-        compiler_params=pltpu.CompilerParams(vmem_limit_bytes=16*2**20,collective_id=collective_id,has_side_effects=True),
-        cost_estimate=pl.CostEstimate(flops=0,bytes_accessed=100*2**20,transcendentals=0),
-    )(weights,V)
-    k=vectors.shape[0]
-    vec=vout[:,:,:k].reshape(dps,pairs,k,2,128)[...,:r]
-    vec=jnp.transpose(vec,(2,0,1,3,4)).reshape(k,r*n*dps)
-    return out,vec
-
-def tail_kernel(dps, pairs, cap, q_ref, k_ref, v_ref, lse_ref, g_ref, dcol_ref, drow_ref, gain_ref,
-                x_ref, mixed_ref, ga_ref, prod_ref, w_ref, gh_ref, in_ref,
-                out_ref, gain_out, returned_ref, dx_ref,
+            from_partner(dd, q)
+
+    outs = [
+        pltpu.make_async_copy(w, w_out, out_sem.at[0]),
+        pltpu.make_async_copy(normed, normed_out, out_sem.at[1]),
+    ]
+    for c in outs:
+        c.start()
+
+    def project(i, _):
+        c = i // 2
+        at = pl.ds(pl.multiple_of(i % 2 * (T // 2), T // 2), T // 2)
+        proj[c, at, :] = jnp.dot(normed[at, :], w[c], preferred_element_type=f32).astype(bf)
+        return 0
+
+    lax.fori_loop(0, 6, project, 0)
+    outs.append(pltpu.make_async_copy(proj, proj_out, out_sem.at[2]))
+    outs[-1].start()
+    low_lane = lax.broadcasted_iota(jnp.int32, (QB, 128), 1) < HEAD_DIM
+
+    def attend(h, _):
+        lanes = pl.ds(pl.multiple_of(h * 128, 128), 128)
+        for i in range(LEN // QB):
+            here = slice(i * QB, (i + 1) * QB)
+            first = max(0, i - WINDOW // QB) * QB
+            W = (i + 1) * QB - first
+            keys = slice(first, first + W)
+            q = proj[0, here, lanes] * jnp.bfloat16(HEAD_DIM**-0.5)
+            zero = jnp.zeros_like(q)
+            qs = jnp.concatenate([jnp.where(low_lane, q, zero), jnp.where(low_lane, zero, q)], axis=0)
+            s = lax.dot_general(qs, proj[1, keys, lanes], NT, preferred_element_type=f32)
+            s = (s.reshape(2, QB, W) + bias[here, :W][None]).reshape(2 * QB, W)
+            top = jnp.max(s, axis=1, keepdims=True)
+            e = jnp.exp(s - top)
+            total = jnp.sum(e, axis=1, keepdims=True)
+            p = (e * (1.0 / total)).astype(bf)
+            o = jnp.dot(p, proj[2, keys, lanes], preferred_element_type=f32)
+            mixed[here, lanes] = jnp.where(low_lane, o[:QB], o[QB:]).astype(bf)
+            ends = top + jnp.log(total)
+            lse[h, here, :] = jnp.where(low_lane, ends[:QB], ends[QB:])
+        return 0
+
+    lax.fori_loop(0, D // 128, attend, 0)
+    outs += [
+        pltpu.make_async_copy(mixed, mixed_out, out_sem.at[3]),
+        pltpu.make_async_copy(lse, lse_out, out_sem.at[4]),
+    ]
+    outs[-2].start()
+    outs[-1].start()
+    E = vec_out.shape[0] - 2
+    hidden = unit
+
+    def finish(b, _):
+        at = pl.ds(pl.multiple_of(b * 256, 256), 256)
+        state = x_ref[at, :].astype(f32) + jnp.dot(mixed[at, :], w[3], preferred_element_type=f32)
+        hidden[at, :] = state
+        center = state - jnp.mean(state, axis=-1, keepdims=True)
+        spread = jnp.mean(center * center, axis=-1, keepdims=True)
+        two = center * lax.rsqrt(spread + norm_eps) * vec_out[1:2, :]
+        sent[at, :] = two.astype(bf)
+        which = lax.broadcasted_iota(jnp.int32, (vec_out.shape[0], 256), 0) - 2
+        chosen = (which == slots[0:1, at] // cap).astype(bf)
+        rows_c = lax.dot_general(chosen, vec_out[...].astype(bf), TN, preferred_element_type=f32)
+        logit = jnp.sum(two * rows_c, axis=1, keepdims=True)
+        gate = 1.0 / (1.0 + jnp.exp(-logit))
+        gate_out[:, at] = jnp.transpose(jnp.broadcast_to(gate, (256, 128)))[0:8, :]
+        return 0
+
+    lax.fori_loop(0, T // 256, finish, 0)
+    outs.append(pltpu.make_async_copy(hidden, hidden_out, out_sem.at[5]))
+    outs[-1].start()
+    tiles[...] = jnp.zeros(tiles.shape, f32)
+    part = pl.ds(pl.multiple_of(me % (TILE // cap) * cap, 128), cap)
+
+    def fill(p, _):
+        chosen = pick(p)
+        sends[p] = jnp.dot(chosen.astype(bf), sent[...], preferred_element_type=f32).astype(bf)
+        tiles[p, :, part] = lax.dot_general(
+            gate_out[...], chosen.astype(f32), NT, precision=lax.Precision.HIGHEST, preferred_element_type=f32
+        )
+        pltpu.make_async_copy(sends.at[p], send_out.at[p], send_sem).start()
+        return 0
+
+    lax.fori_loop(0, n, fill, 0)
+    outs.append(pltpu.make_async_copy(tiles, tile_out, out_sem.at[6]))
+    outs[-1].start()
+    for q, dev in along:
+        along_copy(q, dev).wait_send()
+        v_along(q, dev).wait_send()
+        hand(d, q).wait_send()
+    for dd, dev in over:
+        v_over(dd, dev).wait_send()
+        for q in [pair] + [x[0] for x in along]:
+            over_copy(dd, q, dev).wait_send()
+            hand(dd, q).wait_send()
+
+    def settle(o, _):
+        p = flip(me, o, n)
+        cot_copy(p).wait_send()
+        cot_in(p).wait_recv()
+        return 0
+
+    lax.fori_loop(1, n, settle, 0)
+    pltpu.make_async_copy(cots.at[me], cot_out.at[me], loc.at[0]).wait()
+    own_ew.wait()
+    for m in range(2):
+        x_copy(ew.at[m], d, m).wait_send()
+        y_copy(ew.at[m], d, m).wait_send()
+        x_copy(ew.at[m], side_x, m).wait_recv()
+        y_copy(ew.at[m], side_y, m).wait_recv()
+    for c in outs:
+        c.wait()
+    pltpu.make_async_copy(sends, send_out, send_sem).wait()
+
+
+def head(weights, vectors, inputs, cotangent, token_order, counts, documents, expert_weights, dps, n, cap):
+    pairs = n // 2
+    m, r, D = weights.shape
+    T = inputs.shape[0]
+    k = vectors.shape[0]
+    f32, bf = jnp.float32, jnp.bfloat16
+    dma = pltpu.SemaphoreType.DMA
+    any_ = pl.BlockSpec(memory_space=pl.ANY)
+    vm = pl.BlockSpec(memory_space=pltpu.VMEM)
+    dev = lax.axis_index("dp") * n + lax.axis_index("expert")
+    K = (k + 15) // 16 * 16
+    placed = lax.dynamic_update_slice(jnp.zeros((K, D), f32), vectors, (0, dev * r))
+    shape = jax.ShapeDtypeStruct
+    grid = lambda: dma((dps, pairs))
+    return pl.pallas_call(
+        partial(head_kernel, dps, pairs, n, cap),
+        out_shape=[
+            shape((m, D, D), bf), shape((K, D), f32), shape((8, T), jnp.int32), shape((n, cap, D), bf),
+            shape((3, T, D), bf), shape((T, D), bf), shape((T, D), bf), shape((D // 128, T, 128), f32),
+            shape((T, D), f32), shape((8, T), f32), shape((n, cap, D), bf), shape((n, 8, TILE), f32),
+            shape((dps,) + expert_weights.shape[1:], bf),
+        ],
+        in_specs=[vm] * 5 + [pl.BlockSpec(memory_space=pltpu.SMEM), vm, any_],
+        out_specs=[any_, vm, vm, any_, any_, any_, any_, any_, any_, vm, any_, any_, any_],
+        scratch_shapes=[
+            pltpu.VMEM(expert_weights.shape[1:], f32), pltpu.VMEM(expert_weights.shape[1:], bf),
+            pltpu.VMEM((m, 2 * r, D), f32), pltpu.VMEM((m, 2 * r, D), bf), pltpu.VMEM((2, K, D), f32),
+            pltpu.VMEM((K, D), bf), pltpu.VMEM((m, D, D), bf), pltpu.VMEM((dps, pairs, K, D), bf),
+            pltpu.VMEM((8, T), jnp.int32), pltpu.VMEM((T, D), f32), pltpu.VMEM((T, D), bf),
+            pltpu.VMEM((3, T, D), bf), pltpu.VMEM((T, D), bf), pltpu.VMEM((D // 128, T, 128), f32),
+            pltpu.VMEM((T, min(T, WINDOW + QB)), f32), pltpu.VMEM((T, D), bf), pltpu.VMEM((n, cap, D), bf),
+            pltpu.VMEM((n, cap, D), bf), pltpu.VMEM((n, 8, TILE), f32),
+            dma((2,)), dma((2,)), dma((1,)), dma((pairs,)), dma((pairs,)), dma((pairs,)), dma((pairs,)),
+            grid(), grid(), dma((dps,)), dma((dps,)), grid(), grid(), dma((n,)), dma((n,)),
+            dma((1,)), dma((dps, 2)), dma((dps, 2)), dma((dps, 2)), dma((dps, 2)), dma((7,)), dma(()),
+        ],
+        compiler_params=pltpu.CompilerParams(
+            vmem_limit_bytes=60 * 2**20, collective_id=2, has_side_effects=True
+        ),
+        cost_estimate=pl.CostEstimate(flops=20 * T * D * D, bytes_accessed=200 * 2**20, transcendentals=0),
+    )(weights, placed, inputs, cotangent, token_order, counts, documents, expert_weights)
+
+
+def tail_kernel(dps, pairs, cap, q_ref, k_ref, v_ref, lse_ref, drow_ref, vec_ref, slot_ref, gate_ref,
+                scale_ref, chosen_ref, x_ref, mixed_ref, prod_ref, w_ref, in_ref, late_ref, back_ref, cot_ref,
+                hidden_ref,
+                out_ref, vec_out, dx_ref, block_ref,
                 bias_ref, dk_ref, dv_ref, left, right, got, own, total, in2, tb, in3, u, in4, w, gh, xin,
-                ls, s1, r1, s2, r2, s3, r3, s4, r4, rs, rr, own_sem, dx_sem):
+                ret, hid, back, cot, g_ref, chs, dcol_ref,
+                ls, s1, r1, s2, r2, s3, r3, s4, r4, rs, rr, bs, br, own_sem, dx_sem, block_sem):
     h = pl.program_id(0)
     n = 2 * pairs
+    per = late_ref.shape[0]
+    early = (n - per) * cap
     me = lax.axis_index("expert")
     d, pair, core, partner, over, along = near(dps, pairs)
     rows = out_ref.shape[1]
     R = 2 * rows
     T, D = x_ref.shape
+    bf, f32 = jnp.bfloat16, jnp.float32
+    B = 256
     loads = [
-        pltpu.make_async_copy(x_ref, left.at[0], ls.at[0]),
-        pltpu.make_async_copy(mixed_ref, left.at[1], ls.at[1]),
-        pltpu.make_async_copy(ga_ref, right.at[3], ls.at[2]),
-        pltpu.make_async_copy(w_ref.at[pl.ds(0, 3)], w, ls.at[3]),
-        pltpu.make_async_copy(gh_ref, gh, ls.at[4]),
-        pltpu.make_async_copy(in_ref, xin, ls.at[5]),
+        pltpu.make_async_copy(back_ref, back.at[pl.ds(0, n - per)], ls.at[0]),
+        pltpu.make_async_copy(hidden_ref, hid, ls.at[1]),
+        pltpu.make_async_copy(cot_ref, cot, ls.at[2]),
+        pltpu.make_async_copy(w_ref, w, ls.at[3]),
+        pltpu.make_async_copy(mixed_ref, left.at[1], ls.at[4]),
+        pltpu.make_async_copy(x_ref, left.at[0], ls.at[5]),
+        pltpu.make_async_copy(in_ref, xin, ls.at[6]),
     ]
 
     def product(m):
-        return lax.dot_general(left[m // 3], right[m], TN, preferred_element_type=jnp.float32)
+        return lax.dot_general(left[m // 3], right[m], TN, preferred_element_type=f32)
 
     def ret_copy(peer):
-        return remote(prod_ref.at[peer], returned_ref.at[me], rs.at[peer], rr.at[me], {"expert": peer})
+        return remote(prod_ref.at[peer], ret.at[me], rs.at[peer], rr.at[me], {"expert": peer})
 
     def ret_in(peer):
-        return remote(prod_ref.at[peer], returned_ref.at[peer], rs.at[peer], rr.at[peer], {"expert": peer})
-
-    own_ret = pltpu.make_async_copy(prod_ref.at[me], returned_ref.at[me], own_sem)
+        return remote(prod_ref.at[peer], ret.at[peer], rs.at[peer], rr.at[peer], {"expert": peer})
+
+    own_ret = pltpu.make_async_copy(prod_ref.at[me], ret.at[me], own_sem)
+    last = flip(me // per, n // per - 1, n // per) * per
+
+    def late_copy(j):
+        k = flip(j, me % per, per)
+        return remote(late_ref.at[j], back.at[n - per + k], bs.at[k], br.at[k], {"expert": last + j})
 
     def to_partner(i):
         return remote(total.at[i], got.at[i], s1.at[i], r1.at[i], partner)
+
+    def column(row):
+        return jnp.transpose(row)[:, 0:1]
+
+    def normal(x):
+        center = x - jnp.mean(x, axis=-1, keepdims=True)
+        scale = lax.rsqrt(jnp.mean(center * center, axis=-1, keepdims=True) + norm_eps)
+        return center * scale, scale
+
+    def normal_back(grad, unit, scale, gain):
+        gu = grad * gain
+        return scale * (
+            gu - jnp.mean(gu, axis=-1, keepdims=True) - unit * jnp.mean(gu * unit, axis=-1, keepdims=True)
+        )
+
+    def offset_slots(at):
+        slot = slot_ref[:, at]
+        return flip(slot // cap, me, n) * cap + slot % cap
+
+    def match(slot_rows, first, count):
+        here = column(slot_rows.astype(f32))
+        return here == (first + lax.broadcasted_iota(jnp.int32, (B, count), 1)).astype(f32)
 
     @pl.when(h == 0)
     def _():
@@ -544,6 +825,8 @@
         for _, dev in over:
             pl.semaphore_signal(barrier, inc=1, device_id=dev, device_id_type=MESH)
         pl.semaphore_wait(barrier, n - 1 + dps - 1)
+        for j in range(per):
+            late_copy(j).start()
 
         def send(i, _):
             ret_copy(flip(me, n - 1 - i, n)).start()
@@ -551,14 +834,63 @@
 
         lax.fori_loop(0, n - 1, send, 0)
         own_ret.start()
+        dcol_ref[...] = upright(jnp.broadcast_to(drow_ref[...], (8, T)))
         transposed_bias(bias_ref, dcol_ref, drow_ref, QB)
-        for c in loads[:3]:
+        part = pl.ds(pl.multiple_of(me % per * cap, 128), cap)
+        for o in range(n):
+            chs[:, o * cap : (o + 1) * cap] = chosen_ref[o, :, part]
+        loads[0].wait()
+
+        def first_rows(b, _):
+            at = pl.ds(pl.multiple_of(b * B, B), B)
+            pick = match(offset_slots(at), 0, early).astype(bf)
+            gh[at, :] = jnp.dot(pick, back[pl.ds(0, n - per)].reshape(early, D), preferred_element_type=f32)
+            return 0
+
+        lax.fori_loop(0, T // B, first_rows, 0)
+        vec_out[...] = jnp.zeros(vec_out.shape, f32)
+        for c in loads[1:4]:
             c.wait()
+        for j in range(per):
+            late_copy(j).wait_recv()
+
+        def second(b, _):
+            at = pl.ds(pl.multiple_of(b * B, B), B)
+            slot_rows = offset_slots(at)
+            all_slots = match(slot_rows, 0, n * cap)
+            chosen = jnp.sum(jnp.where(all_slots, chs[0:1, :], 0.0), axis=1, keepdims=True)
+            pick = match(slot_rows, early, per * cap).astype(bf)
+            sent = gh[at, :] + jnp.dot(
+                pick, back[pl.ds(n - per, per)].reshape(per * cap, D), preferred_element_type=f32
+            )
+            which = lax.broadcasted_iota(jnp.int32, (vec_ref.shape[0], B), 0) - 2
+            expert = which == slot_ref[0:1, at] // cap
+            centroid = lax.dot_general(
+                expert.astype(bf), vec_ref[...].astype(bf), TN, preferred_element_type=f32
+            )
+            grad = sent + chosen * centroid
+            unit, scale = normal(hid[at, :])
+            gain = vec_ref[1:2, :]
+            chosen_row = jnp.transpose(jnp.broadcast_to(chosen, (B, 128)))[0:1, :]
+            vec_out[...] += jnp.dot(
+                jnp.where(expert, chosen_row, 0.0), unit * gain,
+                precision=lax.Precision.HIGHEST, preferred_element_type=f32,
+            )
+            vec_out[1:2, :] += jnp.sum(grad * unit, axis=0, keepdims=True)
+            total_grad = cot[at, :].astype(f32) * scale_ref[0:1, 0:1] + normal_back(grad, unit, scale, gain)
+            gh[at, :] = total_grad
+            low = total_grad.astype(bf)
+            right[3, at, :] = low
+            g_ref[at, :] = lax.dot_general(low, w[3], NT, preferred_element_type=f32).astype(bf)
+            return 0
+
+        lax.fori_loop(0, T // B, second, 0)
+        loads[4].wait()
         out = product(3)
 
         @pl.when(core == 0)
         def _():
-            total[1] = out.astype(jnp.bfloat16)
+            total[1] = out.astype(bf)
             to_partner(1).start()
 
         @pl.when(core == 1)
@@ -566,32 +898,39 @@
             own[1] = out
 
     lanes = pl.ds(pl.multiple_of(h * 128, 128), 128)
-    dq_at = lambda r, value: right.__setitem__((0, r, lanes), value)
-    head_pair_backward(QB, q_ref, k_ref, v_ref, lse_ref, g_ref, bias_ref, dk_ref, dv_ref, dq_at)
-    right[1, :, lanes] = dk_ref[...].astype(jnp.bfloat16)
-    right[2, :, lanes] = dv_ref[...].astype(jnp.bfloat16)
+
+    def put_dq(r, value):
+        right[0, r, lanes] = value
+
+    head_pair_backward(
+        QB, q_ref, k_ref, v_ref, lse_ref, g_ref.at[:, lanes], bias_ref, dk_ref, dv_ref, put_dq
+    )
+    right[1, :, lanes] = dk_ref[...].astype(bf)
+    right[2, :, lanes] = dv_ref[...].astype(bf)
 
     @pl.when(h == pl.num_programs(0) - 1)
     def _():
+        loads[5].wait()
+
         @pl.when(core == 0)
         def _():
-            total[0] = product(2).astype(jnp.bfloat16)
+            total[0] = product(2).astype(bf)
             to_partner(0).start()
             own[0] = product(0)
             own[1] = product(1)
 
         @pl.when(core == 1)
         def _():
-            total[0] = product(0).astype(jnp.bfloat16)
+            total[0] = product(0).astype(bf)
             to_partner(0).start()
-            total[1] = product(1).astype(jnp.bfloat16)
+            total[1] = product(1).astype(bf)
             to_partner(1).start()
             own[0] = product(2)
 
         for i in range(2):
             to_partner(i).wait_send()
             to_partner(i).wait_recv()
-            total[i] = (own[i] + got[i].astype(jnp.float32)).astype(jnp.bfloat16)
+            total[i] = (own[i] + got[i].astype(f32)).astype(bf)
 
         order = along + [(pair, None)]
 
@@ -604,48 +943,58 @@
                 c = remote(total.at[:, piece(dd, q), :], in2.at[d, q], s2.at[dd, q], r2.at[d, q], dev)
                 c.start()
                 c2.append(c)
-        for c in loads[3:]:
-            c.wait()
-        gain = gain_ref[...]
-        gain_sum = jnp.zeros((8, D), jnp.float32)
-        for b in range(T // 256):
-            at = pl.ds(b * 256, 256)
+        loads[6].wait()
+
+        def norm_one(b, _):
+            at = pl.ds(pl.multiple_of(b * B, B), B)
             gn = sum(
-                lax.dot_general(right[c, at, :], w[c], NT, preferred_element_type=jnp.float32)
-                for c in range(3)
+                lax.dot_general(right[c, at, :], w[c], NT, preferred_element_type=f32) for c in range(3)
             )
-            x = xin[at, :].astype(jnp.float32)
-            center = x - jnp.mean(x, axis=-1, keepdims=True)
-            scale = lax.rsqrt(jnp.mean(center * center, axis=-1, keepdims=True) + norm_eps)
-            unit = center * scale
-            gain_sum = gain_sum + jnp.sum((gn * unit).reshape(32, 8, D), axis=0)
-            gu = gn * gain
-            gx = scale * (
-                gu
-                - jnp.mean(gu, axis=-1, keepdims=True)
-                - unit * jnp.mean(gu * unit, axis=-1, keepdims=True)
-            )
-            gh[at, :] = gh[at, :] + gx
-        gain_out[...] = gain_sum
+            unit, scale = normal(xin[at, :].astype(f32))
+            vec_out[0:1, :] += jnp.sum(gn * unit, axis=0, keepdims=True)
+            gh[at, :] += normal_back(gn, unit, scale, vec_ref[0:1, :])
+            return 0
+
+        lax.fori_loop(0, T // B, norm_one, 0)
         dx = pltpu.make_async_copy(gh, dx_ref, dx_sem)
         dx.start()
         c3 = []
         for q, zdev in order:
-            acc = total[:, piece(d, q), :].astype(jnp.float32)
+            acc = total[:, piece(d, q), :].astype(f32)
             for dd, dev in over:
                 remote(in2.at[dd, q], in2.at[dd, q], s2.at[dd, q], r2.at[dd, q], dev).wait_recv()
-                acc = acc + in2[dd, q].astype(jnp.float32)
+                acc = acc + in2[dd, q].astype(f32)
             if zdev is None:
                 u[...] = acc
             else:
-                tb[q] = acc.astype(jnp.bfloat16)
+                tb[q] = acc.astype(bf)
                 c = remote(tb.at[q], in3.at[pair], s3.at[q], r3.at[pair], zdev)
                 c.start()
                 c3.append(c)
+
+        def settle(o, _):
+            peer = flip(me, o, n)
+            ret_copy(peer).wait_send()
+            ret_in(peer).wait_recv()
+            return 0
+
+        lax.fori_loop(1, n, settle, 0)
+        own_ret.wait()
+
+        def add_rows(b, _):
+            at = pl.ds(pl.multiple_of(b * B, B), B)
+            pick = match(slot_ref[:, at], 0, n * cap).astype(bf)
+            got_rows = jnp.dot(pick, ret[...].reshape(n * cap, D), preferred_element_type=f32)
+            hid[at, :] += column(gate_ref[:, at]) * got_rows
+            return 0
+
+        lax.fori_loop(0, T // B, add_rows, 0)
+        block = pltpu.make_async_copy(hid, block_ref, block_sem)
+        block.start()
         acc = u[...]
         for q, dev in along:
             remote(in3.at[q], in3.at[q], s3.at[q], r3.at[q], dev).wait_recv()
-            acc = acc + in3[q].astype(jnp.float32)
+            acc = acc + in3[q].astype(f32)
         u[...] = acc
         theirs = pl.ds(pl.multiple_of((1 - core) * rows, 8), rows)
         mine = pl.ds(pl.multiple_of(core * rows, 8), rows)
@@ -656,25 +1005,20 @@
         out_ref[pl.ds(2 - 2 * core, 2)] = in4[...]
         for c in c2 + c3 + [c4]:
             c.wait_send()
-
-        def settle(o, _):
-            peer = flip(me, o, n)
-            ret_copy(peer).wait_send()
-            ret_in(peer).wait_recv()
-            return 0
-
-        lax.fori_loop(1, n, settle, 0)
-        own_ret.wait()
+        for j in range(per):
+            late_copy(j).wait_send()
         dx.wait()
-
-
-def tail(projected, lse, grad_mixed, documents, gain, normed, mixed, grad_attn, produced, dense_low,
-         grad_hidden, inputs, dps, n):
+        block.wait()
+
+
+def tail(projected, lse, documents, vec, slot_rows, gate_rows, scale, chosen, normed, mixed, produced, dense_low,
+         inputs, late, back, cotangent, hidden, dps, n):
     pairs = n // 2
     _, T, D = projected.shape
     rows = D // (dps * n)
     R = 2 * rows
     cap = produced.shape[1]
+    per = late.shape[0]
     f32, bf = jnp.float32, jnp.bfloat16
     dma = pltpu.SemaphoreType.DMA
     any_ = pl.BlockSpec(memory_space=pl.ANY)
@@ -682,20 +1026,23 @@
     def sp(c):
         return pl.BlockSpec((1, T, 128), lambda h, c=c: (c, 0, h))
 
-    fixed = lambda shape: pl.BlockSpec(shape, lambda h: (0,) * len(shape))
+    def fixed(shape):
+        return pl.BlockSpec(shape, lambda h: (0,) * len(shape))
+
     return pl.pallas_call(
         partial(tail_kernel, dps, pairs, cap),
         grid=(D // 128,),
         out_shape=[
             jax.ShapeDtypeStruct((4, rows, D), f32),
-            jax.ShapeDtypeStruct((8, D), f32),
-            jax.ShapeDtypeStruct(produced.shape, bf),
+            jax.ShapeDtypeStruct(vec.shape, f32),
+            jax.ShapeDtypeStruct((T, D), f32),
             jax.ShapeDtypeStruct((T, D), f32),
         ],
         in_specs=[sp(0), sp(1), sp(2), pl.BlockSpec((1, T, 128), lambda h: (h, 0, 0)),
-                  pl.BlockSpec((T, 128), lambda h: (0, h)), fixed((T, 1)), fixed((1, T)), fixed((1, D))]
-        + [any_] * 7,
-        out_specs=[fixed((4, rows, D)), fixed((8, D)), any_, any_],
+                  fixed((1, T)), fixed(vec.shape), fixed((8, T)), fixed((8, T)), fixed((8, 128)),
+                  fixed(chosen.shape)]
+        + [any_] * 9,
+        out_specs=[fixed((4, rows, D)), fixed(vec.shape), any_, any_],
         scratch_shapes=[
             pltpu.VMEM((min(T, WINDOW + QB), T), f32),
             pltpu.VMEM((T, 128), f32),
@@ -710,18 +1057,25 @@
             pltpu.VMEM((pairs, 2, R, D), bf),
             pltpu.VMEM((2, R, D), f32),
             pltpu.VMEM((2, rows, D), f32),
-            pltpu.VMEM((3, D, D), bf),
+            pltpu.VMEM((4, D, D), bf),
             pltpu.VMEM((T, D), f32),
             pltpu.VMEM((T, D), bf),
-            dma((6,)), dma((2,)), dma((2,)), dma((dps, pairs)), dma((dps, pairs)), dma((pairs,)), dma((pairs,)),
-            dma(()), dma(()), dma((n,)), dma((n,)), dma(()), dma(()),
+            pltpu.VMEM((n, cap, D), bf),
+            pltpu.VMEM((T, D), f32),
+            pltpu.VMEM((n, cap, D), bf),
+            pltpu.VMEM((T, D), bf),
+            pltpu.VMEM((T, D), bf),
+            pltpu.VMEM((8, n * cap), f32),
+            pltpu.VMEM((T, 1), jnp.int32),
+            dma((7,)), dma((2,)), dma((2,)), dma((dps, pairs)), dma((dps, pairs)), dma((pairs,)), dma((pairs,)),
+            dma(()), dma(()), dma((n,)), dma((n,)), dma((per,)), dma((per,)), dma(()), dma(()), dma(()),
         ],
         compiler_params=pltpu.CompilerParams(
-            vmem_limit_bytes=56 * 2**20, collective_id=3, has_side_effects=True
+            vmem_limit_bytes=62 * 2**20, collective_id=3, has_side_effects=True
         ),
-        cost_estimate=pl.CostEstimate(flops=30 * T * D * D, bytes_accessed=100 * 2**20, transcendentals=0),
-    )(projected, projected, projected, lse, grad_mixed, documents.reshape(T, 1), documents.reshape(1, T), gain,
-      normed, mixed, grad_attn, produced, dense_low, grad_hidden, inputs)
+        cost_estimate=pl.CostEstimate(flops=40 * T * D * D, bytes_accessed=200 * 2**20, transcendentals=0),
+    )(projected, projected, projected, lse, documents, vec, slot_rows,
+      gate_rows, scale, chosen, normed, mixed, produced, dense_low, inputs, late, back, cotangent, hidden)
 
 
 def norm_kernel(dps, pairs, d_ref, v_ref, e_ref, out_ref, a, b, c, s1, r1, s2, r2, s3, r3):
@@ -797,6 +1151,11 @@
     )
     average_new = ema_keep * average + (1.0 - ema_keep) * updated
     return (updated, first_new, second_new, average_new)
+
+
+def inverse_order(row_order, sorted_slot):
+    at_token = row_order[:, None] == jnp.arange(row_order.shape[0])[None, :]
+    return jnp.sum(jnp.where(at_token, sorted_slot[:, None], 0), axis=0)
 
 
 def shards(
@@ -828,116 +1187,121 @@
     sequences = tokens // LEN
     splits = lax.axis_size("dp")
     own_rows = dense_weights.shape[1]
-    if own_rows % 8 == 0:
-        dense_low, vector_low = gather_dense(dense_weights, vector_params, splits, owners)
-    else:
-        dense_low, vector_low = (
-            lax.all_gather(dense_weights.astype(jnp.bfloat16), ("dp", "expert"), axis=1, tiled=True),
-            lax.all_gather(vector_params.astype(jnp.bfloat16), ("dp", "expert"), axis=1, tiled=True),
-        )
     me = lax.axis_index("expert")
     seq_index = lax.axis_index("dp") * owners + jnp.arange(owners)
-    bounds = jnp.cumsum(domain_counts)
+    domains = jnp.arange(NDOM)
+    bounds = jnp.sum(jnp.where(domains[None, :] <= domains[:, None], domain_counts[None, :], 0), axis=1)
     domain = jnp.sum((seq_index[:, None] >= bounds[None, :]).astype(jnp.int32), axis=1)
     seq_pick = (domain[:, None] == jnp.arange(NDOM)[None, :]).astype(jnp.float32)
     seq_weight = jnp.sum(seq_pick * domain_weight[None, :], axis=1)
     seq_count = jnp.sum(seq_pick * domain_counts[None, :].astype(jnp.float32), axis=1)
     seq_scale = seq_weight * (sequences * groups) / (NDOM * seq_count)
-    slot_scale = jnp.repeat(seq_scale, capacity)[:, None]
-    token_scale = jnp.broadcast_to(seq_scale[me], (tokens,))
-    row_counts = expert_counts[0]
-    row_order = token_order[0]
-    count_ends = jnp.cumsum(row_counts)
-    count_starts = count_ends - row_counts
-    sorted_pos = jnp.arange(tokens)
-    sorted_expert = jnp.sum((sorted_pos[:, None] >= count_ends[None, :]).astype(jnp.int32), axis=1)
-    sorted_pick = sorted_expert[:, None] == jnp.arange(experts_total)[None, :]
-    sorted_start = jnp.sum(jnp.where(sorted_pick, count_starts[None, :], 0), axis=1)
-    sorted_slot = sorted_expert * capacity + sorted_pos - sorted_start
-    at_token = row_order[:, None] == jnp.arange(tokens)[None, :]
-    token_slot = jnp.sum(jnp.where(at_token, sorted_slot[:, None], 0), axis=0)
-    token_expert = token_slot // capacity
-    expert_pick = (token_expert[:, None] == jnp.arange(experts_total)[None, :]).astype(jnp.float32)
-    slot_match = token_slot[:, None] == jnp.arange(experts_total * capacity)[None, :]
-    slot_pick = slot_match.astype(jnp.bfloat16)
-
-    def to_slots(rows):
-        placed = jnp.dot(slot_pick.T, rows, preferred_element_type=jnp.float32)
-        return placed.astype(jnp.bfloat16).reshape(experts_total, capacity, model_width)
-
-    def from_slots(rows):
-        return jnp.dot(
-            slot_pick, rows.reshape(-1, model_width), preferred_element_type=jnp.float32
+    source_scale = jnp.broadcast_to(seq_scale[:, None], (owners, 128))
+    documents = document_ids.reshape(-1)
+    inputs_float = inputs.astype(jnp.float32)
+    per = TILE // capacity
+    fused = own_rows % 8 == 0 and capacity % 128 == 0 and splits == 4
+    if fused:
+        (dense_low, vec_rows, slot_rows, cot_received, projected, normed_low, mixed_low, totals,
+         hidden_state, gate_rows, send_rows, gate_tiles, expert_low) = head(
+            dense_weights, vector_params, inputs, cotangent, token_order, expert_counts, document_ids,
+            expert_weights, splits, owners, capacity
         )
-
-    later_cot, dense_low = lax.optimization_barrier((cotangent, dense_low))
-    cot_received = lax.all_to_all(
-        to_slots(later_cot), "expert", split_axis=0, concat_axis=0, tiled=True
-    ).reshape(-1, model_width)
-    own_low = expert_weights[0].astype(jnp.bfloat16)
-    expert_low = lax.all_gather(own_low, "dp", axis=0)
-    inputs_float = inputs.astype(jnp.float32)
-    normed_one, norm_one_back = jax.vjp(layer_norm, inputs_float, vector_low[0].astype(jnp.float32))
-    normed_low = normed_one.astype(jnp.bfloat16)
-    projected = jnp.einsum(
-        "td,cde->cte", normed_low, dense_low[:3], preferred_element_type=jnp.float32
-    ).astype(jnp.bfloat16)
-    documents = document_ids.reshape(-1)
-    mixed_low, totals = attend_forward(projected, documents)
-    hidden_state = inputs_float + jnp.dot(
-        mixed_low, dense_low[3], preferred_element_type=jnp.float32
-    )
-    normed_two, norm_two_back = jax.vjp(layer_norm, hidden_state, vector_low[1].astype(jnp.float32))
-    centroids = vector_low[2:].astype(jnp.float32)
-    logits = jnp.dot(normed_two, centroids.T, precision=lax.Precision.HIGHEST)
-    gate_value = jax.nn.sigmoid(jnp.sum(logits * expert_pick, axis=1))
-    sent_rows = normed_two.astype(jnp.bfloat16)
-    send_rows = to_slots(sent_rows)
-    per = TILE // capacity
-    gate_slots = jnp.sum(
-        jnp.where(slot_match, gate_value[:, None], 0.0), axis=0
-    ).reshape(experts_total, 1, 1, capacity)
-    lane_part = (jnp.arange(per) == me % per).astype(jnp.float32)
-    gate_tiles = jnp.broadcast_to(
-        gate_slots * lane_part[None, None, :, None], (experts_total, 8, per, capacity)
-    ).reshape(experts_total, 8, TILE)
+    else:
+        row_counts = expert_counts[0]
+        row_order = token_order[0]
+        count_ends = jnp.cumsum(row_counts)
+        count_starts = count_ends - row_counts
+        sorted_pos = jnp.arange(tokens)
+        sorted_expert = jnp.sum((sorted_pos[:, None] >= count_ends[None, :]).astype(jnp.int32), axis=1)
+        sorted_pick = sorted_expert[:, None] == jnp.arange(experts_total)[None, :]
+        sorted_start = jnp.sum(jnp.where(sorted_pick, count_starts[None, :], 0), axis=1)
+        sorted_slot = sorted_expert * capacity + sorted_pos - sorted_start
+        token_slot = inverse_order(row_order, sorted_slot)
+        own_low = expert_weights[0].astype(jnp.bfloat16)
+        expert_low = lax.all_gather(own_low, "dp", axis=0)
+        dense_low, vector_low = (
+            lax.all_gather(dense_weights.astype(jnp.bfloat16), ("dp", "expert"), axis=1, tiled=True),
+            lax.all_gather(vector_params.astype(jnp.bfloat16), ("dp", "expert"), axis=1, tiled=True),
+        )
+        vector_low = vector_low.astype(jnp.float32)
+        token_expert = token_slot // capacity
+        expert_pick = (token_expert[:, None] == jnp.arange(experts_total)[None, :]).astype(jnp.float32)
+        slot_match = token_slot[:, None] == jnp.arange(experts_total * capacity)[None, :]
+        slot_pick = slot_match.astype(jnp.bfloat16)
+
+        def to_slots(rows):
+            placed = jnp.dot(slot_pick.T, rows, preferred_element_type=jnp.float32)
+            return placed.astype(jnp.bfloat16).reshape(experts_total, capacity, model_width)
+
+        def from_slots(rows):
+            return jnp.dot(
+                slot_pick, rows.reshape(-1, model_width), preferred_element_type=jnp.float32
+            )
+
+        cot_received = lax.all_to_all(
+            to_slots(cotangent), "expert", split_axis=0, concat_axis=0, tiled=True
+        )
+        normed_one, norm_one_back = jax.vjp(layer_norm, inputs_float, vector_low[0])
+        normed_low = normed_one.astype(jnp.bfloat16)
+        projected = jnp.einsum(
+            "td,cde->cte", normed_low, dense_low[:3], preferred_element_type=jnp.float32
+        ).astype(jnp.bfloat16)
+        mixed_low, totals = attend_forward(projected, documents)
+        hidden_state = inputs_float + jnp.dot(
+            mixed_low, dense_low[3], preferred_element_type=jnp.float32
+        )
+        normed_two, norm_two_back = jax.vjp(layer_norm, hidden_state, vector_low[1])
+        centroids = vector_low[2:]
+        logits = jnp.dot(normed_two, centroids.T, precision=lax.Precision.HIGHEST)
+        gate_value = jax.nn.sigmoid(jnp.sum(logits * expert_pick, axis=1))
+        send_rows = to_slots(normed_two.astype(jnp.bfloat16))
+        gate_slots = jnp.sum(
+            jnp.where(slot_match, gate_value[:, None], 0.0), axis=0
+        ).reshape(experts_total, 1, 1, capacity)
+        lane_part = (jnp.arange(per) == me % per).astype(jnp.float32)
+        gate_tiles = jnp.broadcast_to(
+            gate_slots * lane_part[None, None, :, None], (experts_total, 8, per, capacity)
+        ).reshape(experts_total, 8, TILE)
     back_rows, late_rows, chosen_tiles, produced_low, grad_expert = moe(
-        send_rows, gate_tiles, cot_received, slot_scale, expert_low
+        send_rows, gate_tiles, cot_received.reshape(-1, model_width), source_scale, expert_low, fused
     )
     expert_low_grad = lax.psum_scatter(grad_expert, "dp", scatter_dimension=0)
     expert_grad = expert_low_grad.astype(jnp.float32)[None]
-    grad_out = cotangent.astype(jnp.float32) * token_scale[:, None]
-    back_slot = (token_slot // capacity ^ me) * capacity + token_slot % capacity
-    back_match = back_slot[:, None] == jnp.arange(experts_total * capacity)[None, :]
-    back_pick = back_match.astype(jnp.bfloat16)
-    early = back_rows.shape[0] * capacity
-    grad_sent_rows = jnp.dot(
-        back_pick[:, :early], back_rows.reshape(-1, model_width), preferred_element_type=jnp.float32
-    ) + jnp.dot(
-        back_pick[:, early:], late_rows.reshape(-1, model_width), preferred_element_type=jnp.float32
-    )
-    chosen_slots = lax.dynamic_slice_in_dim(
-        chosen_tiles[:, 0, :], me % per * capacity, capacity, axis=1
-    )
-    grad_chosen = jnp.sum(jnp.where(back_match, chosen_slots.reshape(1, -1), 0.0), axis=1)
-    chosen_grad = grad_chosen[:, None] * expert_pick
-    grad_normed_two = grad_sent_rows + jnp.dot(
-        chosen_grad, centroids, precision=lax.Precision.HIGHEST
-    )
-    grad_centroids = jnp.dot(chosen_grad.T, normed_two, precision=lax.Precision.HIGHEST)
-    grad_hidden_norm, grad_gain_two = norm_two_back(grad_normed_two)
-    grad_hidden = grad_out + grad_hidden_norm
-    grad_attn = grad_hidden.astype(jnp.bfloat16)
-    grad_mixed = jnp.dot(grad_attn, dense_low[3].T, preferred_element_type=jnp.float32).astype(
-        jnp.bfloat16
-    )
-    if own_rows % 8 == 0:
-        dense_grad, gain_tiles, returned, input_grad = tail(
-            projected, totals, grad_mixed, documents, vector_low[0:1].astype(jnp.float32), normed_low,
-            mixed_low, grad_attn, produced_low, dense_low, grad_hidden, inputs, splits, owners
+    if fused:
+        dense_grad, vector_grad, input_grad, block_output = tail(
+            projected, totals, document_ids, vec_rows, slot_rows, gate_rows,
+            jnp.broadcast_to(seq_scale[me], (8, 128)), chosen_tiles, normed_low, mixed_low, produced_low,
+            dense_low, inputs, late_rows, back_rows, cotangent, hidden_state, splits, owners
         )
-        grad_gain_one = jnp.sum(gain_tiles, axis=0)
+        vector_grad = vector_grad[: vector_params.shape[0]]
     else:
+        late_rows = send_late(late_rows, owners)
+        grad_out = cotangent.astype(jnp.float32) * seq_scale[me]
+        back_slot = (token_slot // capacity ^ me) * capacity + token_slot % capacity
+        back_match = back_slot[:, None] == jnp.arange(experts_total * capacity)[None, :]
+        back_pick = back_match.astype(jnp.bfloat16)
+        early = back_rows.shape[0] * capacity
+        grad_sent_rows = jnp.dot(
+            back_pick[:, :early], back_rows.reshape(-1, model_width), preferred_element_type=jnp.float32
+        ) + jnp.dot(
+            back_pick[:, early:], late_rows.reshape(-1, model_width), preferred_element_type=jnp.float32
+        )
+        chosen_slots = lax.dynamic_slice_in_dim(
+            chosen_tiles[:, 0, :], me % per * capacity, capacity, axis=1
+        )
+        grad_chosen = jnp.sum(jnp.where(back_match, chosen_slots.reshape(1, -1), 0.0), axis=1)
+        chosen_grad = grad_chosen[:, None] * expert_pick
+        grad_normed_two = grad_sent_rows + jnp.dot(
+            chosen_grad, centroids, precision=lax.Precision.HIGHEST
+        )
+        grad_centroids = jnp.dot(chosen_grad.T, normed_two, precision=lax.Precision.HIGHEST)
+        grad_hidden_norm, grad_gain_two = norm_two_back(grad_normed_two)
+        grad_hidden = grad_out + grad_hidden_norm
+        grad_attn = grad_hidden.astype(jnp.bfloat16)
+        grad_mixed = jnp.dot(grad_attn, dense_low[3].T, preferred_element_type=jnp.float32).astype(
+            jnp.bfloat16
+        )
         returned = lax.all_to_all(produced_low, "expert", split_axis=0, concat_axis=0, tiled=True)
         grad_proj = attend_backward(projected, documents, totals, grad_mixed)
         grad_normed_one = jnp.einsum(
@@ -955,11 +1319,11 @@
             scatter_dimension=1,
             tiled=True,
         )
-    returned_rows = from_slots(returned)
-    block_output = hidden_state + gate_value[:, None] * returned_rows
-    vector_grad = jnp.concatenate(
-        [grad_gain_one[None], grad_gain_two[None], grad_centroids], axis=0
-    )
+        returned_rows = from_slots(returned)
+        block_output = hidden_state + gate_value[:, None] * returned_rows
+        vector_grad = jnp.concatenate(
+            [grad_gain_one[None], grad_gain_two[None], grad_centroids], axis=0
+        )
     vector_grad, squares = norm_squares(dense_grad, vector_grad, expert_low_grad, splits, owners)
     grad_norm = jnp.sqrt(squares)
     factor = jnp.minimum(1.0, clip_norm / (grad_norm + 1e-06))

time: 473 us -> 434 us (0.918)
  Pallas kernels: 326 us -> 376 us
  matrix products: 48.3 us -> 0 us
  waiting for transfers between devices: 26 us -> 0.02 us
  other arithmetic: 34 us -> 20.3 us
  starting transfers between devices: 4.82 us -> 0.04 us
    dot_general x11 -> x0, matrix products: 48.3 us -> none  [the longest x2 12.3 us: to_slots(): placed = jnp.dot(slot_pick.T, rows, preferred_element_type=jnp.float32)]
    pallas_call x1, Pallas kernels: 103 us -> 141 us  [tail(): pl.pallas_call(partial(tail_kernel, dps, pairs, cap), grid=(D // 128,), o...]
    all_to_all x1 -> x0, waiting for transfers between devices: 25.9 us -> none  [shards(): lax.all_to_all(to_slots(later_cot), 'expert', split_axis=0, concat_axis=0...]
    pallas_call x4 -> x2, Pallas kernels: 206 us -> 214 us  [the longest x1 117 us: moe(): pl.pallas_call(partial(moe_kernel, n, cap, square), out_shape=[jax.ShapeD...]
    convert_element_type x5 -> x0, other arithmetic: 7.44 us -> none  [the longest x1 4.09 us: shards(): own_low = expert_weights[0].astype(jnp.bfloat16)]
    reduce_sum x10 -> x1, other arithmetic: 7.04 us -> 0.77 us  [shards(): jnp.sum(jnp.where(domains[None, :] <= domains[:, None], domain_counts[Non...]
  transfers between devices with their start and end apart: 3 -> 1, of which waited for: 1 -> 0; matrix products, arithmetic and copies ran while one was open for 14% -> 1% of each run, Pallas kernels for 42% -> 33%
where the time goes in v5:
time: 434 us; the launch traced here: 426 us
  Pallas kernels  376 us (87%)
  other arithmetic  20.3 us (5%)
  between operations  16.9 us (4%)
  local copies, waits for them, and re-layouts  12.6 us (3%)
    pallas_call x1, Pallas kernels, tail(): pl.pallas_call(partial(tail_kernel, dps, pairs, cap), grid=(D // 128,), o...  141 us
    pallas_call x1, Pallas kernels, moe(): pl.pallas_call(partial(moe_kernel, n, cap, square), out_shape=[jax.ShapeD...  117 us
    pallas_call x1, Pallas kernels, head(): pl.pallas_call(partial(head_kernel, dps, pairs, n, cap), out_shape=[shape...  97 us
    pallas_call x1, Pallas kernels, norm_squares(): pl.pallas_call(partial(norm_kernel, dps, pairs), out_shape=jax.ShapeDtype...  20.3 us
    add x3, other arithmetic, adam_update(): average_new = ema_keep * average + (1.0 - ema_keep) * updated  16.4 us
  transfers between devices with their start and end apart: 1, of which 0 were waited for; matrix products, arithmetic and copies ran while one was open for 1% of the time, Pallas kernels for 33%

profile of v5, /device:TPU:0, one launch (start us, length us, event | category | flops | bytes accessed | tf_op | source)
XLA Modules:
  0.0 425.6 jit_solution(15566330617143329487)
XLA Ops:
  7.2 0.8 select_reduce_fusion.2
  8.0 0.7 convert_element_type.16
  8.7 0.2 convert_reduce_fusion
  8.8 0.9 select_reduce_fusion.1
  9.7 1.6 dynamic_update_slice.3.v_ref
  11.3 0.6 copy-done.8
  11.9 97.0 %shard_map.298 = (bf16[4,768,768]{2,1,0:T(8,128)(2,1)}, f32[16,768]{1,0:T(8,128)}, s32[8,1024]{1,0:T(8,128)}, bf16[8,256,768]{2,1,0:T(8,128)(2,1)}, bf16[3,1024,...) custom-call(f32[4,24,768]{2,1,0:T(8,128)} %w_ref.1, ...), custom_call_target="tpu_custom_call" | custom-call | flops 12079595520 | bytes 209715200 | tf_op jit(solution)/shard_map/pallas_call | solution.py:716
  108.9 0.7 broadcast_in_dim.22.scale_ref
  109.6 116.9 %shard_map.299 = (bf16[6,256,768]{2,1,0:T(8,128)(2,1)}, bf16[2,256,768]{2,1,0:T(8,128)(2,1)}, f32[8,8,512]{2,1,0:T(8,128)}, bf16[8,256,768]{2,1,0:T(8,128)(2,1)}, bf16[4,2,768,768]{3,2,1,0:T(8,128)(2,1)}) custom-call(bf16[8,256,768]{2,1,0:T(8,128)(2,1)} %get-tuple-element.42.send_ref, f32[8,8,512]{2,1,0:T(8,128)} %get-tuple-element.43.gate_ref, ...), custom_call_target="tpu_custom_call" | custom-call | flops 57982058496 | bytes 41943040 | tf_op jit(solution)/shard_map/pallas_call | solution.py:364
  226.6 0.6 dynamic_slice.6
  227.1 1.2 broadcast_in_dim.21.scale_ref
  228.4 141.5 %shard_map.300 = (f32[4,24,768]{2,1,0:T(8,128)}, f32[16,768]{1,0:T(8,128)}, f32[1024,768]{1,0:T(8,128)}, f32[1024,768]{1,0:T(8,128)}) custom-call(bf16[3,1024,768]{2,1,0:T(8,128)(2,1)} %get-tuple-element.37.q_ref.k_ref.v_ref, bf16[3,1024,768]{2,1,0:T(8,128)(2,1)} %get-tuple-element.37.q_ref.k_ref.v_ref, ...), custom_call_target="tpu_custom_call" | custom-call | flops 24159191040 | bytes 209715200 | tf_op jit(solution)/shard_map/pallas_call | solution.py:1032
  370.0 0.9 broadcast_select_fusion.v_ref
  370.8 1.7 copy-done
  372.5 1.0 copy-done.2
  373.5 20.3 %shard_map.301 = f32[16,768]{1,0:T(8,128)S(1)} custom-call(f32[4,24,768]{2,1,0:T(8,128)S(1)} %copy-done.2, f32[16,768]{1,0:T(8,128)S(1)} %broadcast_select_fusion.v_ref, bf16[2,768,768]{2,1,0:T(8,128)(2,1)S(1)} %bitcast.5), custom_call_target="tpu_custom_call" | custom-call | tf_op jit(solution)/shard_map/pallas_call | solution.py:1122
  393.8 0.6 fusion.6
  394.4 0.5 slice.8
  396.3 2.2 multiply_add_fusion.2
  398.6 0.7 multiply_add_fusion.4
  399.3 13.4 %multiply_add_fusion = (f32[1,2,768,768]{3,2,1,0:T(8,128)}, f32[1,2,768,768]{3,2,1,0:T(8,128)}, f32[1,2,768,768]{3,2,1,0:T(8,128)}, f32[1,2,768,768]{3,2,1,0:T(8,128)}) fusion(f32[1,2,768,768]{3,2,1,0:T(8,128)} %param.37, f32[1,2,768,768]{3,2,1,0:T(8,128)} %ew_ref.1, f32[]{:T(128)S(6)} %min.3, bf16[1,2,768,768]{3,2,1,0:T(8,128)(2,1)S(1)} %copy-done.1, ...), kind=kLoop, calls=%fused_computation.2 | loop fusion | flops 23592960 | bytes 40108036 | tf_op jit(solution)/shard_map/add | solution.py:1152
  412.7 1.7 copy.37
  414.4 1.4 copy-done.3
  415.7 1.7 copy.38
  (30 shorter events, 0.1 us)
Async XLA Ops:
  7.2 363.7 %reduce-scatter.4.cloned.1.call-start = ((), (), s32[]{:S(2)}) async-start(), calls=%async_computation.1 | async-start | bytes 11796480
  11.3 0.6 copy-start.8
  228.4 141.6 %copy-start.13 = (pred[16]{0:T(512)(128)(4,1)S(1)}, pred[16]{0:T(512)(128)(4,1)}, u32[]{:S(2)}) copy-start(pred[16]{0:T(512)(128)(4,1)} %constant.32.clone.1) | copy-start | bytes 52
  228.4 167.9 %copy-start.5 = (f32[4,24,768]{2,1,0:T(8,128)S(1)}, f32[4,24,768]{2,1,0:T(8,128)}, u32[]{:S(2)}) copy-start(f32[4,24,768]{2,1,0:T(8,128)} %w_ref.1) | copy-start | bytes 884740
  228.4 167.9 %copy-start.6 = (f32[4,24,768]{2,1,0:T(8,128)S(1)}, f32[4,24,768]{2,1,0:T(8,128)}, u32[]{:S(2)}) copy-start(f32[4,24,768]{2,1,0:T(8,128)} %param.31) | copy-start | bytes 884740
  228.4 167.9 %copy-start.7 = (f32[4,24,768]{2,1,0:T(8,128)S(1)}, f32[4,24,768]{2,1,0:T(8,128)}, u32[]{:S(2)}) copy-start(f32[4,24,768]{2,1,0:T(8,128)} %param.29) | copy-start | bytes 884740
  369.9 28.6 %copy-start.9 = (f32[10,24]{1,0:T(8,128)S(1)}, f32[10,24]{1,0:T(8,128)}, u32[]{:S(2)}) copy-start(f32[10,24]{1,0:T(8,128)} %param.27) | copy-start | bytes 2884
  369.9 28.6 %copy-start.10 = (f32[10,24]{1,0:T(8,128)S(1)}, f32[10,24]{1,0:T(8,128)}, u32[]{:S(2)}) copy-start(f32[10,24]{1,0:T(8,128)} %param.34) | copy-start | bytes 2884
  369.9 28.6 %copy-start.11 = (f32[10,24]{1,0:T(8,128)S(1)}, f32[10,24]{1,0:T(8,128)}, u32[]{:S(2)}) copy-start(f32[10,24]{1,0:T(8,128)} %param.32) | copy-start | bytes 2884
  369.9 28.6 %copy-start.12 = (f32[10,24]{1,0:T(8,128)S(1)}, f32[10,24]{1,0:T(8,128)}, u32[]{:S(2)}) copy-start(f32[10,24]{1,0:T(8,128)} %param.33) | copy-start | bytes 2884
  370.8 1.7 copy-start
  372.5 1.0 copy-start.2
  373.5 25.8 %copy-start.1 = (bf16[1,2,768,768]{3,2,1,0:T(8,128)(2,1)S(1)}, bf16[1,2,768,768]{3,2,1,0:T(8,128)(2,1)}, u32[]{:S(2)}) copy-start(bf16[1,2,768,768]{3,2,1,0:T(8,128)(2,1)} %reduce-scatter.4.cloned.1.call-done) | copy-start | bytes 7077892
  399.3 13.4 %copy-start.4 = (f32[1024,768]{1,0:T(8,128)S(1)}, f32[1024,768]{1,0:T(8,128)}, u32[]{:S(2)}) copy-start(f32[1024,768]{1,0:T(8,128)} %get-tuple-element.90) | copy-start | bytes 9437188
  412.7 3.0 copy-start.3
Sparse Core Ops, SparseCore 0:
  226.7 118.7 reduce-scatter.3
